TPU v7x, 32 devices: a whole 2x2x4 slice. The times are simulated.
32 devices in a mesh: dp: 4 (over x, core), blk: 8 (over z, y).
Axes of the slice: x: 2, y: 2, z: 4, core: 2. Of those that a mesh axis runs over, the one named last changes fastest.
Arguments:
- hidden: bfloat16 [4096, 1536], P(('dp', 'blk')), may hold values from -6 to 6
- segments: int32 [4096], P(('dp', 'blk')), may hold values from 0 to 1, as said below
- positions: int32 [3, 4096], P(None, ('dp', 'blk')), may hold values from 0 to 63
- condition: float32 [8, 1024], P('dp'), may hold values from -6 to 6
- captions: bfloat16 [8, 128, 4096], P('dp', None, 'blk'), may hold values from -6 to 6
- dropped: int32 [8], P('dp'), may hold values from 0 to 1, as said below
- null_caption: bfloat16 [128, 4096], P(None, 'blk'), may hold values from -6 to 6
- ada_weight: bfloat16 [1024, 6144], P('blk'), may hold values from -0.1875 to 0.1875
- ada_bias: float32 [6144], replicated, may hold values from -1.5 to 1.5
- qkv_weight: bfloat16 [1536, 4608], P('blk'), may hold values from -0.15625 to 0.15625
- out_weight: bfloat16 [1536, 1536], P('blk'), may hold values from -0.15625 to 0.15625
- caption_weight: bfloat16 [4096, 3072], P('blk'), may hold values from -0.09375 to 0.09375
- gate_up: bfloat16 [1536, 8192], P('blk'), may hold values from -0.15625 to 0.15625
- down_weight: bfloat16 [4096, 1536], P('blk'), may hold values from -0.09375 to 0.09375
- gains: float32 [7, 1536], replicated, may hold values from 0.5 to 1.5
- head_gate: float32 [24], replicated, may hold values from 0.3 to 1
- cotangent: bfloat16 [4096, 1536], P(('dp', 'blk')), may hold values from -6 to 6
Outputs:
- output: float32 [4096, 1536], P(('dp', 'blk'))
- input_grad: float32 [4096, 1536], P(('dp', 'blk'))
- ada_weight_grad: float32 [1024, 6144], P('blk')
- ada_bias_grad: float32 [6144], replicated
- qkv_grad: float32 [1536, 4608], P('blk')
- out_grad: float32 [1536, 1536], P('blk')
- caption_grad: float32 [4096, 3072], P('blk')
- gate_up_grad: float32 [1536, 8192], P('blk')
- down_grad: float32 [4096, 1536], P('blk')
- null_grad: float32 [128, 4096], P(None, 'blk')
- gains_grad: float32 [7, 1536], replicated
- head_gate_grad: float32 [24], replicated
Inputs may be any that keep to these rules, and one draw needn't show every extreme that they name: `segments`: within each group of 1024 tokens the clip numbers never fall and each of the 2 clips holds one token or more. Some clip is dropped and some is kept.
All inputs are finite; a program needn't handle non-finite values.
Results may differ from a plain program's by a relative error of at most 0.039.
Values may be sent and summed in bfloat16 or wider, within the bound.
No kernel may reach another device: no remote copies, remote signals or barrier semaphores. Data moves between devices by JAX's collectives and lax.ppermute only.
A program may use at most 320 MiB of HBM per device.

v0:
```python
import math

import jax
import jax.numpy as jnp
from jax import lax
from jax.sharding import PartitionSpec as P

HEADS = 24
HEAD = 64
D = 1536
FF = 4096
CAP = 128
CLIPS = 2


PRECISE = lax.Precision.HIGHEST
EPSILON = 1e-06
NEGATIVE = -1e30


def unit_rows(values):
    return values * lax.rsqrt(jnp.mean(values * values, -1, keepdims=True) + EPSILON)


def norm_back(grad_in, values, gain):
    inv_root = lax.rsqrt(jnp.mean(values * values, -1, keepdims=True) + EPSILON)
    normed = values * inv_root
    inner_grad = grad_in * gain
    back_grad = inv_root * (inner_grad - normed * jnp.mean(inner_grad * normed, -1, keepdims=True))
    return (back_grad, jnp.sum(grad_in * normed, 0))


def rope_tables(positions):
    pair_count = HEAD // 2
    pair_index = jnp.arange(pair_count)
    frequency = 10000.0 ** (-3.0 * (pair_index // 3).astype(jnp.float32) / pair_count)
    select = ((pair_index % 3)[None, :] == jnp.arange(3)[:, None]).astype(jnp.float32)
    angles = (
        jnp.dot(positions.astype(jnp.float32).T, select, precision=PRECISE) * frequency[None, :]
    )
    return (jnp.cos(angles), jnp.sin(angles))


def rotate(tensor, cosine_table, sine_table, sign):
    row_count = tensor.shape[0]
    paired = tensor.reshape(row_count, -1, cosine_table.shape[1], 2)
    even_part = paired[..., 0]
    odd_part = paired[..., 1]
    cosines = cosine_table[:, None, :]
    sines = sign * sine_table[:, None, :]
    turned = jnp.stack(
        [even_part * cosines - odd_part * sines, even_part * sines + odd_part * cosines], -1
    )
    return turned.reshape(row_count, -1)


def forward_product(left_rows, local_rows):
    return (
        jnp.dot(
            left_rows,
            lax.all_gather(local_rows, "blk", axis=0, tiled=True),
            preferred_element_type=jnp.float32,
        ),
        local_rows,
    )


def backward_product(grad_rows, local_rows):
    return lax.dot_general(
        grad_rows,
        lax.all_gather(local_rows, "blk", axis=0, tiled=True),
        (((1,), (1,)), ((), ())),
        preferred_element_type=jnp.float32,
    )


def weight_grad(left_rows, grad_rows):
    return lax.psum_scatter(
        lax.dot_general(
            left_rows, grad_rows, (((0,), (0,)), ((), ())), preferred_element_type=jnp.float32
        ).astype(jnp.bfloat16),
        "blk",
        scatter_dimension=0,
        tiled=True,
    ).astype(jnp.float32)


def attend_piece(queries, query_seg, scaling, state_now, key_part, value_part, seg_part):
    running_max, running_sum, weighted = state_now
    scores = (
        jnp.einsum("thd,khd->htk", queries, key_part, preferred_element_type=jnp.float32) * scaling
    )
    allowed = (query_seg[:, None] == seg_part[None, :])[None]
    masked = jnp.where(allowed, scores, NEGATIVE)
    new_max = jnp.maximum(running_max, jnp.max(masked, -1))
    prob_self = jnp.where(allowed, jnp.exp(masked - new_max[:, :, None]), 0.0)
    factor = jnp.exp(running_max - new_max)
    running_sum = running_sum * factor + jnp.sum(prob_self, -1)
    weighted = weighted * factor.T[:, :, None] + jnp.einsum(
        "htk,khd->thd",
        prob_self.astype(jnp.bfloat16),
        value_part,
        preferred_element_type=jnp.float32,
    )
    return (new_max, running_sum, weighted)


def self_forward(queries, query_seg, key_rows, value_rows, seg_rows):
    scaling = HEAD ** (-0.5)
    token_count = queries.shape[0]
    initial = (
        jnp.full((HEADS, token_count), NEGATIVE, jnp.float32),
        jnp.zeros((HEADS, token_count), jnp.float32),
        jnp.zeros((token_count, HEADS, HEAD), jnp.float32),
    )
    key_piece = lax.all_gather(key_rows, "blk", axis=0, tiled=True)
    value_piece = lax.all_gather(value_rows, "blk", axis=0, tiled=True)
    seg_piece = lax.all_gather(seg_rows, "blk", axis=0, tiled=True)
    length = key_piece.shape[0]
    span_rows = math.gcd(length, 512)
    step_count = length // span_rows
    stacked = (
        key_piece.reshape(step_count, span_rows, HEADS, HEAD),
        value_piece.reshape(step_count, span_rows, HEADS, HEAD),
        seg_piece.reshape(step_count, span_rows),
    )

    def absorb_visit_block(state_in, block_items):
        return (attend_piece(queries, query_seg, scaling, state_in, *block_items), None)

    result, unused = lax.scan(absorb_visit_block, initial, stacked)
    return result


def score_terms(
    query_part, dout_part, lse_part, delta_part, query_segs, key_part, value_part, key_segs, scaling
):
    scores = (
        jnp.einsum("thd,khd->htk", query_part, key_part, preferred_element_type=jnp.float32)
        * scaling
    )
    allowed = (query_segs[:, None] == key_segs[None, :])[None]
    prob_self = jnp.where(
        allowed, jnp.exp(jnp.where(allowed, scores, NEGATIVE) - lse_part[:, :, None]), 0.0
    )
    d_prob = jnp.einsum("thd,khd->htk", dout_part, value_part, preferred_element_type=jnp.float32)
    d_score = (prob_self * (d_prob - delta_part[:, :, None])).astype(jnp.bfloat16)
    return (prob_self, d_score)


def self_backward(
    queries, query_seg, grad_out, out_self, log_total, key_rows, value_rows, seg_rows
):
    scaling = HEAD ** (-0.5)
    whole_keys, whole_values, whole_segs = (
        lax.all_gather(key_rows, "blk", axis=0, tiled=True),
        lax.all_gather(value_rows, "blk", axis=0, tiled=True),
        lax.all_gather(seg_rows, "blk", axis=0, tiled=True),
    )
    length = whole_keys.shape[0]
    span_rows = math.gcd(length, 512)
    step_count = length // span_rows
    stacked = (
        whole_keys.reshape(step_count, span_rows, HEADS, HEAD),
        whole_values.reshape(step_count, span_rows, HEADS, HEAD),
        whole_segs.reshape(step_count, span_rows),
    )
    delta_rows = jnp.sum(grad_out.astype(jnp.float32) * out_self, -1).T
    zero_start = jnp.zeros(queries.shape, jnp.float32)

    def self_visit_block(grad_query, block_items):
        key_part, value_part, seg_part = block_items
        prob_self, d_score = score_terms(
            queries,
            grad_out,
            log_total,
            delta_rows,
            query_seg,
            key_part,
            value_part,
            seg_part,
            scaling,
        )
        grad_query = (
            grad_query
            + jnp.einsum("htk,khd->thd", d_score, key_part, preferred_element_type=jnp.float32)
            * scaling
        )
        grad_key = (
            jnp.einsum("htk,thd->khd", d_score, queries, preferred_element_type=jnp.float32)
            * scaling
        )
        grad_value = jnp.einsum(
            "htk,thd->khd",
            prob_self.astype(jnp.bfloat16),
            grad_out,
            preferred_element_type=jnp.float32,
        )
        return (grad_query, (grad_key, grad_value))

    grad_query, key_terms = lax.scan(self_visit_block, zero_start, stacked)
    key_grad, value_grad = (
        lax.psum_scatter(
            key_terms[0].reshape(length, HEADS * HEAD).astype(jnp.bfloat16),
            "blk",
            scatter_dimension=0,
            tiled=True,
        ).astype(jnp.float32),
        lax.psum_scatter(
            key_terms[1].reshape(length, HEADS * HEAD).astype(jnp.bfloat16),
            "blk",
            scatter_dimension=0,
            tiled=True,
        ).astype(jnp.float32),
    )
    return (grad_query, key_grad, value_grad)


def on_device(
    hidden,
    segments,
    positions,
    condition,
    captions,
    dropped,
    null_caption,
    ada_weight,
    ada_bias,
    qkv_weight,
    out_weight,
    caption_weight,
    gate_up,
    down_weight,
    gains,
    head_gate,
    cotangent,
):
    scaling = HEAD ** (-0.5)
    blk_index = lax.axis_index("blk")
    cond_rows = ada_weight.shape[0]
    cond_low = lax.dynamic_slice_in_dim(
        jax.nn.silu(condition), blk_index * cond_rows, cond_rows, 1
    ).astype(jnp.bfloat16)
    mod_part = jnp.dot(cond_low, ada_weight, preferred_element_type=jnp.float32)
    chosen = jnp.where(dropped[:, None, None] == 1, null_caption[None], captions)
    chosen_rows = chosen.reshape(CLIPS * CAP, chosen.shape[2])
    caption_part = jnp.dot(chosen_rows, caption_weight, preferred_element_type=jnp.float32)
    mod_sum, caption_proj = (
        lax.psum(mod_part.astype(jnp.bfloat16), "blk").astype(jnp.float32),
        lax.psum(caption_part.astype(jnp.bfloat16), "blk").astype(jnp.float32),
    )
    modulation = mod_sum + ada_bias
    caption_keys = (
        (unit_rows(caption_proj[:, :D]) * gains[6]).astype(jnp.bfloat16).reshape(-1, HEADS, HEAD)
    )
    caption_values = caption_proj[:, D:].astype(jnp.bfloat16).reshape(-1, HEADS, HEAD)
    onehot = (segments[:, None] == jnp.arange(CLIPS)[None, :]).astype(jnp.float32)
    token_mod = jnp.dot(onehot, modulation, precision=PRECISE)
    scale_attn = token_mod[:, :D]
    gate_attn = jnp.tanh(token_mod[:, D : 2 * D])
    scale_ffn = token_mod[:, 2 * D : 3 * D]
    gate_ffn = jnp.tanh(token_mod[:, 3 * D :])
    source = hidden.astype(jnp.float32)
    unit_in = unit_rows(source)
    first_in = (unit_in * gains[0] * (1.0 + scale_attn)).astype(jnp.bfloat16)
    projected, qkv_whole = forward_product(first_in, qkv_weight)
    cosine_table, sine_table = rope_tables(positions)
    queries = rotate(unit_rows(projected[:, :D]) * gains[4], cosine_table, sine_table, 1.0).astype(
        jnp.bfloat16
    )
    key_rows = rotate(
        unit_rows(projected[:, D : 2 * D]) * gains[5], cosine_table, sine_table, 1.0
    ).astype(jnp.bfloat16)
    value_rows = projected[:, 2 * D :].astype(jnp.bfloat16)
    query_heads = queries.reshape(-1, HEADS, HEAD)
    running_max, running_sum, weighted = self_forward(
        query_heads, segments, key_rows, value_rows, segments
    )
    out_self = weighted / running_sum.T[:, :, None]
    log_total = running_max + jnp.log(running_sum)
    cross_clip = jnp.arange(CLIPS * CAP) // CAP
    cross_scores = (
        jnp.einsum("thd,khd->htk", query_heads, caption_keys, preferred_element_type=jnp.float32)
        * scaling
    )
    cross_allowed = (segments[:, None] == cross_clip[None, :])[None]
    cross_masked = jnp.where(cross_allowed, cross_scores, NEGATIVE)
    cross_top = jnp.max(cross_masked, -1, keepdims=True)
    exp_cross = jnp.where(cross_allowed, jnp.exp(cross_masked - cross_top), 0.0)
    cross_total = jnp.sum(exp_cross, -1)
    out_cross = (
        jnp.einsum(
            "htk,khd->thd",
            exp_cross.astype(jnp.bfloat16),
            caption_values,
            preferred_element_type=jnp.float32,
        )
        / cross_total.T[:, :, None]
    )
    cross_probs = exp_cross / cross_total[:, :, None]
    head_tanh = jnp.tanh(head_gate)
    mixed_heads = (
        (out_self + head_tanh[None, :, None] * out_cross).reshape(-1, D).astype(jnp.bfloat16)
    )
    attended, out_whole = forward_product(mixed_heads, out_weight)
    attn_unit = unit_rows(attended)
    middle = source + gate_attn * attn_unit * gains[1]
    unit_mid = unit_rows(middle)
    second_in = (unit_mid * gains[2] * (1.0 + scale_ffn)).astype(jnp.bfloat16)
    gate_values, gate_up_whole = forward_product(second_in, gate_up)
    gate_part = gate_values[:, :FF]
    up_part = gate_values[:, FF:]
    activated = (jax.nn.silu(gate_part) * up_part).astype(jnp.bfloat16)
    lowered, down_whole = forward_product(activated, down_weight)
    low_unit = unit_rows(lowered)
    result = middle + gate_ffn * low_unit * gains[3]
    upstream = cotangent.astype(jnp.float32)
    d_gate_ffn = upstream * low_unit * gains[3] * (1.0 - gate_ffn * gate_ffn)
    d_lowered, grad_gain3 = norm_back(upstream * gate_ffn, lowered, gains[3])
    d_lowered_low = d_lowered.astype(jnp.bfloat16)
    grad_down = weight_grad(activated, d_lowered_low)
    d_activated = backward_product(d_lowered_low, down_weight)
    sigmoid_gate = jax.nn.sigmoid(gate_part)
    d_gate_part = d_activated * up_part * sigmoid_gate * (1.0 + gate_part * (1.0 - sigmoid_gate))
    d_up_part = d_activated * gate_part * sigmoid_gate
    d_gate_values = jnp.concatenate([d_gate_part, d_up_part], 1).astype(jnp.bfloat16)
    grad_gate_up = weight_grad(second_in, d_gate_values)
    d_second = backward_product(d_gate_values, gate_up)
    d_scale_ffn = d_second * unit_mid * gains[2]
    d_middle_norm, grad_gain2 = norm_back(d_second * (1.0 + scale_ffn), middle, gains[2])
    d_middle = upstream + d_middle_norm
    d_gate_attn = d_middle * attn_unit * gains[1] * (1.0 - gate_attn * gate_attn)
    d_attended, grad_gain1 = norm_back(d_middle * gate_attn, attended, gains[1])
    d_attended_low = d_attended.astype(jnp.bfloat16)
    grad_out = weight_grad(mixed_heads, d_attended_low)
    d_mixed = (
        backward_product(d_attended_low, out_weight).astype(jnp.bfloat16).reshape(-1, HEADS, HEAD)
    )
    d_cross = (head_tanh[None, :, None] * d_mixed.astype(jnp.float32)).astype(jnp.bfloat16)
    d_head = jnp.sum(d_mixed.astype(jnp.float32) * out_cross, (0, 2)) * (
        1.0 - head_tanh * head_tanh
    )
    d_prob_cross = jnp.einsum(
        "thd,khd->htk", d_cross, caption_values, preferred_element_type=jnp.float32
    )
    delta_cross = jnp.sum(d_cross.astype(jnp.float32) * out_cross, -1).T
    d_score_cross = (cross_probs * (d_prob_cross - delta_cross[:, :, None])).astype(jnp.bfloat16)
    grad_q_cross = (
        jnp.einsum("htk,khd->thd", d_score_cross, caption_keys, preferred_element_type=jnp.float32)
        * scaling
    )
    grad_caption_keys = (
        jnp.einsum("htk,thd->khd", d_score_cross, query_heads, preferred_element_type=jnp.float32)
        * scaling
    )
    grad_caption_values = jnp.einsum(
        "htk,thd->khd",
        cross_probs.astype(jnp.bfloat16),
        d_cross,
        preferred_element_type=jnp.float32,
    )
    grad_q_self, key_grad, value_grad = self_backward(
        query_heads, segments, d_mixed, out_self, log_total, key_rows, value_rows, segments
    )
    d_query = (grad_q_self + grad_q_cross).reshape(-1, D)
    d_q_raw, grad_gain4 = norm_back(
        rotate(d_query, cosine_table, sine_table, -1.0), projected[:, :D], gains[4]
    )
    d_k_raw, grad_gain5 = norm_back(
        rotate(key_grad, cosine_table, sine_table, -1.0), projected[:, D : 2 * D], gains[5]
    )
    d_projected = jnp.concatenate([d_q_raw, d_k_raw, value_grad], 1).astype(jnp.bfloat16)
    grad_qkv = weight_grad(first_in, d_projected)
    d_first = backward_product(d_projected, qkv_weight)
    d_scale_attn = d_first * unit_in * gains[0]
    d_source_norm, grad_gain0 = norm_back(d_first * (1.0 + scale_attn), source, gains[0])
    input_grad = d_middle + d_source_norm
    d_token_mod = jnp.concatenate([d_scale_attn, d_gate_attn, d_scale_ffn, d_gate_ffn], 1)
    d_mod_part = lax.dot_general(onehot, d_token_mod, (((0,), (0,)), ((), ())), precision=PRECISE)
    d_ckeys_raw, grad_gain6 = norm_back(
        grad_caption_keys.reshape(-1, D), caption_proj[:, :D], gains[6]
    )
    d_caption_part = jnp.concatenate([d_ckeys_raw, grad_caption_values.reshape(-1, D)], 1)
    gain_part = jnp.stack(
        [grad_gain0, grad_gain1, grad_gain2, grad_gain3, grad_gain4, grad_gain5, grad_gain6]
    )
    d_mod, d_caption, gain_sum, head_sum = (
        lax.psum(d_mod_part.astype(jnp.bfloat16), "blk").astype(jnp.float32),
        lax.psum(d_caption_part.astype(jnp.bfloat16), "blk").astype(jnp.float32),
        lax.psum(gain_part.astype(jnp.bfloat16), "blk").astype(jnp.float32),
        lax.psum(d_head.astype(jnp.bfloat16), "blk").astype(jnp.float32),
    )
    d_caption_low = d_caption.astype(jnp.bfloat16)
    grad_caption_w = lax.dot_general(
        chosen_rows, d_caption_low, (((0,), (0,)), ((), ())), preferred_element_type=jnp.float32
    )
    d_chosen = lax.dot_general(
        d_caption_low, caption_weight, (((1,), (1,)), ((), ())), preferred_element_type=jnp.float32
    ).reshape(CLIPS, CAP, -1)
    grad_null = jnp.sum(jnp.where(dropped[:, None, None] == 1, d_chosen, 0.0), 0)
    grad_ada_w = lax.dot_general(
        cond_low,
        d_mod.astype(jnp.bfloat16),
        (((0,), (0,)), ((), ())),
        preferred_element_type=jnp.float32,
    )
    grad_ada_b = jnp.sum(d_mod, 0)
    summed = (
        lax.psum(grad_ada_w.astype(jnp.bfloat16), "dp").astype(jnp.float32),
        lax.psum(grad_ada_b.astype(jnp.bfloat16), "dp").astype(jnp.float32),
        lax.psum(grad_qkv.astype(jnp.bfloat16), "dp").astype(jnp.float32),
        lax.psum(grad_out.astype(jnp.bfloat16), "dp").astype(jnp.float32),
        lax.psum(grad_caption_w.astype(jnp.bfloat16), "dp").astype(jnp.float32),
        lax.psum(grad_gate_up.astype(jnp.bfloat16), "dp").astype(jnp.float32),
        lax.psum(grad_down.astype(jnp.bfloat16), "dp").astype(jnp.float32),
        lax.psum(grad_null.astype(jnp.bfloat16), "dp").astype(jnp.float32),
        lax.psum(gain_sum.astype(jnp.bfloat16), "dp").astype(jnp.float32),
        lax.psum(head_sum.astype(jnp.bfloat16), "dp").astype(jnp.float32),
    )
    return (result, input_grad) + tuple(summed)


def solution(mesh):
    in_specs = (
        P(("dp", "blk"), None),
        P(("dp", "blk")),
        P(None, ("dp", "blk")),
        P("dp", None),
        P("dp", None, "blk"),
        P("dp"),
        P(None, "blk"),
        P("blk", None),
        P(),
        P("blk", None),
        P("blk", None),
        P("blk", None),
        P("blk", None),
        P("blk", None),
        P(),
        P(),
        P(("dp", "blk"), None),
    )
    out_specs = (
        P(("dp", "blk"), None),
        P(("dp", "blk"), None),
        P("blk", None),
        P(),
        P("blk", None),
        P("blk", None),
        P("blk", None),
        P("blk", None),
        P("blk", None),
        P(None, "blk"),
        P(),
        P(),
    )
    return jax.shard_map(
        on_device, mesh=mesh, in_specs=in_specs, out_specs=out_specs, check_vma=False
    )
```

profile of v0, /device:TPU:1, one launch (start us, length us, event | category | flops | bytes accessed | tf_op | source)
XLA Modules:
  0.0 2703.0 jit_solution(8403620305530692315)
XLA Ops:
  15.2 33.4 %psum.112 = bf16[2,6144]{1,0:T(2,128)(2,1)} all-reduce(bf16[2,6144]{1,0:T(2,128)(2,1)} %convolution_convert_fusion.6), channel_id=1, replica_groups=mesh['dp'=4,'blk'=8] {'blk'}, use_global_device_ids=true, to_apply=%region_0.1 | all-reduce | flops 12288 | bytes 49152 | tf_op jit(solution)/shard_map/psum | solution.py:249
  57.2 150.9 %all-gather.8.cloned.1.call-done = bf16[1536,4608]{1,0:T(8,128)(2,1)} async-done(((bf16[192,4608]{1,0:T(8,128)(2,1)}), bf16[1536,4608]{1,0:T(8,128)(2,1)}) %all-gather.8.cloned.1.call-update) | async-done | bytes 14155792 | tf_op jit(solution)/shard_map/all_gather | solution.py:61
  208.1 7.2 fusion.155
  222.6 4.2 subtract_convert_fusion.1
  233.1 14.5 all-gather
  249.6 50.4 %all-reduce.7.cloned.1.call-done = bf16[256,3072]{1,0:T(8,128)(2,1)} async-done(((bf16[256,3072]{1,0:T(8,128)(2,1)}), bf16[256,3072]{1,0:T(8,128)(2,1)}) %all-reduce.7.cloned.1.call-update) | async-done | bytes 1572880 | tf_op jit(solution)/shard_map/psum | solution.py:250
  312.4 4.8 fusion.154
  317.2 47.3 %all-gather.10.cloned.1.call-done = bf16[1024,1536]{0,1:T(8,128)(2,1)} async-done(((bf16[128,1536]{0,1:T(8,128)(2,1)}), bf16[1024,1536]{0,1:T(8,128)(2,1)}) %all-gather.10.cloned.1.call-update) | async-done | bytes 3145744 | tf_op jit(solution)/shard_map/all_gather | solution.py:116
  364.4 6.1 reshape.309
  370.6 4.3 copy.80
  374.8 49.9 %all-gather.12.cloned.1.call-done = bf16[1024,1536]{1,0:T(8,128)(2,1)} async-done(((bf16[128,1536]{1,0:T(8,128)(2,1)}), bf16[1024,1536]{1,0:T(8,128)(2,1)}) %all-gather.12.cloned.1.call-update) | async-done | bytes 3145744 | tf_op jit(solution)/shard_map/all_gather | solution.py:117
  424.7 8.9 reshape.331
  433.6 7.7 copy.81
  441.3 33.3 %while.30 = (s32[]{:T(128)}, f32[24,128]{1,0:T(8,128)S(1)}, f32[24,128]{1,0:T(8,128)}, f32[128,24,64]{0,2,1:T(8,128)}, s32[128]{0:T(128)}, /*index=5*/s32[2,512]...) while((s32[]{:T(128)}, f32[24,128]{1,0:T(8,128)S(1)}, ...), condition=%wide.region_7.8_spmd.clone, body=%wide.region_4.7_spmd.clone.sunk | while | flops 423774208 | bytes 50240280 | solution.py:131
  442.1 6.1 fusion.227
  448.9 4.5 fusion.229
  453.6 4.2 fusion.231
  458.6 6.1 fusion.227
  465.5 4.4 fusion.229
  470.1 4.4 fusion.231
  474.6 4.0 add_convert_fusion
  478.6 26.5 all-gather.14.cloned.1.call-done
  505.1 3.5 multiply_reduce_fusion.13
  511.7 474.4 %all-gather.16.cloned.1.call-done = bf16[1536,8192]{1,0:T(8,128)(2,1)} async-done(((bf16[192,8192]{1,0:T(8,128)(2,1)}), bf16[1536,8192]{1,0:T(8,128)(2,1)}) %all-gather.16.cloned.1.call-update) | async-done | bytes 25165840 | tf_op jit(solution)/shard_map/all_gather | solution.py:61
  986.1 10.5 fusion.156
  1000.2 164.1 %all-gather.18.cloned.1.call-done = bf16[4096,1536]{1,0:T(8,128)(2,1)} async-done(((bf16[512,1536]{1,0:T(8,128)(2,1)}), bf16[4096,1536]{1,0:T(8,128)(2,1)}) %all-gather.18.cloned.1.call-update) | async-done | bytes 12582928 | tf_op jit(solution)/shard_map/all_gather | solution.py:61
  1164.3 6.9 multiply_reduce_fusion.11
  1174.0 10.5 multiply_convert_fusion.2
  1184.5 15.5 multiply_reduce_fusion.3
  1200.6 3.9 subtract_multiply_fusion
  1206.4 4.7 convolution_convert_fusion.9
  1215.5 38.9 %while.31 = (s32[]{:T(128)}, f32[128,24,64]{0,2,1:T(8,128)}, bf16[2,512,24,64]{1,3,2,0:T(8,128)(2,1)}, bf16[2,512,24,64]{1,3,2,0:T(8,128)(2,1)}, bf16[2,512,24,6...) while((s32[]{:T(128)}, f32[128,24,64]{0,2,1:T(8,128)}, ...), condition=%wide.region_20.21_spmd.clone, body=%wide.region_19.20_spmd.clone.sunk | while | flops 1026949120 | bytes 145617952 | solution.py:201
  1218.6 4.0 fusion.243
  1222.6 4.1 fusion.244
  1230.7 4.2 bitcast_dynamic-update-slice_fusion.5
  1237.8 4.0 fusion.243
  1241.8 4.3 fusion.244
  1250.3 4.1 bitcast_dynamic-update-slice_fusion.5
  1254.4 7.8 copy.106
  1262.2 9.2 reshape.329
  1271.5 7.8 copy.101
  1279.3 9.2 reshape.328
  1289.2 3.8 multiply_convert_fusion
  1297.8 3.6 fusion.92
  1309.7 4.6 convolution_convert_fusion.3
  1315.2 7.8 convolution_convert_fusion.2
  1323.4 3.4 fusion.103
  1326.7 17.3 reduce-scatter.19.cloned.1.call-done
  1345.6 3.6 multiply_subtract_fusion.1
  1363.5 58.1 %reduce-scatter.9.cloned.1.call-done = bf16[128,1536]{1,0:T(8,128)(2,1)} async-done(((bf16[1024,1536]{1,0:T(8,128)(2,1)}), bf16[128,1536]{1,0:T(8,128)(2,1)}) %reduce-scatter.9.cloned.1.call-update) | async-done | bytes 393232 | tf_op jit(solution)/shard_map/reduce_scatter | solution.py:209
  1421.6 8.3 convolution_convert_fusion.1
  1430.9 13.5 convolution_convert_fusion
  1448.0 66.6 %all-reduce.9.cloned.1.call-done = bf16[256,3072]{1,0:T(8,128)(2,1)} async-done(((bf16[256,3072]{1,0:T(8,128)(2,1)}), bf16[256,3072]{1,0:T(8,128)(2,1)}) %all-reduce.9.cloned.1.call-update) | async-done | bytes 1572880 | tf_op jit(solution)/shard_map/psum | solution.py:389
  1520.7 11.4 fusion.116
  1540.3 30.9 %all-reduce = (bf16[2,6144]{1,0:T(2,128)(2,1)S(1)}, bf16[7,1536]{1,0:T(8,128)(2,1)S(1)}, bf16[24]{0:T(256)(128)(2,1)S(1)}) all-reduce(bf16[2,6144]{1,0:T(2,128)(2,1)S(1)} %convolution_convert_fusion.5, bf16[7,1536]{1,0:T(8,128)(2,1)S(1)} %copy-done.69, bf16[24]{0:T(256)(128)(2,1)S(1)} %copy-done.101), channel_id=1, replica_groups=mesh['dp'=4,'blk'=8] {'blk'}, use_global_device_ids=true, to_apply=%region_27.28 | all-reduce | flops 23064 | bytes 92256 | tf_op jit(solution)/shard_map/psum | solution.py:388
  1573.6 41.3 %reduce-scatter.13.cloned.1.call-done = bf16[192,1536]{1,0:T(8,128)(2,1)} async-done(((bf16[1536,1536]{1,0:T(8,128)(2,1)}), bf16[192,1536]{1,0:T(8,128)(2,1)}) %reduce-scatter.13.cloned.1.call-update) | async-done | bytes 589840 | tf_op jit(solution)/shard_map/reduce_scatter | solution.py:78
  1615.0 210.6 %reduce-scatter.17.cloned.1.call-done = bf16[512,1536]{1,0:T(8,128)(2,1)} async-done(((bf16[4096,1536]{1,0:T(8,128)(2,1)}), bf16[512,1536]{1,0:T(8,128)(2,1)}) %reduce-scatter.17.cloned.1.call-update) | async-done | bytes 1572880 | tf_op jit(solution)/shard_map/reduce_scatter | solution.py:78
  1825.5 232.0 %reduce-scatter.11.cloned.1.call-done = bf16[192,4608]{1,0:T(8,128)(2,1)} async-done(((bf16[1536,4608]{1,0:T(8,128)(2,1)}), bf16[192,4608]{1,0:T(8,128)(2,1)}) %reduce-scatter.11.cloned.1.call-update) | async-done | bytes 1769488 | tf_op jit(solution)/shard_map/reduce_scatter | solution.py:78
  2057.5 406.5 %reduce-scatter.15.cloned.1.call-done = bf16[192,8192]{1,0:T(8,128)(2,1)} async-done(((bf16[1536,8192]{1,0:T(8,128)(2,1)}), bf16[192,8192]{1,0:T(8,128)(2,1)}) %reduce-scatter.15.cloned.1.call-update) | async-done | bytes 3145744 | tf_op jit(solution)/shard_map/reduce_scatter | solution.py:78
  2464.2 10.7 all-reduce.1
  2476.6 202.6 %all-reduce.11.cloned.1.call-done = (bf16[128,6144]{1,0:T(8,128)(2,1)}, bf16[192,4608]{1,0:T(8,128)(2,1)}, bf16[192,1536]{1,0:T(8,128)(2,1)}, bf16[512,3072]{1,0...) async-done(((bf16[128,6144]{1,0:T(8,128)(2,1)}, bf16[192,4608]{1,0:T(8,128)(2,1)}, bf16[192,1536]{1,0:T(8,128)(2,1)}, ...) | async-done | bytes 11927568 | tf_op jit(solution)/shard_map/psum | solution.py:409
  2679.2 3.5 convert_element_type.220
  2686.2 3.5 convert_element_type.228
  2689.7 3.4 convert_element_type.230
  (390 shorter events, 137.6 us)
Async XLA Ops:
  7.2 200.9 %all-gather.8.cloned.1.call-start = ((), (), s32[]{:S(2)}) async-start(), calls=%async_computation.6 | async-start | bytes 15925248 | tf_op jit(solution)/shard_map/all_gather | solution.py:61
  7.9 292.0 %all-reduce.7.cloned.1.call-start = ((), (), s32[]{:S(2)}) async-start(), calls=%async_computation.9 | async-start | bytes 3145728 | tf_op jit(solution)/shard_map/psum | solution.py:250
  10.6 40.0 %copy-start.23 = (bf16[128,1536]{1,0:T(8,128)(2,1)S(1)}, bf16[128,1536]{1,0:T(8,128)(2,1)}, u32[]{:S(2)}) copy-start(bf16[128,1536]{1,0:T(8,128)(2,1)} %param.21) | copy-start | bytes 1179652
  10.6 40.2 %copy-start.102 = (s32[3,128]{1,0:T(4,128)S(1)}, s32[3,128]{1,0:T(4,128)}, u32[]{:S(2)}) copy-start(s32[3,128]{1,0:T(4,128)} %param.23) | copy-start | bytes 4612
  12.8 351.6 %all-gather.10.cloned.1.call-start = ((), (), s32[]{:S(2)}) async-start(), calls=%async_computation.7 | async-start | bytes 3538944 | tf_op jit(solution)/shard_map/all_gather | solution.py:116
  52.3 170.3 %copy-start.60 = (f32[128,32]{0,1:T(8,128)}, f32[128,32]{0,1:T(8,128)S(1)}, u32[]{:S(2)}) copy-start(f32[128,32]{0,1:T(8,128)S(1)} %get-tuple-element.378) | copy-start | bytes 49156
  57.2 159.5 %copy-start.62 = (f32[1536]{0:T(1024)S(1)}, f32[1536]{0:T(1024)}, u32[]{:S(2)}) copy-start(f32[1536]{0:T(1024)} %get-tuple-element.287) | copy-start | bytes 18436
  57.2 159.5 %copy-start.64 = (f32[1536]{0:T(1024)S(1)}, f32[1536]{0:T(1024)}, u32[]{:S(2)}) copy-start(f32[1536]{0:T(1024)} %get-tuple-element.288) | copy-start | bytes 18436
  215.5 7.1 copy-start.91
  215.5 7.1 copy-start.92
  216.7 5.9 copy-start.77
  228.6 4.6 copy-start.70
  228.6 196.2 %all-gather.12.cloned.1.call-start = ((), (), s32[]{:S(2)}) async-start(), calls=%async_computation.8 | async-start | bytes 3538944 | tf_op jit(solution)/shard_map/all_gather | solution.py:117
  230.6 70.8 %copy-start.66 = (f32[1536]{0:T(1024)S(1)}, f32[1536]{0:T(1024)}, u32[]{:S(2)}) copy-start(f32[1536]{0:T(1024)} %get-tuple-element.286) | copy-start | bytes 18436
  230.6 274.5 %all-gather.14.cloned.1.call-start = ((), (), s32[]{:S(2)}) async-start(), calls=%async_computation.10 | async-start | bytes 5308416 | tf_op jit(solution)/shard_map/all_gather | solution.py:61
  231.2 754.9 %all-gather.16.cloned.1.call-start = ((), (), s32[]{:S(2)}) async-start(), calls=%async_computation.11 | async-start | bytes 28311552 | tf_op jit(solution)/shard_map/all_gather | solution.py:61
  231.8 932.6 %all-gather.18.cloned.1.call-start = ((), (), s32[]{:S(2)}) async-start(), calls=%async_computation.12 | async-start | bytes 14155776 | tf_op jit(solution)/shard_map/all_gather | solution.py:61
  232.5 1111.5 %reduce-scatter.19.cloned.1.call-start = ((), (), s32[]{:S(2)}) async-start(), calls=%async_computation.19 | async-start | bytes 3538944
  301.3 9.0 copy-start.83
  442.1 6.1 copy-start.15
  448.9 4.5 copy-start.52
  448.9 4.7 copy-start.1
  448.9 4.7 copy-start.16
  453.4 4.4 copy-start.53
  458.6 6.1 copy-start.15
  465.5 4.5 copy-start.52
  465.5 4.7 copy-start.1
  465.5 4.7 copy-start.16
  470.0 4.6 copy-start.53
  505.1 4.4 copy-start.6
  505.1 4.4 copy-start.24
  505.1 4.4 copy-start.58
  505.1 4.8 copy-start.54
  505.1 5.7 copy-start.75
  1000.2 171.1 %copy-start.76 = (f32[1536]{0:T(1024)S(1)}, f32[1536]{0:T(1024)}, u32[]{:S(2)}) copy-start(f32[1536]{0:T(1024)} %get-tuple-element.284) | copy-start | bytes 18436
  1164.3 7.0 copy-start.7
  1164.3 7.0 copy-start.30
  1164.3 7.9 copy-start.20
  1184.5 16.1 copy-start.59
  1184.5 16.1 copy-start.90
  1206.4 6.6 copy-start.55
  1222.5 4.3 copy-start.35
  1228.0 6.9 copy-start.36
  1241.8 4.3 copy-start.2
  1241.8 4.6 copy-start.35
  1247.6 6.8 copy-start.36
  1271.4 150.1 %reduce-scatter.9.cloned.1.call-start = ((), (), s32[]{:S(2)}) async-start(), calls=%async_computation.13 | async-start | bytes 3538944 | tf_op jit(solution)/shard_map/reduce_scatter | solution.py:209
  1288.5 226.0 %all-reduce.9.cloned.1.call-start = ((), (), s32[]{:S(2)}) async-start(), calls=%async_computation.16 | async-start | bytes 3145728 | tf_op jit(solution)/shard_map/psum | solution.py:389
  1297.8 5.9 copy-start.67
  1297.8 5.9 copy-start.84
  1303.7 4.5 copy-start.33
  1309.6 305.4 %reduce-scatter.13.cloned.1.call-start = ((), (), s32[]{:S(2)}) async-start(), calls=%async_computation.15 | async-start | bytes 5308416 | tf_op jit(solution)/shard_map/reduce_scatter | solution.py:78
  1314.2 511.3 %reduce-scatter.17.cloned.1.call-start = ((), (), s32[]{:S(2)}) async-start(), calls=%async_computation.18 | async-start | bytes 14155776 | tf_op jit(solution)/shard_map/reduce_scatter | solution.py:78
  1323.0 22.5 copy-start.61
  1323.1 734.5 %reduce-scatter.11.cloned.1.call-start = ((), (), s32[]{:S(2)}) async-start(), calls=%async_computation.14 | async-start | bytes 15925248 | tf_op jit(solution)/shard_map/reduce_scatter | solution.py:78
  1349.1 8.8 copy-start.63
  1349.1 8.8 copy-start.65
  1358.0 63.6 %copy-start.26 = (bf16[128,1536]{1,0:T(8,128)(2,1)S(1)}, bf16[128,1536]{1,0:T(8,128)(2,1)}, u32[]{:S(2)}) copy-start(bf16[128,1536]{1,0:T(8,128)(2,1)} %fusion.110) | copy-start | bytes 1179652
  1429.9 1034.2 %reduce-scatter.15.cloned.1.call-start = ((), (), s32[]{:S(2)}) async-start(), calls=%async_computation.17 | async-start | bytes 28311552 | tf_op jit(solution)/shard_map/reduce_scatter | solution.py:78
  1444.5 72.7 %copy-start.98 = (pred[2]{0:T(512)(128)(4,1)S(1)}, pred[2]{0:T(512)(128)(4,1)}, u32[]{:S(2)}) copy-start(pred[2]{0:T(512)(128)(4,1)} %copy-done.97) | copy-start | bytes 10
  1444.5 1234.7 %all-reduce.11.cloned.1.call-start = ((), (), s32[]{:S(2)}) async-start(), calls=%async_computation.20 | async-start | bytes 23855104 | tf_op jit(solution)/shard_map/psum | solution.py:409
  1520.7 12.1 copy-start.82
  1520.7 12.7 copy-start.81
  1532.1 6.9 copy-start.72
  (74 other events, 197.3 us)
Sparse Core Ops, SparseCore 0:
  10.2 197.8 all-gather.7
  212.2 87.7 all-reduce.6
  302.6 61.8 all-gather.9
  366.5 58.2 all-gather.11
  426.8 78.3 all-gather.13
  506.5 479.5 all-gather.15
  988.3 175.9 all-gather.17
  1271.6 72.3 reduce-scatter.18
  1348.2 73.3 reduce-scatter.8
  1425.5 89.0 all-reduce.8
  1518.8 96.1 reduce-scatter.12
  1618.4 207.0 reduce-scatter.16
  1829.2 228.2 reduce-scatter.10
  2061.2 402.7 reduce-scatter.14
  2468.3 210.9 all-reduce.10
where the time goes:
time: 2710 us; the launch traced here: 2700 us
  waiting for transfers between devices  2200 us (81%)
  matrix products  195 us (7%)
  local copies, waits for them, and re-layouts  113 us (4%)
  blocking collectives  89.6 us (3%)
  other arithmetic  86.7 us (3%)
    reduce_scatter x4, waiting for transfers between devices, weight_grad(): lax.psum_scatter(lax.dot_general(left_rows, grad_rows, (((0,), (0,)), (()...  890 us
    all_gather x4, waiting for transfers between devices, forward_product(): lax.all_gather(local_rows, 'blk', axis=0, tiled=True)  816 us
    psum x1, waiting for transfers between devices, on_device(): lax.psum(grad_ada_w.astype(jnp.bfloat16), 'dp').astype(jnp.float32)  203 us
    psum x1, waiting for transfers between devices, on_device(): lax.psum(d_caption_part.astype(jnp.bfloat16), 'blk').astype(jnp.float32)  66.6 us
    reduce_scatter x1, waiting for transfers between devices, self_backward(): lax.psum_scatter(key_terms[1].reshape(length, HEADS * HEAD).astype(jnp.bf...  58.1 us
  transfers between devices with their start and end apart: 15, of which 15 were waited for; matrix products, arithmetic and copies ran while one was open for 10% of the time, Pallas kernels for 0%

commit v1 on v0

v1 whole, which is shorter than its diff:
```python
import functools

import jax
import jax.numpy as jnp
from jax import lax
from jax.experimental import pallas as pl
from jax.experimental.pallas import tpu as pltpu
from jax.sharding import Mesh, PartitionSpec as P

HEADS = 24
HEAD = 64
D = 1536
FF = 4096
CAP = 128
CLIPS = 2
PAIR = 2 * HEAD

PRECISE = lax.Precision.HIGHEST
EPSILON = 1e-06
NEGATIVE = -1e30
F32 = jnp.float32
LOW = jnp.bfloat16
SWAP = [(0, 1), (1, 0)]


def inv_root(values):
    return lax.rsqrt(jnp.mean(values * values, -1, keepdims=True) + EPSILON)


def unit_rows(values):
    return values * inv_root(values)


def norm_back(grad_in, values, gain):
    root = inv_root(values)
    normed = values * root
    inner = grad_in * gain
    back = root * (inner - normed * jnp.mean(inner * normed, -1, keepdims=True))
    return back, jnp.sum(grad_in * normed, 0)


def rounded(values):
    return lax.reduce_precision(values, 8, 7)


def low(values):
    return rounded(values).astype(LOW)


def dot(a, b, dims=((1,), (0,))):
    return lax.dot_general(a, b, (dims, ((), ())), preferred_element_type=F32)


def nt(a, b):
    return lax.dot_general(a, b, (((1,), (1,)), ((), ())), preferred_element_type=F32)


def tn(a, b):
    return lax.dot_general(a, b, (((0,), (0,)), ((), ())), preferred_element_type=F32)


def nn(a, b):
    return lax.dot_general(a, b, (((1,), (0,)), ((), ())), preferred_element_type=F32)


def cross_bias(seg_col, count):
    clip = lax.broadcasted_iota(jnp.int32, (1, count), 1) // CAP
    return jnp.where(seg_col == clip, 0.0, NEGATIVE)


def forward_near(q_ref, k_ref, v_ref, ck_ref, cv_ref, sq_ref, sk_ref, o_ref, oc_ref, st_ref):
    seg_col = sq_ref[...]
    bias = jnp.where(seg_col == sk_ref[...], 0.0, NEGATIVE)
    bias_cross = cross_bias(seg_col, ck_ref.shape[0])
    for h in range(2):
        at = slice(h * HEAD, (h + 1) * HEAD)
        q = q_ref[:, at]
        s = nt(q, k_ref[:, at]) + bias
        m = jnp.max(s, -1, keepdims=True)
        e = jnp.exp(s - m)
        st_ref[0, :, h : h + 1] = m
        st_ref[0, :, 2 + h : 3 + h] = jnp.sum(e, -1, keepdims=True)
        o_ref[:, at] = nn(e.astype(LOW), v_ref[:, at])
        s = nt(q, ck_ref[:, at]) + bias_cross
        m = jnp.max(s, -1, keepdims=True)
        e = jnp.exp(s - m)
        total = jnp.sum(e, -1, keepdims=True)
        st_ref[0, :, 4 + h : 5 + h] = m + jnp.log(total)
        oc_ref[:, at] = nn(e.astype(LOW), cv_ref[:, at]) / total


def forward_far(
    count, q_ref, k_ref, v_ref, sq_ref, sk_ref, o_ref, oc_ref, st_ref, gate_ref, os_ref, mix_ref, lse_ref, m_ref, l_ref
):
    step = pl.program_id(1)

    @pl.when(step == 0)
    def _():
        os_ref[...] = o_ref[...]
        m_ref[...] = st_ref[0, :, 0:2]
        l_ref[...] = st_ref[0, :, 2:4]

    bias = jnp.where(sq_ref[...] == sk_ref[0], 0.0, NEGATIVE)
    for h in range(2):
        at = slice(h * HEAD, (h + 1) * HEAD)
        s = nt(q_ref[:, at], k_ref[0, :, at]) + bias
        before = m_ref[:, h : h + 1]
        m = jnp.maximum(before, jnp.max(s, -1, keepdims=True))
        e = jnp.exp(s - m)
        factor = jnp.exp(before - m)
        m_ref[:, h : h + 1] = m
        l_ref[:, h : h + 1] = l_ref[:, h : h + 1] * factor + jnp.sum(e, -1, keepdims=True)
        os_ref[:, at] = os_ref[:, at] * factor + nn(e.astype(LOW), v_ref[0, :, at])

    @pl.when(step == count - 1)
    def _():
        for h in range(2):
            at = slice(h * HEAD, (h + 1) * HEAD)
            total = l_ref[:, h : h + 1]
            out = os_ref[:, at] / total
            os_ref[:, at] = out
            mix_ref[:, at] = (out + gate_ref[:, at] * oc_ref[:, at]).astype(LOW)
            lse_ref[0, :, h : h + 1] = m_ref[:, h : h + 1] + jnp.log(total)


def backward_far(
    q_ref, g_ref, os_ref, oc_ref, lse_ref, st_ref, gate_ref, k_ref, v_ref, ck_ref, cv_ref, sq_ref, sk_ref,
    dq_ref, dk_ref, dv_ref, dck_ref, dcv_ref, dh_ref, delta_ref,
):
    step = pl.program_id(1)
    seg_col = sq_ref[...]
    scaling = HEAD**-0.5

    @pl.when(step == 0)
    def _():
        bias_cross = cross_bias(seg_col, ck_ref.shape[0])
        g = g_ref[...].astype(F32)
        dh_ref[...] = jnp.sum(g * oc_ref[...], 0, keepdims=True)
        for h in range(2):
            at = slice(h * HEAD, (h + 1) * HEAD)
            gh = g[:, at]
            delta_ref[0, :, h : h + 1] = jnp.sum(gh * os_ref[:, at], -1, keepdims=True)
            gc = (gate_ref[:, at] * gh).astype(LOW)
            delta = jnp.sum(gc.astype(F32) * oc_ref[:, at], -1, keepdims=True)
            q = q_ref[:, at]
            p = jnp.exp(nt(q, ck_ref[:, at]) + bias_cross - st_ref[0, :, 4 + h : 5 + h])
            ds = (p * (nt(gc, cv_ref[:, at]) - delta)).astype(LOW)
            dq_ref[:, at] = nn(ds, ck_ref[:, at]) * scaling
            dck_ref[:, at] = tn(ds, q).astype(dck_ref.dtype)
            dcv_ref[:, at] = tn(p.astype(LOW), gc).astype(dcv_ref.dtype)

    bias = jnp.where(seg_col == sk_ref[0], 0.0, NEGATIVE)
    for h in range(2):
        at = slice(h * HEAD, (h + 1) * HEAD)
        q = q_ref[:, at]
        g = g_ref[:, at]
        k = k_ref[0, :, at]
        p = jnp.exp(nt(q, k) + bias - lse_ref[0, :, h : h + 1])
        ds = (p * (nt(g, v_ref[0, :, at]) - delta_ref[0, :, h : h + 1])).astype(LOW)
        dq_ref[:, at] += nn(ds, k) * scaling
        dk_ref[0, :, at] = tn(ds, q).astype(dk_ref.dtype)
        dv_ref[0, :, at] = tn(p.astype(LOW), g).astype(dv_ref.dtype)


def backward_near(q_ref, g_ref, lse_ref, delta_ref, k_ref, v_ref, sq_ref, sk_ref, dp_ref, dq_ref, dk_ref, dv_ref):
    bias = jnp.where(sq_ref[...] == sk_ref[...], 0.0, NEGATIVE)
    scaling = HEAD**-0.5
    for h in range(2):
        at = slice(h * HEAD, (h + 1) * HEAD)
        q = q_ref[:, at]
        g = g_ref[:, at]
        k = k_ref[:, at]
        p = jnp.exp(nt(q, k) + bias - lse_ref[0, :, h : h + 1])
        ds = (p * (nt(g, v_ref[:, at]) - delta_ref[0, :, h : h + 1])).astype(LOW)
        dq_ref[:, at] = dp_ref[:, at] + nn(ds, k) * scaling
        dk_ref[:, at] = tn(ds, q)
        dv_ref[:, at] = tn(p.astype(LOW), g)


def attention_calls(tokens, width, capt, far):
    pairs = width // PAIR
    sds = jax.ShapeDtypeStruct

    def cols(rows):
        return pl.BlockSpec((rows, PAIR), lambda i, *r: (0, i))

    def stat(n):
        return pl.BlockSpec((1, tokens, n), lambda i, *r: (i, 0, 0))

    seg_col = pl.BlockSpec((tokens, 1), lambda i, *r: (0, 0))
    seg_row = pl.BlockSpec((1, tokens), lambda i, *r: (0, 0))
    far_cols = pl.BlockSpec((1, tokens, PAIR), lambda i, r: (r, 0, i))
    far_row = pl.BlockSpec((1, 1, tokens), lambda i, r: (r, 0, 0))
    gate = cols(1)
    tok, cap = cols(tokens), cols(capt)

    def cost(keys, products):
        return pl.CostEstimate(
            flops=2 * tokens * keys * width * products,
            bytes_accessed=8 * tokens * width * 4,
            transcendentals=tokens * keys * (width // HEAD),
        )

    params = pltpu.CompilerParams(vmem_limit_bytes=48 * 1024 * 1024)
    near = pl.pallas_call(
        forward_near,
        grid=(pairs,),
        in_specs=[tok, tok, tok, cap, cap, seg_col, seg_row],
        out_specs=[tok, tok, stat(8)],
        out_shape=[sds((tokens, width), F32), sds((tokens, width), F32), sds((pairs, tokens, 8), F32)],
        compiler_params=params,
        cost_estimate=cost(tokens + capt, 2),
        name="attn_near",
    )
    away = pl.pallas_call(
        functools.partial(forward_far, far),
        grid=(pairs, far),
        in_specs=[tok, far_cols, far_cols, seg_col, far_row, tok, tok, stat(8), gate],
        out_specs=[tok, tok, stat(2)],
        out_shape=[sds((tokens, width), F32), sds((tokens, width), LOW), sds((pairs, tokens, 2), F32)],
        scratch_shapes=[pltpu.VMEM((tokens, 2), F32), pltpu.VMEM((tokens, 2), F32)],
        compiler_params=params,
        cost_estimate=cost(tokens * far, 2),
        name="attn_far",
    )
    back_away = pl.pallas_call(
        backward_far,
        grid=(pairs, far),
        in_specs=[tok, tok, tok, tok, stat(2), stat(8), gate, far_cols, far_cols, cap, cap, seg_col, far_row],
        out_specs=[tok, far_cols, far_cols, cap, cap, gate, stat(2)],
        out_shape=[
            sds((tokens, width), F32),
            sds((far, tokens, width), LOW),
            sds((far, tokens, width), LOW),
            sds((capt, width), F32),
            sds((capt, width), F32),
            sds((1, width), F32),
            sds((pairs, tokens, 2), F32),
        ],
        compiler_params=params,
        cost_estimate=cost(tokens * far + capt, 5),
        name="attn_back_far",
    )
    back_near = pl.pallas_call(
        backward_near,
        grid=(pairs,),
        in_specs=[tok, tok, stat(2), stat(2), tok, tok, seg_col, seg_row, tok],
        out_specs=[tok, tok, tok],
        out_shape=[sds((tokens, width), F32)] * 3,
        compiler_params=params,
        cost_estimate=cost(tokens, 5),
        name="attn_back_near",
    )
    return near, away, back_away, back_near


def swap(value, axis):
    return lax.ppermute(value, axis, SWAP)


def pair_stack(value, axis, dim):
    other = swap(value, axis)
    first = lax.axis_index(axis) == 0
    return jnp.concatenate([jnp.where(first, value, other), jnp.where(first, other, value)], dim)


def pair_reduce(value, axis, dim):
    half = value.shape[dim] // 2
    me = lax.axis_index(axis)
    sent = lax.dynamic_slice_in_dim(value, (1 - me) * half, half, dim).astype(LOW)
    kept = lax.dynamic_slice_in_dim(value, me * half, half, dim)
    return kept.astype(F32) + swap(sent, axis).astype(F32)


def on_device(
    far_count,
    lead,
    hidden,
    segments,
    positions,
    condition,
    captions,
    dropped,
    null_caption,
    ada_weight,
    ada_bias,
    qkv_weight,
    out_weight,
    caption_weight,
    gate_up,
    down_weight,
    gains,
    head_gate,
    cotangent,
):
    outer = far_count
    me_c = lax.axis_index("p") * 2 + lax.axis_index("y")
    me_o = lax.axis_index("o")
    core = lax.axis_index("core")
    me_x = lax.axis_index("x")
    me_b = lax.axis_index(("p", "y", "o") if lead else ("o", "p", "y"))
    tokens = hidden.shape[0]
    square = 4 * tokens
    width = D // 4

    def blocks(value):
        rest = value.shape[-1] // (4 * outer)
        if lead:
            return value.reshape(value.shape[:-1] + (4, outer, rest)).swapaxes(-3, -2)
        return value.reshape(value.shape[:-1] + (outer, 4, rest))

    def unblocks(value):
        if lead:
            value = value.swapaxes(-3, -2)
        return value.reshape(value.shape[:-3] + (-1,))

    def row_blocks(value):
        rest = value.shape[0] // (4 * outer)
        if lead:
            return value.reshape((4, outer, rest) + value.shape[1:]).swapaxes(0, 1)
        return value.reshape((outer, 4, rest) + value.shape[1:])

    def row_unblocks(value):
        if lead:
            value = value.swapaxes(0, 1)
        return value.reshape((-1,) + value.shape[3:])

    def my_cols(value):
        mine = lax.dynamic_index_in_dim(blocks(value), me_c, value.ndim, keepdims=False)
        return mine.reshape(value.shape[:-1] + (-1,))

    def put_cols(value):
        split = value.reshape(value.shape[:-1] + (outer, 1, value.shape[-1] // outer))
        here = (jnp.arange(4) == me_c).reshape(4, 1)
        return unblocks(jnp.where(here, split, 0.0))

    def outer_stack(value):
        if outer == 2:
            return pair_stack(value[None], "o", 0)
        return lax.all_gather(value, "o", axis=0)

    def outer_reduce(value):
        if outer == 2:
            return pair_reduce(value, "o", 0)[0]
        return lax.psum_scatter(value.astype(LOW), "o", scatter_dimension=0).astype(F32)

    def outer_sum(value):
        if outer == 2:
            return rounded(value) + swap(low(value), "o").astype(F32)
        return lax.psum(low(value), "o").astype(F32)

    def outer_sum_wide(value):
        if outer == 2:
            return value + swap(value, "o")
        return lax.psum(value, "o")

    def far(value):
        return jnp.stack([lax.ppermute(value, "o", [(i, i ^ r) for i in range(outer)]) for r in range(1, outer)])

    def far_back(value):
        total = 0.0
        for r in range(1, outer):
            total = total + lax.ppermute(value[r - 1], "o", [(i, i ^ r) for i in range(outer)]).astype(F32)
        return total

    def gather_square(rows):
        half = rows.shape[0] // 2
        a, b = rows[:half], rows[half:]
        ya, pb = swap(a, "y"), swap(b, "p")
        pa = swap(jnp.concatenate([a, ya]), "p")
        yb = swap(jnp.concatenate([b, pb]), "y")
        return jnp.concatenate([a, b, ya, yb[:half], pa[:half], pb, pa[half:], yb[half:]])

    def scatter_square(full):
        count = full.shape[0] // 4
        half = count // 2
        a = [full[i * count : i * count + half] for i in range(4)]
        b = [full[i * count + half : (i + 1) * count] for i in range(4)]
        ra = swap(jnp.concatenate([a[2], a[3]]).astype(LOW), "p").astype(F32)
        rb = swap(jnp.concatenate([b[1], b[3]]).astype(LOW), "y").astype(F32)
        a0 = a[0] + ra[:half] + swap((a[1] + ra[half:]).astype(LOW), "y").astype(F32)
        b0 = b[0] + rb[:half] + swap((b[2] + rb[half:]).astype(LOW), "p").astype(F32)
        return jnp.concatenate([a0, b0])

    def square_exchange(value):
        result = jnp.zeros_like(value)
        for r, axes in ((0, ()), (1, ("y",)), (2, ("p",)), (3, ("p", "y"))):
            piece = lax.dynamic_slice_in_dim(value, me_c ^ r, 1, 0)
            if r:
                piece = lax.ppermute(piece, axes if r == 3 else axes[0], [(i, i ^ r) for i in range(4)] if r == 3 else SWAP)
            result = lax.dynamic_update_slice_in_dim(result, piece, me_c ^ r, 0)
        return result

    def square_sum(own_rows, shared):
        count = own_rows.shape[0]
        split = own_rows.reshape(count, 4, -1)
        width_in = split.shape[2]
        whole = jnp.concatenate([split.reshape(count * 4, width_in), shared.reshape(-1, width_in)])
        for axis, order in (("y", (1, 0, 3, 2)), ("p", (2, 3, 0, 1))):
            other = swap(whole, axis)
            order = [4 * i + j for i in range(count) for j in order]
            whole = whole + jnp.concatenate([other[i : i + 1] for i in order] + [other[count * 4 :]])
        return whole[: count * 4].reshape(count, -1), whole[count * 4 :].reshape(-1)

    def group_sum(value):
        value = rounded(value) + swap(low(value), "y").astype(F32)
        value = rounded(value) + swap(low(value), "p").astype(F32)
        return outer_sum(value)

    def all_dp(value):
        return pair_stack(pair_stack(value[None], "x", 0)[None], "core", 0)

    def fetch_qkv(weight):
        quarter = weight.shape[0] // 4
        mine = lax.dynamic_slice_in_dim(weight, (me_x * 2 + core) * quarter, quarter, 0)
        sent = jnp.moveaxis(blocks(mine.reshape(quarter, 3, D)), -2, 0)
        part = outer_stack(square_exchange(sent.reshape(4, quarter, -1)))
        part = pair_stack(part[None], "x", 0)
        other = swap(part, "core")
        whole = jnp.stack([jnp.where(core == i, part, other) for i in range(2)], 1)
        whole = whole.transpose(2, 3, 0, 1, 4, 5)
        return row_unblocks(whole.reshape(whole.shape[:2] + (4 * quarter, whole.shape[-1])))

    def fetch_rows(weight):
        quarter = weight.shape[1] // 4
        mine = lax.dynamic_slice_in_dim(weight, (core * 2 + me_x) * quarter, quarter, 1)
        part = outer_stack(mine).reshape(outer * weight.shape[0], quarter)
        return pair_stack(pair_stack(part, "x", 1), "core", 1)

    def fetch_gate_up(weight):
        rows = weight.shape[0]
        split = blocks(weight.reshape(rows, 2, FF))
        f = split.shape[-1]
        mine = lax.dynamic_slice(
            split, (0, core, me_x * (outer // 2), 0, 0), (rows, 1, outer // 2, 4, f)
        )[:, 0]
        sent = jnp.moveaxis(mine, -2, 0).reshape(4, rows, -1)
        part = row_unblocks(outer_stack(square_exchange(sent)))
        return pair_stack(pair_stack(part, "x", 1), "core", 1)

    def finish(part, dim):
        mine = pair_stack(low(part), "x", dim)
        return pair_stack(mine, "core", dim).astype(F32)

    def two_cores(value):
        return jnp.concatenate([value, swap(value, "core")])

    def two_cores_half(value):
        half = value.shape[1] // 2
        sent = lax.dynamic_slice_in_dim(value, (1 - core) * half, half, 1)
        kept = lax.dynamic_slice_in_dim(value, core * half, half, 1)
        return jnp.concatenate([kept, swap(sent, "core")])

    def weight_grad(left_both, grad):
        both = two_cores_half(grad)
        return pair_reduce(dot(left_both, both, ((0,), (0,))).astype(LOW), "x", 1)

    cond_rows = ada_weight.shape[0]
    cond_low = lax.dynamic_slice_in_dim(jax.nn.silu(condition), me_b * cond_rows, cond_rows, 1).astype(LOW)
    mod_sum = group_sum(dot(cond_low, ada_weight))
    modulation = mod_sum + ada_bias
    cond_all = all_dp(cond_low).reshape(-1, cond_rows)

    ints = jnp.concatenate([segments[None], positions]).T
    ints = gather_square(ints)
    seg_square, pos_square = ints[:, 0], ints[:, 1:].T
    seg_far = far(seg_square[None])
    seg_col, seg_row = seg_square[:, None], seg_square[None]

    source = hidden.astype(F32)
    hidden_square = gather_square(hidden).astype(F32)
    qkv_mine = fetch_qkv(qkv_weight)

    chosen = jnp.where(dropped[:, None, None] == 1, null_caption[None], captions)
    chosen_rows = chosen.reshape(CLIPS * CAP, chosen.shape[2])
    caption_part = dot(chosen_rows, caption_weight)
    split = blocks(caption_part.reshape(CLIPS * CAP, 2, D))
    split = jnp.moveaxis(split, -2, 0).reshape(4 * CLIPS * CAP, -1)

    def scatter_place(full):
        count = full.shape[0] // 4
        parts = [lax.dynamic_slice_in_dim(full, (me_c ^ r) * count, count, 0) for r in range(4)]
        return scatter_square(jnp.concatenate(parts))

    caption_mine = outer_sum(scatter_place(split))

    outw = fetch_rows(out_weight)
    gate_up_mine = fetch_gate_up(gate_up)
    down_mine = fetch_rows(down_weight)

    first_clip = seg_square[:, None] == 0

    def per_token(rows, sel):
        return jnp.where(sel, rows[0:1], rows[1:2])

    scale_square = per_token(modulation[:, :D], first_clip)
    first_in = (unit_rows(hidden_square) * gains[0] * (1.0 + scale_square)).astype(LOW)
    projected = dot(first_in, qkv_mine)
    q_raw, k_raw, v_raw = projected[:, :width], projected[:, width : 2 * width], projected[:, 2 * width :]
    ck_raw = caption_mine[:, :width]
    sums, sums_c = square_sum(
        jnp.stack([jnp.sum(q_raw * q_raw, -1), jnp.sum(k_raw * k_raw, -1)]), jnp.sum(ck_raw * ck_raw, -1)
    )
    inv = lax.rsqrt(sums / D + EPSILON)[:, :, None]
    inv_q, inv_k = inv[0], inv[1]
    inv_c = lax.rsqrt(sums_c / D + EPSILON)[:, None]
    gain_q, gain_k, gain_c = (my_cols(gains[i])[None] for i in (4, 5, 6))

    pair_index = jnp.arange(HEAD) // 2
    frequency = 10000.0 ** (-3.0 * (pair_index // 3).astype(F32) / (HEAD // 2))
    select = ((pair_index % 3)[None, :] == jnp.arange(3)[:, None]).astype(F32)
    angles = jnp.dot(pos_square.astype(F32).T, select, precision=PRECISE) * frequency[None, :]
    cosine = jnp.tile(jnp.cos(angles), (1, width // HEAD))
    sine = jnp.tile(jnp.sin(angles), (1, width // HEAD))
    lane = jnp.arange(width)
    turn = jnp.where(
        (lane[:, None] ^ 1) == lane[None, :], jnp.where(lane[None, :] % 2 == 0, -1.0, 1.0), 0.0
    ).astype(F32)

    def rotate(values, sign):
        return values * cosine + jnp.dot(values, turn, precision=PRECISE) * (sign * sine)

    unit_q, unit_k = q_raw * inv_q, k_raw * inv_k
    scaling = HEAD**-0.5
    queries = rotate(unit_q * gain_q, 1.0).astype(LOW) * jnp.asarray(scaling, LOW)
    keys = rotate(unit_k * gain_k, 1.0).astype(LOW)
    values = v_raw.astype(LOW)
    unit_c = ck_raw * inv_c
    cap_keys = (unit_c * gain_c).astype(LOW)
    cap_values = caption_mine[:, width:].astype(LOW)
    keys_far, values_far = far(keys), far(values)

    near, away, back_away, back_near = attention_calls(square, width, CLIPS * CAP, outer - 1)
    out_near, out_cross, stats = near(queries, keys, values, cap_keys, cap_values, seg_col, seg_row)
    head_tanh = jnp.tanh(head_gate)
    gate_row = my_cols(jnp.repeat(head_tanh, HEAD))[None]
    out_self, mixed, lse = away(
        queries, keys_far, values_far, seg_col, seg_far, out_near, out_cross, stats, gate_row
    )
    mixed_both = two_cores(mixed)
    attended = scatter_square(dot(mixed, outw))

    clip_here = segments[:, None] == 0
    gate_attn = jnp.tanh(per_token(modulation[:, D : 2 * D], clip_here))
    scale_ffn = per_token(modulation[:, 2 * D : 3 * D], clip_here)
    gate_ffn = jnp.tanh(per_token(modulation[:, 3 * D :], clip_here))
    attn_unit = unit_rows(attended)
    middle = source + gate_attn * attn_unit * gains[1]
    unit_mid = unit_rows(middle)
    second_low = (unit_mid * gains[2] * (1.0 + scale_ffn)).astype(LOW)
    second_in = gather_square(second_low)
    second_both = two_cores(second_in)
    hidden_units = FF // 4
    gate_values = dot(second_in, gate_up_mine)
    gate_part, up_part = gate_values[:, :hidden_units], gate_values[:, hidden_units:]
    activated = (jax.nn.silu(gate_part) * up_part).astype(LOW)
    activated_both = two_cores(activated)
    lowered = scatter_square(dot(activated, down_mine))
    low_unit = unit_rows(lowered)
    result = middle + gate_ffn * low_unit * gains[3]

    upstream = cotangent.astype(F32)
    d_gate_ffn = upstream * low_unit * gains[3] * (1.0 - gate_ffn * gate_ffn)
    d_lowered, grad_gain3 = norm_back(upstream * gate_ffn, lowered, gains[3])
    d_lowered_sq = gather_square(d_lowered.astype(LOW))
    d_activated = dot(d_lowered_sq, down_mine, ((1,), (1,)))
    sigmoid = jax.nn.sigmoid(gate_part)
    d_gate_part = d_activated * up_part * sigmoid * (1.0 + gate_part * (1.0 - sigmoid))
    d_up_part = d_activated * gate_part * sigmoid
    d_gate_values = jnp.concatenate([d_gate_part, d_up_part], 1).astype(LOW)
    d_second = scatter_square(dot(d_gate_values, gate_up_mine, ((1,), (1,))))

    down_part = weight_grad(activated_both, d_lowered_sq)
    grad_down = finish(outer_reduce(down_part.reshape(outer, -1, D // 4)), 1)
    up_quarter = weight_grad(second_both, d_gate_values)
    up_quarter = outer_reduce(row_blocks(up_quarter))
    up_quarter = square_exchange(low(up_quarter))
    rows_up = gate_up.shape[0]
    half_outer = outer // 2
    up_quarter = up_quarter.reshape(4, rows_up, half_outer, -1).transpose(1, 2, 0, 3)

    def finish_gate_up(part):
        if not lead:
            return finish(part.reshape(rows_up, -1).astype(F32), 1)
        whole = finish(part.astype(F32)[:, None], 1)
        whole = whole.reshape(rows_up, 2, outer, 4, -1)
        return unblocks(whole).reshape(rows_up, -1)

    grad_gate_up = finish_gate_up(up_quarter)

    d_scale_ffn = d_second * unit_mid * gains[2]
    d_middle_norm, grad_gain2 = norm_back(d_second * (1.0 + scale_ffn), middle, gains[2])
    d_middle = upstream + d_middle_norm
    d_gate_attn = d_middle * attn_unit * gains[1] * (1.0 - gate_attn * gate_attn)
    d_attended, grad_gain1 = norm_back(d_middle * gate_attn, attended, gains[1])

    d_attended_sq = gather_square(d_attended.astype(LOW))
    d_mixed = dot(d_attended_sq, outw, ((1,), (1,))).astype(LOW)
    dq_part, dk_far, dv_far, dck, dcv, d_head, delta = back_away(
        queries, d_mixed, out_self, out_cross, lse, stats, gate_row, keys_far, values_far, cap_keys, cap_values,
        seg_col, seg_far,
    )
    dk_other, dv_other = far_back(dk_far), far_back(dv_far)
    d_query, dk_near, dv_near = back_near(
        queries, d_mixed, lse, delta, keys, values, seg_col, seg_row, dq_part
    )
    d_cap = outer_sum(jnp.concatenate([dck, dcv], 1))
    d_key, d_value = dk_near + dk_other, dv_near + dv_other

    out_part = weight_grad(mixed_both, d_attended_sq)
    grad_out = finish(outer_reduce(out_part.reshape(outer, -1, D // 4)), 1)

    turned_q, turned_k = rotate(d_query, -1.0), rotate(d_key, -1.0)
    inner_q, inner_k = turned_q * gain_q, turned_k * gain_k
    inner_c = d_cap[:, :width] * gain_c
    sums, sums_c = square_sum(
        jnp.stack([jnp.sum(inner_q * unit_q, -1), jnp.sum(inner_k * unit_k, -1)]), jnp.sum(inner_c * unit_c, -1)
    )
    mean = (sums / D)[:, :, None]
    d_q_raw = inv_q * (inner_q - unit_q * mean[0])
    d_k_raw = inv_k * (inner_k - unit_k * mean[1])
    d_c_raw = inv_c * (inner_c - unit_c * (sums_c / D)[:, None])
    d_projected = jnp.concatenate([d_q_raw, d_k_raw, d_value], 1).astype(LOW)
    d_first = scatter_square(dot(d_projected, qkv_mine, ((1,), (1,))))

    rows_qkv = qkv_weight.shape[0]
    quarter = rows_qkv // 4
    qkv_part = low(dot(first_in, d_projected, ((0,), (0,))))
    qkv_part = row_blocks(qkv_part).reshape(outer, 4, 2, 2, quarter, -1)
    qkv_part = pair_reduce(qkv_part, "core", 2)[:, :, 0]
    qkv_part = pair_reduce(qkv_part, "x", 2)[:, :, 0]
    qkv_part = square_exchange(low(outer_reduce(qkv_part)))
    qkv_part = qkv_part.reshape(4, quarter, 3, outer, -1).transpose(1, 2, 3, 0, 4)
    qkv_part = unblocks(qkv_part).reshape(quarter, -1)
    grad_qkv = finish(qkv_part.astype(F32), 0)

    d_cap_mine = jnp.concatenate([d_c_raw, d_cap[:, width:]], 1).astype(LOW)

    def gather_place(value):
        full = gather_square(value)
        count = value.shape[0]
        result = jnp.zeros((4,) + value.shape, value.dtype)
        for r in range(4):
            result = lax.dynamic_update_slice_in_dim(result, full[None, r * count : (r + 1) * count], me_c ^ r, 0)
        return result

    d_cap_all = gather_place(d_cap_mine).reshape(4, CLIPS * CAP, 2, outer, -1)
    d_cap_low = unblocks(jnp.moveaxis(d_cap_all, 0, -2)).reshape(CLIPS * CAP, 2 * D)
    grad_caption = finish(weight_grad(two_cores(chosen_rows), d_cap_low), 1)
    d_chosen = dot(d_cap_low, caption_weight, ((1,), (1,))).reshape(CLIPS, CAP, -1)
    grad_null = jnp.sum(jnp.where(dropped[:, None, None] == 1, d_chosen, 0.0), 0)
    grad_null = rounded(grad_null) + swap(low(grad_null), "core").astype(F32)
    grad_null = rounded(grad_null) + swap(low(grad_null), "x").astype(F32)

    scale_attn = per_token(modulation[:, :D], clip_here)
    unit_in = unit_rows(source)
    d_scale_attn = d_first * unit_in * gains[0]
    d_source_norm, grad_gain0 = norm_back(d_first * (1.0 + scale_attn), source, gains[0])
    input_grad = d_middle + d_source_norm

    onehot = (segments[:, None] == jnp.arange(CLIPS)[None, :]).astype(F32)

    def per_clip(grad):
        return lax.dot_general(onehot, grad, (((0,), (0,)), ((), ())), precision=PRECISE)

    early = jnp.concatenate(
        [per_clip(d_gate_attn), per_clip(d_scale_ffn), per_clip(d_gate_ffn), grad_gain1[None], grad_gain2[None], grad_gain3[None]]
    )
    grad_gain6 = jnp.where(me_o == 0, jnp.sum(d_cap[:, :width] * unit_c, 0), 0.0)
    late = jnp.concatenate(
        [
            per_clip(d_scale_attn),
            grad_gain0[None],
            put_cols(jnp.sum(turned_q * unit_q, 0))[None],
            put_cols(jnp.sum(turned_k * unit_k, 0))[None],
            put_cols(grad_gain6)[None],
            put_cols(d_head[0])[None],
        ]
    )
    early = all_dp(low(group_sum(early))).astype(F32)
    late = all_dp(low(group_sum(late))).astype(F32)
    d_mod = jnp.concatenate([late[:, :, 0:2], early[:, :, 0:2], early[:, :, 2:4], early[:, :, 4:6]], -1)
    d_mod = d_mod.reshape(4 * CLIPS, 4 * D)
    grad_ada = dot(cond_all, d_mod.astype(LOW), ((0,), (0,)))
    grad_ada_b = jnp.sum(d_mod, 0)
    early_sum, late_sum = jnp.sum(early[:, :, 6:], (0, 1)), jnp.sum(late[:, :, 2:], (0, 1))
    grad_gains = jnp.concatenate([late_sum[0:1], early_sum, late_sum[1:4]])
    grad_head = jnp.sum(late_sum[4].reshape(HEADS, HEAD), -1) * (1.0 - head_tanh * head_tanh)
    return (
        result,
        input_grad,
        grad_ada,
        grad_ada_b,
        grad_qkv,
        grad_out,
        grad_caption,
        grad_gate_up,
        grad_down,
        grad_null,
        grad_gains,
        grad_head,
    )


def solution(mesh):
    devices = mesh.devices
    outer = devices.shape[1] // 4
    lead = (D // devices.shape[1]) % HEAD != 0
    if lead:
        grid = Mesh(devices.reshape(2, 2, 2, 2, outer), ("x", "core", "p", "y", "o"))
        blk = ("p", "y", "o")
    else:
        grid = Mesh(devices.reshape(2, 2, outer, 2, 2), ("x", "core", "o", "p", "y"))
        blk = ("o", "p", "y")
    dp = ("x", "core")
    every = dp + blk
    in_specs = (
        P(every, None),
        P(every),
        P(None, every),
        P(dp, None),
        P(dp, None, blk),
        P(dp),
        P(None, blk),
        P(blk, None),
        P(),
        P(blk, None),
        P(blk, None),
        P(blk, None),
        P(blk, None),
        P(blk, None),
        P(),
        P(),
        P(every, None),
    )
    out_specs = (
        P(every, None),
        P(every, None),
        P(blk, None),
        P(),
        P(blk, None),
        P(blk, None),
        P(blk, None),
        P(blk, None),
        P(blk, None),
        P(None, blk),
        P(),
        P(),
    )
    return jax.shard_map(
        functools.partial(on_device, outer, lead),
        mesh=grid,
        in_specs=in_specs,
        out_specs=out_specs,
        check_vma=False,
    )
```

time: 2710 us -> 920 us (0.34)
  waiting for transfers between devices: 2200 us -> 324 us
  starting transfers between devices: 1.37 us -> 216 us
  matrix products: 195 us -> 66.9 us
  blocking collectives: 89.6 us -> 0 us
  local copies, waits for them, and re-layouts: 113 us -> 151 us
  Pallas kernels: 0 us -> 36.4 us
    reduce_scatter x5 -> x0, waiting for transfers between devices: 949 us -> none  [the longest x4 890 us: weight_grad(): lax.psum_scatter(lax.dot_general(left_rows, grad_rows, (((0,), (0,)), (()...]
    all_gather x6 -> x0, waiting for transfers between devices: 913 us -> none  [the longest x4 816 us: forward_product(): lax.all_gather(local_rows, 'blk', axis=0, tiled=True)]
    ppermute x0 -> x124, waiting for transfers between devices: none -> 324 us  [the longest x107 293 us: swap(): return lax.ppermute(value, axis, SWAP)]
    psum x3 -> x0, waiting for transfers between devices: 320 us -> none  [the longest x1 203 us: on_device(): lax.psum(grad_ada_w.astype(jnp.bfloat16), 'dp').astype(jnp.float32)]
    ppermute x0 -> x124, starting transfers between devices: none -> 216 us  [the longest x107 198 us: swap(): return lax.ppermute(value, axis, SWAP)]
    dot_general x39 -> x26, matrix products: 191 us -> 66.9 us  [the longest x17 50 us: dot(): return lax.dot_general(a, b, (dims, ((), ())), preferred_element_type=F32)]
    psum x3 -> x0, blocking collectives: 75 us -> none  [the longest x1 33.4 us: on_device(): lax.psum(mod_part.astype(jnp.bfloat16), 'blk').astype(jnp.float32)]
    dynamic_update_slice x0 -> x20, local copies, waits for them, and re-layouts: none -> 37.8 us  [the longest x16 37.7 us: square_exchange(): result = lax.dynamic_update_slice_in_dim(result, piece, me_c ^ r, 0)]
  transfers between devices with their start and end apart: 15 -> 124, of which waited for: 15 -> 56; matrix products, arithmetic and copies ran while one was open for 10% -> 32% of each run, Pallas kernels for 0% -> 4%
where the time goes in v1:
time: 920 us; the launch traced here: 909 us
  waiting for transfers between devices  324 us (35%)
  starting transfers between devices  216 us (23%)
  local copies, waits for them, and re-layouts  151 us (16%)
  other arithmetic  111 us (12%)
  matrix products  66.9 us (7%)
  Pallas kernels  36.4 us (4%)
    ppermute x107, waiting for transfers between devices, swap(): return lax.ppermute(value, axis, SWAP)  293 us
    ppermute x107, starting transfers between devices, swap(): return lax.ppermute(value, axis, SWAP)  198 us
    dot_general x17, matrix products, dot(): return lax.dot_general(a, b, (dims, ((), ())), preferred_element_type=F32)  50 us
    dynamic_update_slice x16, local copies, waits for them, and re-layouts, square_exchange(): result = lax.dynamic_update_slice_in_dim(result, piece, me_c ^ r, 0)  37.7 us
    unnamed x383, local copies, waits for them, and re-layouts  25.5 us
    select_n x27, other arithmetic, pair_stack(): jnp.where(first, value, other)  23.4 us
  transfers between devices with their start and end apart: 124, of which 56 were waited for; matrix products, arithmetic and copies ran while one was open for 32% of the time, Pallas kernels for 4%

profile of v1, /device:TPU:1, one launch (start us, length us, event | category | flops | bytes accessed | tf_op | source)
XLA Modules:
  0.0 909.5 jit_solution(17594666912559335519)
XLA Ops:
  0.7 6.3 reshape_reshape.27
  7.0 4.6 constant_dynamic-slice_fusion.11
  44.0 4.3 copy.133
  48.3 5.5 reshape.528
  95.6 4.2 collective-permute-done.27
  109.4 16.2 %collective-permute-start.98 = (bf16[256,512]{1,0:T(8,128)(2,1)}, bf16[256,512]{1,0:T(8,128)(2,1)}, u32[]{:S(2)}, u32[]{:S(2)}) collective-permute-start(bf16[256,512]{1,0:T(8,128)(2,1)} %bitcast.15), channel_id=1, source_target_pairs={{0,8},{8,0},{1,9},{9,1},{2,10},{10,2},{3,11},{11,3},{4,12},{12,4},... | collective-permute-start | bytes 786440 | tf_op jit(solution)/shard_map/ppermute | solution.py:258
  138.3 16.7 %collective-permute-done.14 = bf16[1,4,48,1152]{3,2,1,0:T(8,128)(2,1)S(1)} collective-permute-done((bf16[1,4,48,1152]{3,2,1,0:T(8,128)(2,1)}, bf16[1,4,48,1152]{3,2,1,0:T(8,128)(2,1)S(1)}, u32[]{:S(2)}, u32[]{:S(2)}) %collective-permute-start.14) | collective-permute-done | bytes 442400 | tf_op jit(solution)/shard_map/ppermute | solution.py:258
  155.0 10.6 %collective-permute-start.6 = (bf16[128,1536]{1,0:T(8,128)(2,1)S(1)}, bf16[128,1536]{1,0:T(8,128)(2,1)S(1)}, u32[]{:S(2)}, u32[]{:S(2)}) collective-permute-start(bf16[128,1536]{1,0:T(8,128)(2,1)S(1)} %pad_maximum_fusion.34), channel_id=1, source_target_pairs={{0,2},{2,0},{1,3},{3,1},{4,6},{6,4},{5,7},{7,5},{8,10},{10,8},{9,1... | collective-permute-start | bytes 1179656 | tf_op jit(solution)/shard_map/ppermute | solution.py:258
  167.1 5.5 collective-permute-done.6
  174.0 10.8 %collective-permute-done.15 = bf16[1,2,4,48,1152]{4,3,0,2,1:T(8,128)(2,1)S(1)} collective-permute-done((bf16[1,2,4,48,1152]{4,3,0,2,1:T(8,128)(2,1)S(1)}, bf16[1,2,4,48,1152]{4,3,0,2,1:T(8,128)(2,1)S(1)}, u32[]{:S(2)}, u32[]{:S(2)}) %collective-permute-start.15) | collective-permute-done | bytes 884768 | tf_op jit(solution)/shard_map/ppermute | solution.py:258
  185.2 10.7 %collective-permute-start.16 = (bf16[2,2,4,48,1152]{4,3,0,2,1:T(8,128)(2,1)S(1)}, bf16[2,2,4,48,1152]{4,3,0,2,1:T(8,128)(2,1)S(1)}, u32[]{:S(2)}, u32[]{:S(2)}) collective-permute-start(bf16[2,2,4,48,1152]{4,3,0,2,1:T(8,128)(2,1)S(1)} %pad_maximum_fusion.10), channel_id=1, source_target_pairs={{0,8},{8,0},{1,9},{9,1},{2,10},{10,2},{3,11},{11,3},{4,12},{12,4},... | collective-permute-start | bytes 5308424 | tf_op jit(solution)/shard_map/ppermute | solution.py:258
  198.2 5.3 collective-permute-done.20
  204.1 23.4 %collective-permute-start.21 = (bf16[256,768]{1,0:T(8,128)(2,1)S(1)}, bf16[256,768]{1,0:T(8,128)(2,1)S(1)}, u32[]{:S(2)}, u32[]{:S(2)}) collective-permute-start(bf16[256,768]{1,0:T(8,128)(2,1)S(1)} %fusion.97), channel_id=1, source_target_pairs={{0,4},{4,0},{1,5},{5,1},{2,6},{6,2},{3,7},{7,3},{8,12},{12,8},{9,1... | collective-permute-start | bytes 1179656 | tf_op jit(solution)/shard_map/ppermute | solution.py:258
  232.4 13.0 %collective-permute-done.21 = bf16[256,768]{1,0:T(8,128)(2,1)S(1)} collective-permute-done((bf16[256,768]{1,0:T(8,128)(2,1)S(1)}, bf16[256,768]{1,0:T(8,128)(2,1)S(1)}, u32[]{:S(2)}, u32[]{:S(2)}) %collective-permute-start.21) | collective-permute-done | bytes 393248 | tf_op jit(solution)/shard_map/ppermute | solution.py:258
  247.9 4.0 fusion.219
  265.2 3.7 fusion.38.k_ref
  269.1 3.3 fusion.45.q_ref
  272.4 6.2 attn_near.1
  280.7 10.6 %collective-permute-done.25 = bf16[512,384]{1,0:T(8,128)(2,1)S(1)} collective-permute-done((bf16[512,384]{1,0:T(8,128)(2,1)S(1)}, bf16[512,384]{1,0:T(8,128)(2,1)S(1)}, u32[]{:S(2)}, u32[]{:S(2)}) %collective-permute-start.25) | collective-permute-done | bytes 393248 | tf_op jit(solution)/shard_map/ppermute | solution.py:358
  292.1 7.7 collective-permute-done.24
  300.9 10.6 %attn_far.1 = (f32[512,384]{1,0:T(8,128)S(1)}, bf16[512,384]{1,0:T(8,128)(2,1)S(1)}, f32[3,512,2]{2,1,0:T(8,128)S(1)}) custom-call(bf16[512,384]{1,0:T(8,128)(2,1)S(1)} %fusion.45.q_ref, bf16[1,512,384]{2,1,0:T(8,128)(2,1)S(1)} %bitcast.210, bf16[1,512,384]{2,1,0:T(8,128)(2,1)S(1)} %bitcast.208, s32[512,1]{1,0:T(8,128)S(1)} %copy.140.sq_ref, ...), custom_call_target="tpu_custom_call" | custom-call | flops 402653184 | bytes 6291456 | tf_op jit(solution)/shard_map/attn_far/pallas_call | solution.py:537
  316.2 6.8 collective-permute-done.30
  337.4 3.4 collective-permute-done.35
  342.5 5.1 collective-permute-done.36
  352.0 3.4 fusion.2
  357.7 4.7 fusion.242
  374.7 7.1 collective-permute-start.73
  392.9 4.2 collective-permute-start.107
  403.5 6.2 collective-permute-done.53
  410.7 5.5 collective-permute-done.54
  419.3 3.5 fusion.243
  424.7 4.9 collective-permute-done.55
  431.6 5.1 collective-permute-done.57
  440.9 10.4 %collective-permute-start.117 = (bf16[512,768]{1,0:T(8,128)(2,1)}, bf16[512,768]{1,0:T(8,128)(2,1)}, u32[]{:S(2)}, u32[]{:S(2)}) collective-permute-start(bf16[512,768]{1,0:T(8,128)(2,1)} %get-tuple-element.127), channel_id=1, source_target_pairs={{0,8},{8,0},{1,9},{9,1},{2,10},{10,2},{3,11},{11,3},{4,12},{12,4},... | collective-permute-start | bytes 2359304 | tf_op jit(solution)/shard_map/ppermute | solution.py:258
  473.6 3.6 fusion.18
  486.6 4.1 convolution_convert_fusion
  492.2 3.8 collective-permute-done.61
  498.2 12.6 %attn_back_far.1 = (f32[512,384]{1,0:T(8,128)S(1)}, bf16[1,512,384]{2,1,0:T(8,128)(2,1)}, bf16[1,512,384]{2,1,0:T(8,128)(2,1)S(1)}, f32[256,384]{1,0:T(8,128)S(1...) custom-call(bf16[512,384]{1,0:T(8,128)(2,1)S(1)} %fusion.45.q_ref, ...), custom_call_target="tpu_custom_call" | custom-call | flops 1509949440 | bytes 6291456 | tf_op jit(solution)/shard_map/attn_back_far/pallas_call | solution.py:599
  519.8 7.1 attn_back_near.1
  534.6 24.4 %collective-permute-done.64 = bf16[256,768]{1,0:T(8,128)(2,1)} collective-permute-done((bf16[256,768]{1,0:T(8,128)(2,1)}, bf16[256,768]{1,0:T(8,128)(2,1)}, u32[]{:S(2)}, u32[]{:S(2)}) %collective-permute-start.64) | collective-permute-done | bytes 393248 | tf_op jit(solution)/shard_map/ppermute | solution.py:258
  561.6 4.5 multiply_reduce_fusion.3
  568.1 7.7 collective-permute-done.67
  585.4 3.9 fusion.244
  589.3 4.2 fusion
  609.1 4.0 collective-permute-start.84
  616.2 30.0 %collective-permute-done.120 = bf16[512,384]{1,0:T(8,128)(2,1)S(1)} collective-permute-done((bf16[512,384]{1,0:T(8,128)(2,1)S(1)}, bf16[512,384]{1,0:T(8,128)(2,1)S(1)}, u32[]{:S(2)}, u32[]{:S(2)}) %collective-permute-start.120) | collective-permute-done | bytes 393248 | tf_op jit(solution)/shard_map/ppermute | solution.py:258
  647.9 5.0 collective-permute-done.102
  658.6 6.0 collective-permute-start.121
  687.2 4.4 collective-permute-done.95
  692.4 3.6 collective-permute-done.76
  699.8 6.6 collective-permute-start.78
  717.5 4.2 reshape.527
  738.0 29.8 %collective-permute-done.110 = bf16[1,4,192,512]{3,2,1,0:T(8,128)(2,1)S(1)} collective-permute-done((bf16[1,4,192,512]{3,2,1,0:T(8,128)(2,1)S(1)}, bf16[1,4,192,512]{3,2,1,0:T(8,128)(2,1)S(1)}, u32[]{:S(2)}, u32[]{:S(2)}) %collective-permute-start.110) | collective-permute-done | bytes 786464 | tf_op jit(solution)/shard_map/ppermute | solution.py:258
  770.8 3.6 dynamic_update_slice.88
  790.0 8.0 dynamic_update_slice.89
  798.0 8.0 dynamic_update_slice.90
  806.0 8.0 dynamic_update_slice.91
  821.6 11.4 %collective-permute-done.114 = bf16[192,2048]{1,0:T(8,128)(2,1)S(1)} collective-permute-done((bf16[192,2048]{1,0:T(8,128)(2,1)S(1)}, bf16[192,2048]{1,0:T(8,128)(2,1)S(1)}, u32[]{:S(2)}, u32[]{:S(2)}) %collective-permute-start.114) | collective-permute-done | bytes 786464 | tf_op jit(solution)/shard_map/ppermute | solution.py:258
  833.1 18.8 %collective-permute-done.85 = bf16[2,4,1,48,1152]{4,3,1,0,2:T(8,128)(2,1)S(1)} collective-permute-done((bf16[2,4,1,48,1152]{4,3,1,0,2:T(8,128)(2,1)S(1)}, bf16[2,4,1,48,1152]{4,3,1,0,2:T(8,128)(2,1)S(1)}, u32[]{:S(2)}, u32[]{:S(2)}) %collective-permute-start.85) | collective-permute-done | bytes 884768 | tf_op jit(solution)/shard_map/ppermute | solution.py:258
  853.2 4.5 collective-permute-start.115
  857.6 17.0 %collective-permute-done.86 = bf16[1,4,48,1152]{3,2,1,0:T(8,128)(2,1)S(1)} collective-permute-done((bf16[1,4,48,1152]{3,2,1,0:T(8,128)(2,1)S(1)}, bf16[1,4,48,1152]{3,2,1,0:T(8,128)(2,1)S(1)}, u32[]{:S(2)}, u32[]{:S(2)}) %collective-permute-start.86) | collective-permute-done | bytes 442400 | tf_op jit(solution)/shard_map/ppermute | solution.py:258
  887.7 6.0 collective-permute-done.90
  899.0 3.4 maximum_convert_fusion.1
  905.5 3.5 maximum_convert_fusion
  (933 shorter events, 390.3 us)
Async XLA Ops:
  12.3 93.5 %collective-permute-start.38 = (bf16[1,192,512]{2,1,0:T(8,128)(2,1)}, bf16[1,192,512]{2,1,0:T(8,128)(2,1)}, u32[]{:S(2)}, u32[]{:S(2)}) collective-permute-start(bf16[1,192,512]{2,1,0:T(8,128)(2,1)} %bitcast.207), channel_id=1, source_target_pairs={{0,1},{1,0},{2,3},{3,2},{4,5},{5,4},{6,7},{7,6},{8,9},{9,8},{10,11... | collective-permute-start | bytes 589832 | tf_op jit(solution)/shard_map/ppermute | solution.py:390
  15.1 94.3 %collective-permute-start.39 = (bf16[1,192,512]{2,1,0:T(8,128)(2,1)}, bf16[1,192,512]{2,1,0:T(8,128)(2,1)}, u32[]{:S(2)}, u32[]{:S(2)}) collective-permute-start(bf16[1,192,512]{2,1,0:T(8,128)(2,1)} %bitcast.206), channel_id=1, source_target_pairs={{0,2},{2,0},{1,3},{3,1},{4,6},{6,4},{5,7},{7,5},{8,10},{10,8},{9,1... | collective-permute-start | bytes 589832 | tf_op jit(solution)/shard_map/ppermute | solution.py:390
  17.1 110.1 %collective-permute-start.40 = (bf16[1,192,512]{2,1,0:T(8,128)(2,1)}, bf16[1,192,512]{2,1,0:T(8,128)(2,1)}, u32[]{:S(2)}, u32[]{:S(2)}) collective-permute-start(bf16[1,192,512]{2,1,0:T(8,128)(2,1)} %bitcast.205), channel_id=1, source_target_pairs={{0,3},{1,2},{2,1},{3,0},{4,7},{5,6},{6,5},{7,4},{8,11},{9,10},{10,... | collective-permute-start | bytes 589832 | tf_op jit(solution)/shard_map/ppermute | solution.py:390
  23.2 65.1 %collective-permute-start.11 = (bf16[1,48,1152]{2,1,0:T(8,128)(2,1)}, bf16[1,48,1152]{2,1,0:T(8,128)(2,1)}, u32[]{:S(2)}, u32[]{:S(2)}) collective-permute-start(bf16[1,48,1152]{2,1,0:T(8,128)(2,1)} %get-tuple-element.180), channel_id=1, source_target_pairs={{0,1},{1,0},{2,3},{3,2},{4,5},{5,4},{6,7},{7,6},{8,9},{9,8},{10,11... | collective-permute-start | bytes 331784 | tf_op jit(solution)/shard_map/ppermute | solution.py:390
  25.8 45.2 %collective-permute-start.8 = (s32[64,4]{0,1:T(4,128)}, s32[64,4]{0,1:T(4,128)}, u32[]{:S(2)}, u32[]{:S(2)}) collective-permute-start(s32[64,4]{0,1:T(4,128)} %get-tuple-element.269), channel_id=1, source_target_pairs={{0,2},{2,0},{1,3},{3,1},{4,6},{6,4},{5,7},{7,5},{8,10},{10,8},{9,1... | collective-permute-start | bytes 3080 | tf_op jit(solution)/shard_map/ppermute | solution.py:258
  91.8 10.2 %collective-permute-start.4 = (bf16[64,1536]{1,0:T(8,128)(2,1)S(1)}, bf16[64,1536]{1,0:T(8,128)(2,1)S(1)}, u32[]{:S(2)}, u32[]{:S(2)}) collective-permute-start(bf16[64,1536]{1,0:T(8,128)(2,1)S(1)} %copy-done.105), channel_id=1, source_target_pairs={{0,2},{2,0},{1,3},{3,1},{4,6},{6,4},{5,7},{7,5},{8,10},{10,8},{9,1... | collective-permute-start | bytes 589832 | tf_op jit(solution)/shard_map/ppermute | solution.py:258
  102.0 30.5 %collective-permute-start.17 = (bf16[256,768]{1,0:T(8,128)(2,1)S(1)}, bf16[256,768]{1,0:T(8,128)(2,1)S(1)}, u32[]{:S(2)}, u32[]{:S(2)}) collective-permute-start(bf16[256,768]{1,0:T(8,128)(2,1)S(1)} %copy-done.111), channel_id=1, source_target_pairs={{0,2},{2,0},{1,3},{3,1},{4,6},{6,4},{5,7},{7,5},{8,10},{10,8},{9,1... | collective-permute-start | bytes 1179656 | tf_op jit(solution)/shard_map/ppermute | solution.py:258
  105.1 29.6 %collective-permute-start.19 = (bf16[256,768]{1,0:T(8,128)(2,1)S(1)}, bf16[256,768]{1,0:T(8,128)(2,1)S(1)}, u32[]{:S(2)}, u32[]{:S(2)}) collective-permute-start(bf16[256,768]{1,0:T(8,128)(2,1)S(1)} %copy-done.110), channel_id=1, source_target_pairs={{0,1},{1,0},{2,3},{3,2},{4,5},{5,4},{6,7},{7,6},{8,9},{9,8},{10,11... | collective-permute-start | bytes 1179656 | tf_op jit(solution)/shard_map/ppermute | solution.py:258
  105.9 23.2 %collective-permute-start.44 = (bf16[1,512,384]{2,1,0:T(8,128)(2,1)S(1)}, bf16[1,512,384]{2,1,0:T(8,128)(2,1)S(1)}, u32[]{:S(2)}, u32[]{:S(2)}) collective-permute-start(bf16[1,512,384]{2,1,0:T(8,128)(2,1)S(1)} %copy-done.112), channel_id=1, source_target_pairs={{0,4},{4,0},{1,5},{5,1},{2,6},{6,2},{3,7},{7,3},{8,12},{12,8},{9,1... | collective-permute-start | bytes 1179656 | tf_op jit(solution)/shard_map/ppermute | solution.py:258
  109.4 669.6 %collective-permute-start.98 = (bf16[256,512]{1,0:T(8,128)(2,1)}, bf16[256,512]{1,0:T(8,128)(2,1)}, u32[]{:S(2)}, u32[]{:S(2)}) collective-permute-start(bf16[256,512]{1,0:T(8,128)(2,1)} %bitcast.15), channel_id=1, source_target_pairs={{0,8},{8,0},{1,9},{9,1},{2,10},{10,2},{3,11},{11,3},{4,12},{12,4},... | collective-permute-start | bytes 786440 | tf_op jit(solution)/shard_map/ppermute | solution.py:258
  127.2 151.4 %collective-permute-start.26 = (s32[1,512]{1,0:T(1,128)S(1)}, s32[1,512]{1,0:T(1,128)S(1)}, u32[]{:S(2)}, u32[]{:S(2)}) collective-permute-start(s32[1,512]{1,0:T(1,128)S(1)} %get-tuple-element.244.sk_ref), channel_id=1, source_target_pairs={{0,4},{4,0},{1,5},{5,1},{2,6},{6,2},{3,7},{7,3},{8,12},{12,8},{9,1... | collective-permute-start | bytes 6152 | tf_op jit(solution)/shard_map/ppermute | solution.py:358
  129.0 26.0 %collective-permute-start.14 = (bf16[1,4,48,1152]{3,2,1,0:T(8,128)(2,1)}, bf16[1,4,48,1152]{3,2,1,0:T(8,128)(2,1)S(1)}, u32[]{:S(2)}, u32[]{:S(2)}) collective-permute-start(bf16[1,4,48,1152]{3,2,1,0:T(8,128)(2,1)} %bitcast_dynamic-update-slice_fusion.5), channel_id=1, source_target_pairs={{0,4},{4,0},{1,5},{5,1},{2,6},{6,2},{3,7},{7,3},{8,12},{12,8},{9,1... | collective-permute-start | bytes 1327112 | tf_op jit(solution)/shard_map/ppermute | solution.py:258
  134.8 69.3 %collective-permute-start.41 = (bf16[1,4,192,512]{3,2,1,0:T(8,128)(2,1)}, bf16[1,4,192,512]{3,2,1,0:T(8,128)(2,1)S(1)}, u32[]{:S(2)}, u32[]{:S(2)}) collective-permute-start(bf16[1,4,192,512]{3,2,1,0:T(8,128)(2,1)} %bitcast_dynamic-update-slice_fusion.1), channel_id=1, source_target_pairs={{0,4},{4,0},{1,5},{5,1},{2,6},{6,2},{3,7},{7,3},{8,12},{12,8},{9,1... | collective-permute-start | bytes 2359304 | tf_op jit(solution)/shard_map/ppermute | solution.py:258
  138.1 28.7 %collective-permute-start.5 = (bf16[128,1536]{1,0:T(8,128)(2,1)S(1)}, bf16[128,1536]{1,0:T(8,128)(2,1)S(1)}, u32[]{:S(2)}, u32[]{:S(2)}) collective-permute-start(bf16[128,1536]{1,0:T(8,128)(2,1)S(1)} %pad_maximum_fusion.33), channel_id=1, source_target_pairs={{0,1},{1,0},{2,3},{3,2},{4,5},{5,4},{6,7},{7,6},{8,9},{9,8},{10,11... | collective-permute-start | bytes 1179656 | tf_op jit(solution)/shard_map/ppermute | solution.py:258
  155.0 17.6 %collective-permute-start.6 = (bf16[128,1536]{1,0:T(8,128)(2,1)S(1)}, bf16[128,1536]{1,0:T(8,128)(2,1)S(1)}, u32[]{:S(2)}, u32[]{:S(2)}) collective-permute-start(bf16[128,1536]{1,0:T(8,128)(2,1)S(1)} %pad_maximum_fusion.34), channel_id=1, source_target_pairs={{0,2},{2,0},{1,3},{3,1},{4,6},{6,4},{5,7},{7,5},{8,10},{10,8},{9,1... | collective-permute-start | bytes 1179656 | tf_op jit(solution)/shard_map/ppermute | solution.py:258
  172.6 12.2 %collective-permute-start.15 = (bf16[1,2,4,48,1152]{4,3,0,2,1:T(8,128)(2,1)S(1)}, bf16[1,2,4,48,1152]{4,3,0,2,1:T(8,128)(2,1)S(1)}, u32[]{:S(2)}, u32[]{:S(2)}) collective-permute-start(bf16[1,2,4,48,1152]{4,3,0,2,1:T(8,128)(2,1)S(1)} %maximum_bitcast_fusion), channel_id=1, source_target_pairs={{0,16},{16,0},{1,17},{17,1},{2,18},{18,2},{3,19},{19,3},{4,20},{20... | collective-permute-start | bytes 2654216 | tf_op jit(solution)/shard_map/ppermute | solution.py:258
  185.2 61.6 %collective-permute-start.16 = (bf16[2,2,4,48,1152]{4,3,0,2,1:T(8,128)(2,1)S(1)}, bf16[2,2,4,48,1152]{4,3,0,2,1:T(8,128)(2,1)S(1)}, u32[]{:S(2)}, u32[]{:S(2)}) collective-permute-start(bf16[2,2,4,48,1152]{4,3,0,2,1:T(8,128)(2,1)S(1)} %pad_maximum_fusion.10), channel_id=1, source_target_pairs={{0,8},{8,0},{1,9},{9,1},{2,10},{10,2},{3,11},{11,3},{4,12},{12,4},... | collective-permute-start | bytes 5308424 | tf_op jit(solution)/shard_map/ppermute | solution.py:258
  203.4 26.6 %collective-permute-start.29 = (bf16[384,768]{1,0:T(8,128)(2,1)S(1)}, bf16[384,768]{1,0:T(8,128)(2,1)S(1)}, u32[]{:S(2)}, u32[]{:S(2)}) collective-permute-start(bf16[384,768]{1,0:T(8,128)(2,1)S(1)} %pad_maximum_fusion.28), channel_id=1, source_target_pairs={{0,8},{8,0},{1,9},{9,1},{2,10},{10,2},{3,11},{11,3},{4,12},{12,4},... | collective-permute-start | bytes 1769480 | tf_op jit(solution)/shard_map/ppermute | solution.py:258
  204.1 41.3 %collective-permute-start.21 = (bf16[256,768]{1,0:T(8,128)(2,1)S(1)}, bf16[256,768]{1,0:T(8,128)(2,1)S(1)}, u32[]{:S(2)}, u32[]{:S(2)}) collective-permute-start(bf16[256,768]{1,0:T(8,128)(2,1)S(1)} %fusion.97), channel_id=1, source_target_pairs={{0,4},{4,0},{1,5},{5,1},{2,6},{6,2},{3,7},{7,3},{8,12},{12,8},{9,1... | collective-permute-start | bytes 1179656 | tf_op jit(solution)/shard_map/ppermute | solution.py:258
  230.0 23.9 %collective-permute-start.45 = (bf16[1024,384]{1,0:T(8,128)(2,1)}, bf16[1024,384]{1,0:T(8,128)(2,1)}, u32[]{:S(2)}, u32[]{:S(2)}) collective-permute-start(bf16[1024,384]{1,0:T(8,128)(2,1)} %bitcast.37), channel_id=1, source_target_pairs={{0,16},{16,0},{1,17},{17,1},{2,18},{18,2},{3,19},{19,3},{4,20},{20... | collective-permute-start | bytes 2359304 | tf_op jit(solution)/shard_map/ppermute | solution.py:258
  245.4 67.4 %collective-permute-start.42 = (bf16[1536,512]{1,0:T(8,128)(2,1)}, bf16[1536,512]{1,0:T(8,128)(2,1)}, u32[]{:S(2)}, u32[]{:S(2)}) collective-permute-start(bf16[1536,512]{1,0:T(8,128)(2,1)} %bitcast.35), channel_id=1, source_target_pairs={{0,16},{16,0},{1,17},{17,1},{2,18},{18,2},{3,19},{19,3},{4,20},{20... | collective-permute-start | bytes 4718600 | tf_op jit(solution)/shard_map/ppermute | solution.py:258
  261.9 29.5 %collective-permute-start.25 = (bf16[512,384]{1,0:T(8,128)(2,1)S(1)}, bf16[512,384]{1,0:T(8,128)(2,1)S(1)}, u32[]{:S(2)}, u32[]{:S(2)}) collective-permute-start(bf16[512,384]{1,0:T(8,128)(2,1)S(1)} %slice.1081.v_ref), channel_id=1, source_target_pairs={{0,4},{4,0},{1,5},{5,1},{2,6},{6,2},{3,7},{7,3},{8,12},{12,8},{9,1... | collective-permute-start | bytes 1179656 | tf_op jit(solution)/shard_map/ppermute | solution.py:358
  268.9 30.9 %collective-permute-start.24 = (bf16[512,384]{1,0:T(8,128)(2,1)S(1)}, bf16[512,384]{1,0:T(8,128)(2,1)S(1)}, u32[]{:S(2)}, u32[]{:S(2)}) collective-permute-start(bf16[512,384]{1,0:T(8,128)(2,1)S(1)} %fusion.38.k_ref), channel_id=1, source_target_pairs={{0,4},{4,0},{1,5},{5,1},{2,6},{6,2},{3,7},{7,3},{8,12},{12,8},{9,1... | collective-permute-start | bytes 1179656 | tf_op jit(solution)/shard_map/ppermute | solution.py:358
  278.7 52.1 %collective-permute-start.46 = (bf16[1024,768]{1,0:T(8,128)(2,1)}, bf16[1024,768]{1,0:T(8,128)(2,1)}, u32[]{:S(2)}, u32[]{:S(2)}) collective-permute-start(bf16[1024,768]{1,0:T(8,128)(2,1)} %pad_maximum_fusion.12), channel_id=1, source_target_pairs={{0,8},{8,0},{1,9},{9,1},{2,10},{10,2},{3,11},{11,3},{4,12},{12,4},... | collective-permute-start | bytes 4718600 | tf_op jit(solution)/shard_map/ppermute | solution.py:258
  312.7 10.3 %collective-permute-start.30 = (bf16[128,1536]{1,0:T(8,128)(2,1)S(1)}, bf16[128,1536]{1,0:T(8,128)(2,1)S(1)}, u32[]{:S(2)}, u32[]{:S(2)}) collective-permute-start(bf16[128,1536]{1,0:T(8,128)(2,1)S(1)} %pad_maximum_fusion.37), channel_id=1, source_target_pairs={{0,2},{2,0},{1,3},{3,1},{4,6},{6,4},{5,7},{7,5},{8,10},{10,8},{9,1... | collective-permute-start | bytes 1179656 | tf_op jit(solution)/shard_map/ppermute | solution.py:258
  315.0 11.5 %collective-permute-start.32 = (bf16[128,1536]{1,0:T(8,128)(2,1)S(1)}, bf16[128,1536]{1,0:T(8,128)(2,1)S(1)}, u32[]{:S(2)}, u32[]{:S(2)}) collective-permute-start(bf16[128,1536]{1,0:T(8,128)(2,1)S(1)} %pad_maximum_fusion.38), channel_id=1, source_target_pairs={{0,1},{1,0},{2,3},{3,2},{4,5},{5,4},{6,7},{7,6},{8,9},{9,8},{10,11... | collective-permute-start | bytes 1179656 | tf_op jit(solution)/shard_map/ppermute | solution.py:258
  324.8 25.6 %collective-permute-start.43 = (bf16[1536,1024]{1,0:T(8,128)(2,1)S(1)}, bf16[1536,1024]{1,0:T(8,128)(2,1)S(1)}, u32[]{:S(2)}, u32[]{:S(2)}) collective-permute-start(bf16[1536,1024]{1,0:T(8,128)(2,1)S(1)} %pad_maximum_fusion.4), channel_id=1, source_target_pairs={{0,8},{8,0},{1,9},{9,1},{2,10},{10,2},{3,11},{11,3},{4,12},{12,4},... | collective-permute-start | bytes 9437192 | tf_op jit(solution)/shard_map/ppermute | solution.py:258
  368.1 13.7 %collective-permute-start.49 = (bf16[128,1536]{1,0:T(8,128)(2,1)S(1)}, bf16[128,1536]{1,0:T(8,128)(2,1)S(1)}, u32[]{:S(2)}, u32[]{:S(2)}) collective-permute-start(bf16[128,1536]{1,0:T(8,128)(2,1)S(1)} %pad_maximum_fusion.42), channel_id=1, source_target_pairs={{0,1},{1,0},{2,3},{3,2},{4,5},{5,4},{6,7},{7,6},{8,9},{9,8},{10,11... | collective-permute-start | bytes 1179656 | tf_op jit(solution)/shard_map/ppermute | solution.py:258
  374.7 10.0 %collective-permute-start.73 = (bf16[1,2,2,128]{3,2,1,0:T(2,128)(2,1)S(1)}, bf16[1,2,2,128]{3,2,1,0:T(2,128)(2,1)S(1)}, u32[]{:S(2)}, u32[]{:S(2)}) collective-permute-start(bf16[1,2,2,128]{3,2,1,0:T(2,128)(2,1)S(1)} %maximum_bitcast_fusion.5), channel_id=1, source_target_pairs={{0,8},{8,0},{1,9},{9,1},{2,10},{10,2},{3,11},{11,3},{4,12},{12,4},... | collective-permute-start | bytes 3080 | tf_op jit(solution)/shard_map/ppermute | solution.py:258
  385.4 219.4 %collective-permute-start.92 = (bf16[512,384]{1,0:T(8,128)(2,1)S(1)}, bf16[512,384]{1,0:T(8,128)(2,1)}, u32[]{:S(2)}, u32[]{:S(2)}) collective-permute-start(bf16[512,384]{1,0:T(8,128)(2,1)S(1)} %get-tuple-element.31), channel_id=1, source_target_pairs={{0,8},{8,0},{1,9},{9,1},{2,10},{10,2},{3,11},{11,3},{4,12},{12,4},... | collective-permute-start | bytes 1179656 | tf_op jit(solution)/shard_map/ppermute | solution.py:258
  392.9 38.5 %collective-permute-start.107 = (bf16[512,1536]{1,0:T(8,128)(2,1)S(1)}, bf16[512,1536]{1,0:T(8,128)(2,1)S(1)}, u32[]{:S(2)}, u32[]{:S(2)}) collective-permute-start(bf16[512,1536]{1,0:T(8,128)(2,1)S(1)} %copy-done.122), channel_id=1, source_target_pairs={{0,8},{8,0},{1,9},{9,1},{2,10},{10,2},{3,11},{11,3},{4,12},{12,4},... | collective-permute-start | bytes 4718600 | tf_op jit(solution)/shard_map/ppermute | solution.py:258
  397.1 74.5 %collective-permute-start.116 = (bf16[512,1024]{1,0:T(8,128)(2,1)}, bf16[512,1024]{1,0:T(8,128)(2,1)}, u32[]{:S(2)}, u32[]{:S(2)}) collective-permute-start(bf16[512,1024]{1,0:T(8,128)(2,1)} %multiply_convert_fusion.2), channel_id=1, source_target_pairs={{0,8},{8,0},{1,9},{9,1},{2,10},{10,2},{3,11},{11,3},{4,12},{12,4},... | collective-permute-start | bytes 3145736 | tf_op jit(solution)/shard_map/ppermute | solution.py:258
  438.7 15.2 %collective-permute-start.58 = (bf16[64,1536]{1,0:T(8,128)(2,1)S(1)}, bf16[64,1536]{1,0:T(8,128)(2,1)S(1)}, u32[]{:S(2)}, u32[]{:S(2)}) collective-permute-start(bf16[64,1536]{1,0:T(8,128)(2,1)S(1)} %get-tuple-element.99), channel_id=1, source_target_pairs={{0,2},{2,0},{1,3},{3,1},{4,6},{6,4},{5,7},{7,5},{8,10},{10,8},{9,1... | collective-permute-start | bytes 589832 | tf_op jit(solution)/shard_map/ppermute | solution.py:258
  440.9 32.5 %collective-permute-start.117 = (bf16[512,768]{1,0:T(8,128)(2,1)}, bf16[512,768]{1,0:T(8,128)(2,1)}, u32[]{:S(2)}, u32[]{:S(2)}) collective-permute-start(bf16[512,768]{1,0:T(8,128)(2,1)} %get-tuple-element.127), channel_id=1, source_target_pairs={{0,8},{8,0},{1,9},{9,1},{2,10},{10,2},{3,11},{11,3},{4,12},{12,4},... | collective-permute-start | bytes 2359304 | tf_op jit(solution)/shard_map/ppermute | solution.py:258
  469.2 17.3 %collective-permute-start.108 = (bf16[512,1024]{1,0:T(8,128)(2,1)S(1)}, bf16[512,1024]{1,0:T(8,128)(2,1)S(1)}, u32[]{:S(2)}, u32[]{:S(2)}) collective-permute-start(bf16[512,1024]{1,0:T(8,128)(2,1)S(1)} %copy-done.98), channel_id=1, source_target_pairs={{0,8},{8,0},{1,9},{9,1},{2,10},{10,2},{3,11},{11,3},{4,12},{12,4},... | collective-permute-start | bytes 3145736 | tf_op jit(solution)/shard_map/ppermute | solution.py:258
  481.5 49.1 %collective-permute-start.118 = (bf16[1024,384]{1,0:T(8,128)(2,1)}, bf16[1024,384]{1,0:T(8,128)(2,1)}, u32[]{:S(2)}, u32[]{:S(2)}) collective-permute-start(bf16[1024,384]{1,0:T(8,128)(2,1)} %constant_dynamic-slice_fusion), channel_id=1, source_target_pairs={{0,16},{16,0},{1,17},{17,1},{2,18},{18,2},{3,19},{19,3},{4,20},{20... | collective-permute-start | bytes 2359304 | tf_op jit(solution)/shard_map/ppermute | solution.py:258
  485.1 10.8 %collective-permute-start.62 = (bf16[128,1536]{1,0:T(8,128)(2,1)S(1)}, bf16[128,1536]{1,0:T(8,128)(2,1)S(1)}, u32[]{:S(2)}, u32[]{:S(2)}) collective-permute-start(bf16[128,1536]{1,0:T(8,128)(2,1)S(1)} %pad_maximum_fusion.48), channel_id=1, source_target_pairs={{0,2},{2,0},{1,3},{3,1},{4,6},{6,4},{5,7},{7,5},{8,10},{10,8},{9,1... | collective-permute-start | bytes 1179656 | tf_op jit(solution)/shard_map/ppermute | solution.py:258
  513.3 48.2 %collective-permute-start.63 = (bf16[512,384]{1,0:T(8,128)(2,1)}, bf16[512,384]{1,0:T(8,128)(2,1)}, u32[]{:S(2)}, u32[]{:S(2)}) collective-permute-start(bf16[512,384]{1,0:T(8,128)(2,1)} %bitcast.39), channel_id=1, source_target_pairs={{0,4},{4,0},{1,5},{5,1},{2,6},{6,2},{3,7},{7,3},{8,12},{12,8},{9,1... | collective-permute-start | bytes 1179656 | tf_op jit(solution)/shard_map/ppermute | solution.py:363
  515.7 43.2 %collective-permute-start.64 = (bf16[256,768]{1,0:T(8,128)(2,1)}, bf16[256,768]{1,0:T(8,128)(2,1)}, u32[]{:S(2)}, u32[]{:S(2)}) collective-permute-start(bf16[256,768]{1,0:T(8,128)(2,1)} %fusion.96), channel_id=1, source_target_pairs={{0,4},{4,0},{1,5},{5,1},{2,6},{6,2},{3,7},{7,3},{8,12},{12,8},{9,1... | collective-permute-start | bytes 1179656 | tf_op jit(solution)/shard_map/ppermute | solution.py:258
  530.7 45.1 %collective-permute-start.67 = (bf16[512,384]{1,0:T(8,128)(2,1)S(1)}, bf16[512,384]{1,0:T(8,128)(2,1)}, u32[]{:S(2)}, u32[]{:S(2)}) collective-permute-start(bf16[512,384]{1,0:T(8,128)(2,1)S(1)} %bitcast.214), channel_id=1, source_target_pairs={{0,4},{4,0},{1,5},{5,1},{2,6},{6,2},{3,7},{7,3},{8,12},{12,8},{9,1... | collective-permute-start | bytes 1179656 | tf_op jit(solution)/shard_map/ppermute | solution.py:363
  558.9 47.1 %collective-permute-start.93 = (bf16[512,768]{1,0:T(8,128)(2,1)}, bf16[512,768]{1,0:T(8,128)(2,1)}, u32[]{:S(2)}, u32[]{:S(2)}) collective-permute-start(bf16[512,768]{1,0:T(8,128)(2,1)} %get-tuple-element.135), channel_id=1, source_target_pairs={{0,8},{8,0},{1,9},{9,1},{2,10},{10,2},{3,11},{11,3},{4,12},{12,4},... | collective-permute-start | bytes 2359304 | tf_op jit(solution)/shard_map/ppermute | solution.py:258
  561.5 37.5 %collective-permute-start.119 = (bf16[1,512,384]{2,1,0:T(8,128)(2,1)}, bf16[1,512,384]{2,1,0:T(8,128)(2,1)}, u32[]{:S(2)}, u32[]{:S(2)}) collective-permute-start(bf16[1,512,384]{2,1,0:T(8,128)(2,1)} %dynamic-slice_convert_fusion.3), channel_id=1, source_target_pairs={{0,4},{4,0},{1,5},{5,1},{2,6},{6,2},{3,7},{7,3},{8,12},{12,8},{9,1... | collective-permute-start | bytes 1179656 | tf_op jit(solution)/shard_map/ppermute | solution.py:258
  594.3 14.7 %collective-permute-start.68 = (bf16[128,1536]{1,0:T(8,128)(2,1)}, bf16[128,1536]{1,0:T(8,128)(2,1)}, u32[]{:S(2)}, u32[]{:S(2)}) collective-permute-start(bf16[128,1536]{1,0:T(8,128)(2,1)} %pad_maximum_fusion.49), channel_id=1, source_target_pairs={{0,2},{2,0},{1,3},{3,1},{4,6},{6,4},{5,7},{7,5},{8,10},{10,8},{9,1... | collective-permute-start | bytes 1179656 | tf_op jit(solution)/shard_map/ppermute | solution.py:258
  604.0 10.1 %collective-permute-start.70 = (bf16[128,1536]{1,0:T(8,128)(2,1)S(1)}, bf16[128,1536]{1,0:T(8,128)(2,1)S(1)}, u32[]{:S(2)}, u32[]{:S(2)}) collective-permute-start(bf16[128,1536]{1,0:T(8,128)(2,1)S(1)} %pad_maximum_fusion.50), channel_id=1, source_target_pairs={{0,1},{1,0},{2,3},{3,2},{4,5},{5,4},{6,7},{7,6},{8,9},{9,8},{10,11... | collective-permute-start | bytes 1179656 | tf_op jit(solution)/shard_map/ppermute | solution.py:258
  604.7 91.9 %collective-permute-start.109 = (bf16[1536,512]{1,0:T(8,128)(2,1)}, bf16[1536,512]{1,0:T(8,128)(2,1)}, u32[]{:S(2)}, u32[]{:S(2)}) collective-permute-start(bf16[1536,512]{1,0:T(8,128)(2,1)} %constant_dynamic-slice_fusion.3), channel_id=1, source_target_pairs={{0,16},{16,0},{1,17},{17,1},{2,18},{18,2},{3,19},{19,3},{4,20},{20... | collective-permute-start | bytes 4718600 | tf_op jit(solution)/shard_map/ppermute | solution.py:258
  606.1 47.8 %collective-permute-start.100 = (bf16[128,768]{1,0:T(8,128)(2,1)}, bf16[128,768]{1,0:T(8,128)(2,1)S(1)}, u32[]{:S(2)}, u32[]{:S(2)}) collective-permute-start(bf16[128,768]{1,0:T(8,128)(2,1)} %get-tuple-element.194), channel_id=1, source_target_pairs={{0,2},{2,0},{1,3},{3,1},{4,6},{6,4},{5,7},{7,5},{8,10},{10,8},{9,1... | collective-permute-start | bytes 589832 | tf_op jit(solution)/shard_map/ppermute | solution.py:258
  609.1 165.3 %collective-permute-start.84 = (bf16[2,4,1,2,48,1152]{5,4,3,2,1,0:T(8,128)(2,1)}, bf16[2,4,1,2,48,1152]{5,4,3,2,1,0:T(8,128)(2,1)}, u32[]{:S(2)}, u32[]{:S(2)}) collective-permute-start(bf16[2,4,1,2,48,1152]{5,4,3,2,1,0:T(8,128)(2,1)} %constant_dynamic-slice_fusion.10), channel_id=1, source_target_pairs={{0,8},{8,0},{1,9},{9,1},{2,10},{10,2},{3,11},{11,3},{4,12},{12,4},... | collective-permute-start | bytes 5308424 | tf_op jit(solution)/shard_map/ppermute | solution.py:258
  614.2 32.0 %collective-permute-start.120 = (bf16[512,384]{1,0:T(8,128)(2,1)S(1)}, bf16[512,384]{1,0:T(8,128)(2,1)S(1)}, u32[]{:S(2)}, u32[]{:S(2)}) collective-permute-start(bf16[512,384]{1,0:T(8,128)(2,1)S(1)} %fusion.105), channel_id=1, source_target_pairs={{0,16},{16,0},{1,17},{17,1},{2,18},{18,2},{3,19},{19,3},{4,20},{20... | collective-permute-start | bytes 1179656 | tf_op jit(solution)/shard_map/ppermute | solution.py:258
  653.8 12.3 %collective-permute-start.94 = (bf16[384,384]{1,0:T(8,128)(2,1)S(1)}, bf16[384,384]{1,0:T(8,128)(2,1)}, u32[]{:S(2)}, u32[]{:S(2)}) collective-permute-start(bf16[384,384]{1,0:T(8,128)(2,1)S(1)} %constant_dynamic-slice_fusion.7), channel_id=1, source_target_pairs={{0,16},{16,0},{1,17},{17,1},{2,18},{18,2},{3,19},{19,3},{4,20},{20... | collective-permute-start | bytes 884744 | tf_op jit(solution)/shard_map/ppermute | solution.py:258
  658.6 76.6 %collective-permute-start.121 = (bf16[512,768]{1,0:T(8,128)(2,1)}, bf16[512,768]{1,0:T(8,128)(2,1)}, u32[]{:S(2)}, u32[]{:S(2)}) collective-permute-start(bf16[512,768]{1,0:T(8,128)(2,1)} %pad_maximum_fusion.23), channel_id=1, source_target_pairs={{0,8},{8,0},{1,9},{9,1},{2,10},{10,2},{3,11},{11,3},{4,12},{12,4},... | collective-permute-start | bytes 2359304 | tf_op jit(solution)/shard_map/ppermute | solution.py:258
  696.0 17.4 %collective-permute-start.101 = (bf16[256,768]{1,0:T(8,128)(2,1)}, bf16[256,768]{1,0:T(8,128)(2,1)S(1)}, u32[]{:S(2)}, u32[]{:S(2)}) collective-permute-start(bf16[256,768]{1,0:T(8,128)(2,1)} %get-tuple-element.215), channel_id=1, source_target_pairs={{0,1},{1,0},{2,3},{3,2},{4,5},{5,4},{6,7},{7,6},{8,9},{9,8},{10,11... | collective-permute-start | bytes 1179656 | tf_op jit(solution)/shard_map/ppermute | solution.py:258
  707.3 17.9 %collective-permute-start.96 = (bf16[192,384]{1,0:T(8,128)(2,1)S(1)}, bf16[192,384]{1,0:T(8,128)(2,1)S(1)}, u32[]{:S(2)}, u32[]{:S(2)}) collective-permute-start(bf16[192,384]{1,0:T(8,128)(2,1)S(1)} %fusion.158), channel_id=1, source_target_pairs={{0,16},{16,0},{1,17},{17,1},{2,18},{18,2},{3,19},{19,3},{4,20},{20... | collective-permute-start | bytes 442376 | tf_op jit(solution)/shard_map/ppermute | solution.py:258
  731.1 36.8 %collective-permute-start.110 = (bf16[1,4,192,512]{3,2,1,0:T(8,128)(2,1)S(1)}, bf16[1,4,192,512]{3,2,1,0:T(8,128)(2,1)S(1)}, u32[]{:S(2)}, u32[]{:S(2)}) collective-permute-start(bf16[1,4,192,512]{3,2,1,0:T(8,128)(2,1)S(1)} %copy-done.99), channel_id=1, source_target_pairs={{0,4},{4,0},{1,5},{5,1},{2,6},{6,2},{3,7},{7,3},{8,12},{12,8},{9,1... | collective-permute-start | bytes 2359304 | tf_op jit(solution)/shard_map/ppermute | solution.py:258
  732.6 46.5 %collective-permute-start.103 = (bf16[256,1536]{0,1:T(8,128)(2,1)}, bf16[256,1536]{0,1:T(8,128)(2,1)}, u32[]{:S(2)}, u32[]{:S(2)}) collective-permute-start(bf16[256,1536]{0,1:T(8,128)(2,1)} %get-tuple-element.133), channel_id=1, source_target_pairs={{0,8},{8,0},{1,9},{9,1},{2,10},{10,2},{3,11},{11,3},{4,12},{12,4},... | collective-permute-start | bytes 2359304 | tf_op jit(solution)/shard_map/ppermute | solution.py:258
  769.2 15.8 %collective-permute-start.111 = (bf16[1,192,512]{2,1,0:T(8,128)(2,1)}, bf16[1,192,512]{2,1,0:T(8,128)(2,1)}, u32[]{:S(2)}, u32[]{:S(2)}) collective-permute-start(bf16[1,192,512]{2,1,0:T(8,128)(2,1)} %get-tuple-element.167), channel_id=1, source_target_pairs={{0,1},{1,0},{2,3},{3,2},{4,5},{5,4},{6,7},{7,6},{8,9},{9,8},{10,11... | collective-permute-start | bytes 589832 | tf_op jit(solution)/shard_map/ppermute | solution.py:390
  770.6 16.4 %collective-permute-start.112 = (bf16[1,192,512]{2,1,0:T(8,128)(2,1)}, bf16[1,192,512]{2,1,0:T(8,128)(2,1)}, u32[]{:S(2)}, u32[]{:S(2)}) collective-permute-start(bf16[1,192,512]{2,1,0:T(8,128)(2,1)} %get-tuple-element.166), channel_id=1, source_target_pairs={{0,2},{2,0},{1,3},{3,1},{4,6},{6,4},{5,7},{7,5},{8,10},{10,8},{9,1... | collective-permute-start | bytes 589832 | tf_op jit(solution)/shard_map/ppermute | solution.py:390
  775.2 13.7 %collective-permute-start.113 = (bf16[1,192,512]{2,1,0:T(8,128)(2,1)}, bf16[1,192,512]{2,1,0:T(8,128)(2,1)S(1)}, u32[]{:S(2)}, u32[]{:S(2)}) collective-permute-start(bf16[1,192,512]{2,1,0:T(8,128)(2,1)} %get-tuple-element.165), channel_id=1, source_target_pairs={{0,3},{1,2},{2,1},{3,0},{4,7},{5,6},{6,5},{7,4},{8,11},{9,10},{10,... | collective-permute-start | bytes 589832 | tf_op jit(solution)/shard_map/ppermute | solution.py:390
  783.4 35.9 %collective-permute-start.104 = (bf16[512,768]{1,0:T(8,128)(2,1)}, bf16[512,768]{1,0:T(8,128)(2,1)}, u32[]{:S(2)}, u32[]{:S(2)}) collective-permute-start(bf16[512,768]{1,0:T(8,128)(2,1)} %constant_dynamic-slice_fusion.4), channel_id=1, source_target_pairs={{0,16},{16,0},{1,17},{17,1},{2,18},{18,2},{3,19},{19,3},{4,20},{20... | collective-permute-start | bytes 2359304 | tf_op jit(solution)/shard_map/ppermute | solution.py:258
  815.5 17.4 %collective-permute-start.114 = (bf16[192,2048]{1,0:T(8,128)(2,1)S(1)}, bf16[192,2048]{1,0:T(8,128)(2,1)S(1)}, u32[]{:S(2)}, u32[]{:S(2)}) collective-permute-start(bf16[192,2048]{1,0:T(8,128)(2,1)S(1)} %bitcast.230), channel_id=1, source_target_pairs={{0,16},{16,0},{1,17},{17,1},{2,18},{18,2},{3,19},{19,3},{4,20},{20... | collective-permute-start | bytes 2359304 | tf_op jit(solution)/shard_map/ppermute | solution.py:258
  815.7 36.2 %collective-permute-start.85 = (bf16[2,4,1,48,1152]{4,3,1,0,2:T(8,128)(2,1)S(1)}, bf16[2,4,1,48,1152]{4,3,1,0,2:T(8,128)(2,1)S(1)}, u32[]{:S(2)}, u32[]{:S(2)}) collective-permute-start(bf16[2,4,1,48,1152]{4,3,1,0,2:T(8,128)(2,1)S(1)} %fusion.56), channel_id=1, source_target_pairs={{0,16},{16,0},{1,17},{17,1},{2,18},{18,2},{3,19},{19,3},{4,20},{20... | collective-permute-start | bytes 2654216 | tf_op jit(solution)/shard_map/ppermute | solution.py:258
  821.5 62.5 %collective-permute-start.105 = (bf16[512,768]{1,0:T(8,128)(2,1)}, bf16[512,768]{1,0:T(8,128)(2,1)}, u32[]{:S(2)}, u32[]{:S(2)}) collective-permute-start(bf16[512,768]{1,0:T(8,128)(2,1)} %reduce-precision_convert_fusion.2), channel_id=1, source_target_pairs={{0,16},{16,0},{1,17},{17,1},{2,18},{18,2},{3,19},{19,3},{4,20},{20... | collective-permute-start | bytes 2359304 | tf_op jit(solution)/shard_map/ppermute | solution.py:258
  852.1 22.5 %collective-permute-start.86 = (bf16[1,4,48,1152]{3,2,1,0:T(8,128)(2,1)S(1)}, bf16[1,4,48,1152]{3,2,1,0:T(8,128)(2,1)S(1)}, u32[]{:S(2)}, u32[]{:S(2)}) collective-permute-start(bf16[1,4,48,1152]{3,2,1,0:T(8,128)(2,1)S(1)} %fusion.103), channel_id=1, source_target_pairs={{0,4},{4,0},{1,5},{5,1},{2,6},{6,2},{3,7},{7,3},{8,12},{12,8},{9,1... | collective-permute-start | bytes 1327112 | tf_op jit(solution)/shard_map/ppermute | solution.py:258
  853.2 43.6 %collective-permute-start.115 = (bf16[192,4096]{1,0:T(8,128)(2,1)S(1)}, bf16[192,4096]{1,0:T(8,128)(2,1)}, u32[]{:S(2)}, u32[]{:S(2)}) collective-permute-start(bf16[192,4096]{1,0:T(8,128)(2,1)S(1)} %pad_maximum_fusion.14), channel_id=1, source_target_pairs={{0,8},{8,0},{1,9},{9,1},{2,10},{10,2},{3,11},{11,3},{4,12},{12,4},... | collective-permute-start | bytes 4718600 | tf_op jit(solution)/shard_map/ppermute | solution.py:258
  885.7 19.2 %collective-permute-start.106 = (bf16[512,1536]{1,0:T(8,128)(2,1)S(1)}, bf16[512,1536]{1,0:T(8,128)(2,1)S(1)}, u32[]{:S(2)}, u32[]{:S(2)}) collective-permute-start(bf16[512,1536]{1,0:T(8,128)(2,1)S(1)} %pad_maximum_fusion.13), channel_id=1, source_target_pairs={{0,8},{8,0},{1,9},{9,1},{2,10},{10,2},{3,11},{11,3},{4,12},{12,4},... | collective-permute-start | bytes 4718600 | tf_op jit(solution)/shard_map/ppermute | solution.py:258
  (237 other events, 3327.1 us)

commit v2 on v1

v2 whole, which is shorter than its diff:
```python
import functools

import jax
import jax.numpy as jnp
from jax import lax
from jax.experimental import pallas as pl
from jax.experimental.pallas import tpu as pltpu
from jax.sharding import Mesh, PartitionSpec as P

HEADS = 24
HEAD = 64
D = 1536
FF = 4096
CAP = 128
CLIPS = 2
PAIR = 2 * HEAD

PRECISE = lax.Precision.HIGHEST
EPSILON = 1e-06
NEGATIVE = -1e30
F32 = jnp.float32
LOW = jnp.bfloat16
SWAP = [(0, 1), (1, 0)]


def inv_root(values):
    return lax.rsqrt(jnp.mean(values * values, -1, keepdims=True) + EPSILON)


def unit_rows(values):
    return values * inv_root(values)


def norm_back(grad_in, values, gain):
    root = inv_root(values)
    normed = values * root
    inner = grad_in * gain
    back = root * (inner - normed * jnp.mean(inner * normed, -1, keepdims=True))
    return back, jnp.sum(grad_in * normed, 0)


def rounded(values):
    return lax.reduce_precision(values, 8, 7)


def low(values):
    return rounded(values).astype(LOW)


def dot(a, b, dims=((1,), (0,))):
    return lax.dot_general(a, b, (dims, ((), ())), preferred_element_type=F32)


def nt(a, b):
    return lax.dot_general(a, b, (((1,), (1,)), ((), ())), preferred_element_type=F32)


def tn(a, b):
    return lax.dot_general(a, b, (((0,), (0,)), ((), ())), preferred_element_type=F32)


def nn(a, b):
    return lax.dot_general(a, b, (((1,), (0,)), ((), ())), preferred_element_type=F32)


def cross_bias(seg_col, count):
    clip = lax.broadcasted_iota(jnp.int32, (1, count), 1) // CAP
    return jnp.where(seg_col == clip, 0.0, NEGATIVE)


def forward_near(q_ref, k_ref, v_ref, ck_ref, cv_ref, sq_ref, sk_ref, o_ref, oc_ref, st_ref):
    seg_col = sq_ref[...]
    bias = jnp.where(seg_col == sk_ref[...], 0.0, NEGATIVE)
    bias_cross = cross_bias(seg_col, ck_ref.shape[0])
    for h in range(2):
        at = slice(h * HEAD, (h + 1) * HEAD)
        q = q_ref[:, at]
        s = nt(q, k_ref[:, at]) + bias
        m = jnp.max(s, -1, keepdims=True)
        e = jnp.exp(s - m)
        st_ref[0, :, h : h + 1] = m
        st_ref[0, :, 2 + h : 3 + h] = jnp.sum(e, -1, keepdims=True)
        o_ref[:, at] = nn(e.astype(LOW), v_ref[:, at])
        s = nt(q, ck_ref[:, at]) + bias_cross
        m = jnp.max(s, -1, keepdims=True)
        e = jnp.exp(s - m)
        total = jnp.sum(e, -1, keepdims=True)
        st_ref[0, :, 4 + h : 5 + h] = m + jnp.log(total)
        oc_ref[:, at] = nn(e.astype(LOW), cv_ref[:, at]) / total


def forward_far(
    count, q_ref, k_ref, v_ref, sq_ref, sk_ref, o_ref, oc_ref, st_ref, gate_ref, os_ref, mix_ref, lse_ref, m_ref, l_ref
):
    step = pl.program_id(1)

    @pl.when(step == 0)
    def _():
        os_ref[...] = o_ref[...]
        m_ref[...] = st_ref[0, :, 0:2]
        l_ref[...] = st_ref[0, :, 2:4]

    bias = jnp.where(sq_ref[...] == sk_ref[0], 0.0, NEGATIVE)
    for h in range(2):
        at = slice(h * HEAD, (h + 1) * HEAD)
        s = nt(q_ref[:, at], k_ref[0, :, at]) + bias
        before = m_ref[:, h : h + 1]
        m = jnp.maximum(before, jnp.max(s, -1, keepdims=True))
        e = jnp.exp(s - m)
        factor = jnp.exp(before - m)
        m_ref[:, h : h + 1] = m
        l_ref[:, h : h + 1] = l_ref[:, h : h + 1] * factor + jnp.sum(e, -1, keepdims=True)
        os_ref[:, at] = os_ref[:, at] * factor + nn(e.astype(LOW), v_ref[0, :, at])

    @pl.when(step == count - 1)
    def _():
        for h in range(2):
            at = slice(h * HEAD, (h + 1) * HEAD)
            total = l_ref[:, h : h + 1]
            out = os_ref[:, at] / total
            os_ref[:, at] = out
            mix_ref[:, at] = (out + gate_ref[:, at] * oc_ref[:, at]).astype(LOW)
            lse_ref[0, :, h : h + 1] = m_ref[:, h : h + 1] + jnp.log(total)


def backward_far(
    q_ref, g_ref, os_ref, oc_ref, lse_ref, st_ref, gate_ref, k_ref, v_ref, ck_ref, cv_ref, sq_ref, sk_ref,
    dq_ref, dkv_ref, dck_ref, dcv_ref, dh_ref, delta_ref,
):
    step = pl.program_id(1)
    seg_col = sq_ref[...]
    scaling = HEAD**-0.5

    @pl.when(step == 0)
    def _():
        bias_cross = cross_bias(seg_col, ck_ref.shape[0])
        g = g_ref[...].astype(F32)
        dh_ref[...] = jnp.sum(g * oc_ref[...], 0, keepdims=True)
        for h in range(2):
            at = slice(h * HEAD, (h + 1) * HEAD)
            gh = g[:, at]
            delta_ref[0, :, h : h + 1] = jnp.sum(gh * os_ref[:, at], -1, keepdims=True)
            gc = (gate_ref[:, at] * gh).astype(LOW)
            delta = jnp.sum(gc.astype(F32) * oc_ref[:, at], -1, keepdims=True)
            q = q_ref[:, at]
            p = jnp.exp(nt(q, ck_ref[:, at]) + bias_cross - st_ref[0, :, 4 + h : 5 + h])
            ds = (p * (nt(gc, cv_ref[:, at]) - delta)).astype(LOW)
            dq_ref[:, at] = nn(ds, ck_ref[:, at]) * scaling
            dck_ref[:, at] = tn(ds, q).astype(dck_ref.dtype)
            dcv_ref[:, at] = tn(p.astype(LOW), gc).astype(dcv_ref.dtype)

    bias = jnp.where(seg_col == sk_ref[0], 0.0, NEGATIVE)
    for h in range(2):
        at = slice(h * HEAD, (h + 1) * HEAD)
        q = q_ref[:, at]
        g = g_ref[:, at]
        k = k_ref[0, :, at]
        p = jnp.exp(nt(q, k) + bias - lse_ref[0, :, h : h + 1])
        ds = (p * (nt(g, v_ref[0, :, at]) - delta_ref[0, :, h : h + 1])).astype(LOW)
        dq_ref[:, at] += nn(ds, k) * scaling
        dkv_ref[0, 0, :, at] = tn(ds, q).astype(LOW)
        dkv_ref[0, 1, :, at] = tn(p.astype(LOW), g).astype(LOW)


def backward_near(q_ref, g_ref, lse_ref, delta_ref, k_ref, v_ref, sq_ref, sk_ref, dp_ref, dq_ref, dk_ref, dv_ref):
    bias = jnp.where(sq_ref[...] == sk_ref[...], 0.0, NEGATIVE)
    scaling = HEAD**-0.5
    for h in range(2):
        at = slice(h * HEAD, (h + 1) * HEAD)
        q = q_ref[:, at]
        g = g_ref[:, at]
        k = k_ref[:, at]
        p = jnp.exp(nt(q, k) + bias - lse_ref[0, :, h : h + 1])
        ds = (p * (nt(g, v_ref[:, at]) - delta_ref[0, :, h : h + 1])).astype(LOW)
        dq_ref[:, at] = dp_ref[:, at] + nn(ds, k) * scaling
        dk_ref[:, at] = tn(ds, q)
        dv_ref[:, at] = tn(p.astype(LOW), g)


def swapped(x):
    lane = lax.broadcasted_iota(jnp.int32, x.shape, 1)
    return jnp.where(lane % 2 == 0, pltpu.roll(x, x.shape[1] - 1, 1), pltpu.roll(x, 1, 1))


def heads_in(q_ref, k_ref, v_ref, inv_ref, gq_ref, gk_ref, cos_ref, sin_ref, q_out, kv_out):
    cosine, sine = cos_ref[...], sin_ref[...]
    q = q_ref[...] * inv_ref[:, 0:1] * gq_ref[...]
    k = k_ref[...] * inv_ref[:, 1:2] * gk_ref[...]
    q = (q * cosine + swapped(q) * sine).astype(LOW)
    q_out[...] = (q.astype(F32) * HEAD**-0.5).astype(LOW)
    kv_out[0] = (k * cosine + swapped(k) * sine).astype(LOW)
    kv_out[1] = v_ref[...].astype(LOW)


def heads_back(
    dq_ref, dk_ref, far_ref, q_ref, k_ref, inv_ref, gq_ref, gk_ref, cos_ref, sin_ref, iq_out, ik_out, st_out, gg_out
):
    cosine, sine = cos_ref[...], sin_ref[...]
    dq = dq_ref[...]
    dk = dk_ref[...] + far_ref[0].astype(F32)
    uq = q_ref[...] * inv_ref[:, 0:1]
    uk = k_ref[...] * inv_ref[:, 1:2]
    tq = dq * cosine - swapped(dq) * sine
    tk = dk * cosine - swapped(dk) * sine
    gg_out[0:1] = jnp.sum(tq * uq, 0, keepdims=True)
    gg_out[1:2] = jnp.sum(tk * uk, 0, keepdims=True)
    iq = tq * gq_ref[...]
    ik = tk * gk_ref[...]
    iq_out[...] = iq
    ik_out[...] = ik
    st_out[0, :, 0:1] = jnp.sum(iq * uq, -1, keepdims=True)
    st_out[0, :, 1:2] = jnp.sum(ik * uk, -1, keepdims=True)


def head_calls(tokens, width):
    pairs = width // PAIR
    sds = jax.ShapeDtypeStruct

    def at(first):
        return pl.BlockSpec((tokens, PAIR), lambda i: (0, first + i))

    row = pl.BlockSpec((1, PAIR), lambda i: (0, i))
    fixed = pl.BlockSpec((tokens, PAIR), lambda i: (0, 0))
    inv = pl.BlockSpec((tokens, 2), lambda i: (0, 0))
    both = pl.BlockSpec((2, tokens, PAIR), lambda i: (0, 0, i))
    cost = pl.CostEstimate(flops=20 * tokens * width, bytes_accessed=20 * tokens * width, transcendentals=0)
    into = pl.pallas_call(
        heads_in,
        grid=(pairs,),
        in_specs=[at(0), at(pairs), at(2 * pairs), inv, row, row, fixed, fixed],
        out_specs=[at(0), both],
        out_shape=[sds((tokens, width), LOW), sds((2, tokens, width), LOW)],
        cost_estimate=cost,
        name="heads_in",
    )
    back = pl.pallas_call(
        heads_back,
        grid=(pairs,),
        in_specs=[at(0), at(0), pl.BlockSpec((1, tokens, PAIR), lambda i: (0, 0, i)), at(0), at(pairs), inv, row, row, fixed, fixed],
        out_specs=[at(0), at(0), pl.BlockSpec((1, tokens, 2), lambda i: (i, 0, 0)), pl.BlockSpec((2, PAIR), lambda i: (0, i))],
        out_shape=[sds((tokens, width), F32), sds((tokens, width), F32), sds((pairs, tokens, 2), F32), sds((2, width), F32)],
        cost_estimate=cost,
        name="heads_back",
    )
    return into, back


def place_columns(place, groups, outer, rest, lead):
    whole = 4 * outer * rest
    return [
        g * whole + ((place * outer + o) if lead else (o * 4 + place)) * rest for g in range(groups) for o in range(outer)
    ]


def cut_kernel(columns, rest, me_ref, x_ref, *outs):
    for me in range(4):

        @pl.when(me_ref[0] == me)
        def _():
            for r, out in enumerate(outs):
                for j, start in enumerate(columns[me ^ r]):
                    out[:, j * rest : (j + 1) * rest] = x_ref[:, start : start + rest]


def lay_kernel(columns, rest, blank, me_ref, *refs):
    ins, out = refs[:-1], refs[-1]
    if blank:
        out[...] = jnp.zeros_like(out)
    for me in range(4):

        @pl.when(me_ref[0] == me)
        def _():
            for r, value in enumerate(ins):
                for j, start in enumerate(columns[me ^ r]):
                    out[:, start : start + rest] = value[:, j * rest : (j + 1) * rest]


def caption_kernel(columns, rest, rows_ref, weight_ref, out_ref):
    product = nn(rows_ref[...], weight_ref[...])
    for place in range(4):
        for j, start in enumerate(columns[place]):
            out_ref[place, :, j * rest : (j + 1) * rest] = product[:, start : start + rest].astype(out_ref.dtype)


def assemble_kernel(plan, width, at_ref, *refs):
    ins, out, sems = refs[:-2], refs[-2], refs[-1]
    copies = []
    for i, (source, first, rows) in enumerate(plan):
        row = pl.multiple_of(at_ref[2 * i], 16)
        col = pl.multiple_of(at_ref[2 * i + 1], 128)
        copies.append(
            pltpu.make_async_copy(
                ins[source].at[pl.ds(first, rows)], out.at[pl.ds(row, rows), pl.ds(col, width)], sems.at[i]
            )
        )
    for copy in copies:
        copy.start()
    for copy in copies:
        copy.wait()


def product_kernel(left_ref, right_ref, out_ref):
    out_ref[0] = tn(left_ref[...], right_ref[...]).astype(out_ref.dtype)


def grad_product(left, right, parts):
    rows, cols = left.shape[1], right.shape[1] // parts
    tile = 512 if rows % 512 == 0 else rows
    return pl.pallas_call(
        product_kernel,
        grid=(parts, rows // tile),
        in_specs=[
            pl.BlockSpec((left.shape[0], tile), lambda q, i: (0, i)),
            pl.BlockSpec((left.shape[0], cols), lambda q, i: (0, q)),
        ],
        out_specs=pl.BlockSpec((1, tile, cols), lambda q, i: (q, i, 0)),
        out_shape=jax.ShapeDtypeStruct((parts, rows, cols), LOW),
        cost_estimate=pl.CostEstimate(
            flops=2 * left.shape[0] * rows * right.shape[1],
            bytes_accessed=2 * (rows * right.shape[1] + left.size + right.size),
            transcendentals=0,
        ),
        compiler_params=pltpu.CompilerParams(fuse_transposed_lhs_in_matmul=True),
        name="grad_product",
    )(left, right)


def assemble(inputs, plan, places, shape):
    width = inputs[0].shape[1]
    at = jnp.stack([jnp.asarray(v, jnp.int32) for pair in places for v in pair])
    size = 2 * shape[0] * shape[1] * 2
    return pl.pallas_call(
        functools.partial(assemble_kernel, plan, width),
        grid_spec=pltpu.PrefetchScalarGridSpec(
            num_scalar_prefetch=1,
            grid=(1,),
            in_specs=[pl.BlockSpec(memory_space=pl.ANY)] * len(inputs),
            out_specs=pl.BlockSpec(memory_space=pltpu.VMEM),
            scratch_shapes=[pltpu.SemaphoreType.DMA((len(plan),))],
        ),
        out_shape=jax.ShapeDtypeStruct(shape, inputs[0].dtype),
        compiler_params=pltpu.CompilerParams(vmem_limit_bytes=32 * 1024 * 1024),
        cost_estimate=pl.CostEstimate(flops=0, bytes_accessed=size, transcendentals=0),
        name="assemble",
    )(at, *inputs)


def attention_calls(tokens, width, capt, far):
    pairs = width // PAIR
    sds = jax.ShapeDtypeStruct

    def cols(rows):
        return pl.BlockSpec((rows, PAIR), lambda i, *r: (0, i))

    def stat(n):
        return pl.BlockSpec((1, tokens, n), lambda i, *r: (i, 0, 0))

    seg_col = pl.BlockSpec((tokens, 1), lambda i, *r: (0, 0))
    seg_row = pl.BlockSpec((1, tokens), lambda i, *r: (0, 0))
    far_k = pl.BlockSpec((1, None, tokens, PAIR), lambda i, r: (r, 0, 0, i))
    far_v = pl.BlockSpec((1, None, tokens, PAIR), lambda i, r: (r, 1, 0, i))
    far_both = pl.BlockSpec((1, 2, tokens, PAIR), lambda i, r: (r, 0, 0, i))
    near_k = pl.BlockSpec((None, tokens, PAIR), lambda i, *r: (0, 0, i))
    near_v = pl.BlockSpec((None, tokens, PAIR), lambda i, *r: (1, 0, i))
    far_row = pl.BlockSpec((1, 1, tokens), lambda i, r: (r, 0, 0))
    gate = cols(1)
    tok, cap = cols(tokens), cols(capt)

    def cost(keys, products):
        return pl.CostEstimate(
            flops=2 * tokens * keys * width * products,
            bytes_accessed=8 * tokens * width * 4,
            transcendentals=tokens * keys * (width // HEAD),
        )

    params = pltpu.CompilerParams(vmem_limit_bytes=48 * 1024 * 1024)
    near = pl.pallas_call(
        forward_near,
        grid=(pairs,),
        in_specs=[tok, near_k, near_v, cap, cap, seg_col, seg_row],
        out_specs=[tok, tok, stat(8)],
        out_shape=[sds((tokens, width), F32), sds((tokens, width), F32), sds((pairs, tokens, 8), F32)],
        compiler_params=params,
        cost_estimate=cost(tokens + capt, 2),
        name="attn_near",
    )
    away = pl.pallas_call(
        functools.partial(forward_far, far),
        grid=(pairs, far),
        in_specs=[tok, far_k, far_v, seg_col, far_row, tok, tok, stat(8), gate],
        out_specs=[tok, tok, stat(2)],
        out_shape=[sds((tokens, width), F32), sds((tokens, width), LOW), sds((pairs, tokens, 2), F32)],
        scratch_shapes=[pltpu.VMEM((tokens, 2), F32), pltpu.VMEM((tokens, 2), F32)],
        compiler_params=params,
        cost_estimate=cost(tokens * far, 2),
        name="attn_far",
    )
    back_away = pl.pallas_call(
        backward_far,
        grid=(pairs, far),
        in_specs=[tok, tok, tok, tok, stat(2), stat(8), gate, far_k, far_v, cap, cap, seg_col, far_row],
        out_specs=[tok, far_both, cap, cap, gate, stat(2)],
        out_shape=[
            sds((tokens, width), F32),
            sds((far, 2, tokens, width), LOW),
            sds((capt, width), F32),
            sds((capt, width), F32),
            sds((1, width), F32),
            sds((pairs, tokens, 2), F32),
        ],
        compiler_params=params,
        cost_estimate=cost(tokens * far + capt, 5),
        name="attn_back_far",
    )
    back_near = pl.pallas_call(
        backward_near,
        grid=(pairs,),
        in_specs=[tok, tok, stat(2), stat(2), near_k, near_v, seg_col, seg_row, tok],
        out_specs=[tok, tok, tok],
        out_shape=[sds((tokens, width), F32)] * 3,
        compiler_params=params,
        cost_estimate=cost(tokens, 5),
        name="attn_back_near",
    )
    return near, away, back_away, back_near


def swap(value, axis):
    return lax.ppermute(value, axis, SWAP)


def pair_stack(value, axis, dim):
    other = swap(value, axis)
    first = lax.axis_index(axis) == 0
    return jnp.concatenate([jnp.where(first, value, other), jnp.where(first, other, value)], dim)


def first_of(value):
    return value[(0,) * value.ndim].astype(F32)


def when(value):
    probe = first_of(value)
    return jnp.where(probe != probe, 1, 0)


def hold(value, *after):
    for other in after:
        value = value + (first_of(other) * 0.0).astype(value.dtype)
    return value


def on_device(
    outer,
    lead,
    hidden,
    segments,
    positions,
    condition,
    captions,
    dropped,
    null_caption,
    ada_weight,
    ada_bias,
    qkv_weight,
    out_weight,
    caption_weight,
    gate_up,
    down_weight,
    gains,
    head_gate,
    cotangent,
):
    me_c = lax.axis_index("p") * 2 + lax.axis_index("y")
    me_o = lax.axis_index("o")
    core = lax.axis_index("core")
    me_x = lax.axis_index("x")
    me_b = lax.axis_index(("p", "y", "o") if lead else ("o", "p", "y"))
    me_arg = me_c.reshape(1).astype(jnp.int32)
    tokens = hidden.shape[0]
    square = 4 * tokens
    width = D // 4
    capt = CLIPS * CAP
    blk = 4 * outer
    rest = D // blk
    mirrored = outer == 2
    t_axis, g_axis = ("core", "o") if mirrored else ("o", "core")
    t_size = 2 if mirrored else outer
    me_t, me_g = lax.axis_index(t_axis), lax.axis_index(g_axis)
    across = [[(i, i ^ r) for i in range(4)] for r in range(4)]
    beyond = [[(i, i ^ r) for i in range(outer)] for r in range(outer)]

    def unblocks(value):
        if lead:
            value = value.swapaxes(-3, -2)
        return value.reshape(value.shape[:-3] + (-1,))

    def row_blocks(value):
        size = value.shape[0] // blk
        if lead:
            return value.reshape((4, outer, size) + value.shape[1:]).swapaxes(0, 1)
        return value.reshape((outer, 4, size) + value.shape[1:])

    def block_index(o, c):
        return c * outer + o if lead else o * 4 + c

    def cut(value, groups, count):
        size = value.shape[1] // (groups * blk)
        columns = [place_columns(c, groups, outer, size, lead) for c in range(4)]
        out = jax.ShapeDtypeStruct((value.shape[0], groups * outer * size), value.dtype)
        return pl.pallas_call(
            functools.partial(cut_kernel, columns, size),
            in_specs=[pl.BlockSpec(memory_space=pltpu.SMEM), pl.BlockSpec(memory_space=pltpu.VMEM)],
            out_specs=[pl.BlockSpec(memory_space=pltpu.VMEM)] * count,
            out_shape=[out] * count,
            name="cut",
        )(me_arg, value)

    def lay(pieces, groups):
        size = pieces[0].shape[1] // (groups * outer)
        columns = [place_columns(c, groups, outer, size, lead) for c in range(4)]
        shape = (pieces[0].shape[0], 4 * pieces[0].shape[1])
        return pl.pallas_call(
            functools.partial(lay_kernel, columns, size, len(pieces) < 4),
            in_specs=[pl.BlockSpec(memory_space=pltpu.SMEM)] + [pl.BlockSpec(memory_space=pltpu.VMEM)] * len(pieces),
            out_specs=pl.BlockSpec(memory_space=pltpu.VMEM),
            out_shape=jax.ShapeDtypeStruct(shape, pieces[0].dtype),
            name="lay",
        )(me_arg, *pieces)

    def outer_reduce(value):
        if outer == 2:
            sent = lax.dynamic_index_in_dim(value, 1 - me_o, 0, keepdims=False).astype(LOW)
            kept = lax.dynamic_index_in_dim(value, me_o, 0, keepdims=False)
            return kept.astype(F32) + swap(sent, "o").astype(F32)
        return lax.psum_scatter(value.astype(LOW), "o", scatter_dimension=0).astype(F32)

    def axis_sum(value, axis):
        if axis != "o" or outer == 2:
            return rounded(value) + swap(low(value), axis).astype(F32)
        return lax.psum(low(value), axis).astype(F32)

    def mirror(value):
        if not mirrored:
            return value
        other = lax.ppermute(value, ("core", "o"), [(1, 2), (2, 1)])
        return jnp.where(core == me_o, value, other)

    def far(value):
        return jnp.stack([lax.ppermute(value, t_axis, [(i, i ^ r) for i in range(t_size)]) for r in range(1, t_size)])

    def to_place(value, r):
        return lax.ppermute(value, ("p", "y"), across[r])

    def gather_places(rows):
        return [rows] + [to_place(rows, r) for r in (1, 2, 3)]

    def gather_square(rows):
        return jnp.concatenate(gather_places(rows))

    def scatter_places(parts):
        total = parts[0]
        for r in (1, 2, 3):
            total = total + to_place(parts[r].astype(LOW), r).astype(F32)
        return total

    def scatter_square(full):
        return scatter_places([full[r * tokens : (r + 1) * tokens] for r in range(4)])

    def square_sum(value, shared=None):
        count = 4 * value.shape[0]
        whole = value.reshape(count, tokens)
        if shared is not None:
            whole = jnp.concatenate([whole, shared.reshape(-1, tokens)])
        for axis, order in (("y", (1, 0, 3, 2)), ("p", (2, 3, 0, 1))):
            other = swap(whole, axis)
            order = [4 * i + j for i in range(value.shape[0]) for j in order]
            whole = whole + jnp.concatenate([other[i : i + 1] for i in order] + [other[count:]])
        sums = whole[:count].reshape(value.shape)
        return sums if shared is None else (sums, whole[count:].reshape(-1))

    def sum_over(value, *axes):
        for axis in axes:
            value = axis_sum(value, axis)
        return value

    def hand_on(own, split, sent=None, later=(), last=()):
        pieces = [(own, 0, 0, 0)]
        if split:
            pieces += [(swap(own, "x"), 0, 1, 0)]
        for r in range(1, outer):
            far_piece = hold(lax.ppermute(own if sent is None else sent, "o", beyond[r]), *later)
            pieces += [(far_piece, 0, 0, r)]
            if split:
                pieces += [(hold(swap(far_piece, "x"), *last), 0, 1, r)]
        if split:
            pieces += [(swap(value, "core"), 1, x, o) for value, _, x, o in pieces]
        return pieces

    def fetch_qkv(weight, after):
        rows = weight.shape[0]
        split = (rows // 4) % 16 == 0
        quarter = rows // 4 if split else rows
        if split:
            weight = lax.dynamic_slice_in_dim(weight, (me_x * 2 + core) * quarter, quarter, 0)
        cuts = cut(weight, 3, 4)
        arrived = [to_place(cuts[r], r) for r in (1, 2, 3)]
        pieces = hand_on(hold(jnp.concatenate([cuts[0]] + arrived), after), split)
        plan, places = [], []
        for i, (_, k, x, o) in enumerate(pieces):
            for r in range(4):
                plan.append((i, r * quarter, quarter))
                at = block_index(me_o ^ o, me_c ^ r) * rows
                places.append((at + ((me_x ^ x) * 2 + (core ^ k)) * quarter if split else at, 0))
        whole = assemble([piece[0] for piece in pieces], plan, places, (D, 3 * D // 4))
        return whole, pieces, arrived

    def start_gate_up(weight, start):
        rows = weight.shape[0]
        f = FF // blk

        def piece_of(r):
            cols = []
            for j in range(outer // 2):
                o = me_x * (outer // 2) + j
                at = core * FF + block_index(o, me_c ^ r) * f + start
                cols.append(lax.dynamic_slice(weight, (0, at), (rows, f)))
            return jnp.concatenate(cols, 1) if len(cols) > 1 else cols[0]

        arrived = [to_place(piece_of(r), r) for r in (1, 2, 3)]
        own = jnp.concatenate([piece_of(0)] + arrived)
        return own, arrived

    def fetch_gate_up(own):
        rows, n = own.shape[0] // 4, own.shape[1]
        whole = lax.all_gather(own, ("core", "x", "o"), axis=0, tiled=True)
        plan, places = [], []
        for q in range(4):
            for o in range(outer):
                for r in range(4):
                    plan.append((0, ((q * outer + o) * 4 + r) * rows, rows))
                    places.append((block_index(o, me_c ^ r) * rows, q * n))
        return assemble([whole], plan, places, (D, 2 * FF // 4))

    def fetch_down(weight, after):
        rows, quarter = weight.shape[0], D // 4
        mine = lax.dynamic_slice(weight, (0, (core * 2 + me_x) * quarter), (rows, quarter))
        whole = lax.all_gather(hold(mine, after), ("core", "x", "o"), axis=0, tiled=True)
        plan = [(0, i * rows, rows) for i in range(4 * outer)]
        places = [(o * rows, q * quarter) for q in range(4) for o in range(outer)]
        return assemble([whole], plan, places, (outer * rows, D))

    def fetch_rows(weight, start, after, later):
        rows, quarter = weight.shape[0], D // 4
        mine = lax.dynamic_slice(weight, (0, (core * 2 + me_x) * quarter + start), (rows, quarter))
        pieces = hand_on(mine, True, hold(mine, *after), later)
        plan = [(i, 0, rows) for i in range(len(pieces))]
        places = [((me_o ^ o) * rows, ((core ^ k) * 2 + (me_x ^ x)) * quarter) for _, k, x, o in pieces]
        return assemble([piece[0] for piece in pieces], plan, places, (outer * rows, D)), pieces

    def finish(part, dim):
        return pair_stack(pair_stack(part, "x", dim), "core", dim).astype(F32)

    def two_cores(value):
        return jnp.concatenate([value, swap(value, "core")])

    def two_cores_half(value):
        half = value.shape[1] // 2
        first = core == 0
        a, b = value[:, :half], value[:, half:]
        return jnp.concatenate([jnp.where(first, a, b), swap(jnp.where(first, b, a), "core")])

    def grad_columns(left_both, grad_both):
        half = grad_both.shape[1] // 2
        theirs = lax.dynamic_slice_in_dim(grad_both, (1 - me_x) * half, half, 1)
        mine = lax.dynamic_slice_in_dim(grad_both, me_x * half, half, 1)
        sent = swap(dot(left_both, theirs, ((0,), (0,))).astype(LOW), "x")
        return dot(left_both, mine, ((0,), (0,))) + sent.astype(F32)

    numbers = jnp.concatenate([segments[None], positions]).T.astype(LOW)
    numbers = jnp.pad(numbers, ((0, 0), (0, 128 - numbers.shape[1])))
    mine = mirror(jnp.concatenate([hidden, numbers], 1))
    source = mine[:, :D].astype(F32)
    segment_here = mine[:, D].astype(jnp.int32)
    chosen = jnp.where(dropped[:, None, None] == 1, null_caption[None], captions)
    chosen_rows = chosen.reshape(capt, chosen.shape[2])
    caption_parts = pl.pallas_call(
        functools.partial(caption_kernel, [place_columns(c, 2, outer, rest, lead) for c in range(4)], rest),
        out_shape=jax.ShapeDtypeStruct((4, capt, 2 * width), LOW),
        in_specs=[pl.BlockSpec(memory_space=pltpu.VMEM)] * 2,
        out_specs=pl.BlockSpec(memory_space=pltpu.VMEM),
        compiler_params=pltpu.CompilerParams(vmem_limit_bytes=40 * 1024 * 1024),
        cost_estimate=pl.CostEstimate(
            flops=2 * capt * chosen_rows.shape[1] * 2 * D, bytes_accessed=8 * 1024 * 1024, transcendentals=0
        ),
        name="caption_product",
    )(chosen_rows, caption_weight)
    caption_parts = [lax.dynamic_index_in_dim(caption_parts, me_c ^ r, 0, keepdims=False) for r in range(4)]
    caption_half = scatter_places([caption_parts[0].astype(F32)] + caption_parts[1:])

    qkv_mine, qkv_pieces, qkv_arrived = fetch_qkv(qkv_weight, caption_half)
    tokens_blocks = gather_places(hold(mine, qkv_arrived[2], caption_half))
    tokens_square = jnp.concatenate(tokens_blocks)
    hidden_square = tokens_square[:, :D].astype(F32)
    seg_square = tokens_square[:, D].astype(jnp.int32)
    pos_square = tokens_square[:, D + 1 : D + 4].astype(F32)
    seg_col, seg_row = seg_square[:, None], seg_square[None]
    seg_far = far(seg_row)

    qkv_here = qkv_pieces[2][0] if outer == 2 else qkv_pieces[-1][0]
    late = when(qkv_here)

    cond_rows = ada_weight.shape[0]
    cond_low = lax.dynamic_slice_in_dim(jax.nn.silu(condition), me_b * cond_rows, cond_rows, 1).astype(LOW)
    cond_both = pair_stack(cond_low, "core", 0)
    cond_all = pair_stack(cond_both.reshape(2, 1, CLIPS, cond_rows), "x", 1).reshape(-1, cond_rows)
    modulation = sum_over(hold(dot(cond_both, ada_weight), qkv_here), "o", "y", "p")
    modulation = lax.dynamic_slice_in_dim(modulation, me_g * CLIPS, CLIPS, 0) + ada_bias

    up_own, up_arrived = start_gate_up(gate_up, when(tokens_blocks[3]))
    up_own = hold(up_own, qkv_here)


    head_tanh = jnp.tanh(head_gate)
    (place_gains,) = cut(jnp.concatenate([gains[4:7], jnp.repeat(head_tanh, HEAD)[None]]), 1, 1)
    gain_q, gain_k, gain_c, gate_row = (place_gains[i : i + 1] for i in range(4))

    pair_index = jnp.arange(PAIR) % HEAD // 2
    frequency = 10000.0 ** (-3.0 * (pair_index // 3).astype(F32) / (HEAD // 2))
    select = ((pair_index % 3)[None, :] == jnp.arange(3)[:, None]).astype(F32)
    angles = jnp.dot(pos_square, select, precision=PRECISE) * frequency[None, :]
    cosine = jnp.cos(angles)
    sine = jnp.sin(angles) * jnp.where(jnp.arange(PAIR) % 2 == 0, -1.0, 1.0)[None]

    def per_token(rows, sel):
        return jnp.where(sel, rows[0:1], rows[1:2])

    caption_mine = axis_sum(mirror(hold(caption_half, qkv_here).astype(LOW)).astype(F32), t_axis)
    scale_square = per_token(hold(modulation[:, :D], up_arrived[2], caption_mine, cosine), seg_col == 0)
    first_in = (unit_rows(hidden_square) * gains[0] * (1.0 + scale_square)).astype(LOW)
    projected = dot(first_in, qkv_mine)
    q_raw, k_raw = projected[:, :width], projected[:, width : 2 * width]
    ck_raw = caption_mine[:, :width]
    sums, sums_c = square_sum(
        jnp.stack([jnp.sum(q_raw * q_raw, -1), jnp.sum(k_raw * k_raw, -1)]), jnp.sum(ck_raw * ck_raw, -1)
    )
    outw, out_pieces = fetch_rows(out_weight, late, (), ())
    gate_up_mine = fetch_gate_up(up_own)
    down_mine = fetch_down(down_weight, projected)
    inv = hold(lax.rsqrt(sums / D + EPSILON).T, seg_far, out_pieces[2][0])
    heads_into, heads_out = head_calls(square, width)
    queries, kv = heads_into(projected, projected, projected, inv, gain_q, gain_k, cosine, sine)
    inv_c = lax.rsqrt(sums_c / D + EPSILON)[:, None]
    unit_c = ck_raw * inv_c
    cap_keys = (unit_c * gain_c).astype(LOW)
    cap_values = caption_mine[:, width:].astype(LOW)
    kv_far = far(kv)

    near, away, back_away, back_near = attention_calls(square, width, capt, t_size - 1)
    out_near, out_cross, stats = near(queries, kv, kv, cap_keys, cap_values, seg_col, seg_row)
    out_self, mixed, lse = away(queries, kv_far, kv_far, seg_col, seg_far, out_near, out_cross, stats, gate_row)
    mixed_both = two_cores(mixed)
    attended = scatter_square(dot(mixed, outw))

    clip_here = segment_here[:, None] == 0
    scale_attn = per_token(modulation[:, :D], clip_here)
    gate_attn = jnp.tanh(per_token(modulation[:, D : 2 * D], clip_here))
    scale_ffn = per_token(modulation[:, 2 * D : 3 * D], clip_here)
    gate_ffn = jnp.tanh(per_token(modulation[:, 3 * D :], clip_here))
    attn_unit = unit_rows(attended)
    middle = source + gate_attn * attn_unit * gains[1]
    unit_mid = unit_rows(middle)
    second_low = (unit_mid * gains[2] * (1.0 + scale_ffn)).astype(LOW)
    second_in = gather_square(second_low)
    hidden_units = FF // 4
    gate_values = dot(second_in, gate_up_mine)
    gate_part, up_part = gate_values[:, :hidden_units], gate_values[:, hidden_units:]
    activated = (jax.nn.silu(gate_part) * up_part).astype(LOW)
    activated_both = two_cores(activated)
    lowered = scatter_square(dot(activated, down_mine))
    low_unit = unit_rows(lowered)
    result = middle + gate_ffn * low_unit * gains[3]

    upstream = mirror(cotangent).astype(F32)
    d_gate_ffn = upstream * low_unit * gains[3] * (1.0 - gate_ffn * gate_ffn)
    d_lowered, grad_gain3 = norm_back(upstream * gate_ffn, lowered, gains[3])
    d_lowered_sq = gather_square(d_lowered.astype(LOW))
    d_activated = dot(d_lowered_sq, down_mine, ((1,), (1,)))
    sigmoid = jax.nn.sigmoid(gate_part)
    d_gate_part = d_activated * up_part * sigmoid * (1.0 + gate_part * (1.0 - sigmoid))
    d_up_part = d_activated * gate_part * sigmoid
    d_gate_values = jnp.concatenate([d_gate_part, d_up_part], 1).astype(LOW)
    d_second = scatter_square(dot(d_gate_values, gate_up_mine, ((1,), (1,))))

    down_sum = grad_columns(activated_both, two_cores_half(d_lowered_sq))
    up_terms = grad_product(second_in, d_gate_values, 4)
    up_terms = jnp.stack([row_blocks(up_terms[q]) for q in range(4)]) if lead else up_terms
    up_terms = up_terms.reshape((4 * outer, D // outer) + up_terms.shape[-1:])
    up_rows = lax.psum_scatter(up_terms, ("core", "x", "o"), scatter_dimension=0)
    up_rows = up_rows.reshape(4, gate_up.shape[0], -1)

    d_scale_ffn = d_second * unit_mid * gains[2]
    d_middle_norm, grad_gain2 = norm_back(d_second * (1.0 + scale_ffn), middle, gains[2])
    d_middle = upstream + d_middle_norm
    d_gate_attn = d_middle * attn_unit * gains[1] * (1.0 - gate_attn * gate_attn)
    d_attended, grad_gain1 = norm_back(d_middle * gate_attn, attended, gains[1])

    d_attended_sq = gather_square(d_attended.astype(LOW))
    d_mixed = dot(d_attended_sq, outw, ((1,), (1,))).astype(LOW)
    dq_part, dkv_far, dck, dcv, d_head, delta = back_away(
        queries, d_mixed, out_self, out_cross, lse, stats, gate_row, kv_far, kv_far, cap_keys,
        cap_values, seg_col, seg_far,
    )
    far_terms = [lax.ppermute(dkv_far[r - 1], t_axis, [(i, i ^ r) for i in range(t_size)]) for r in range(1, t_size)]
    d_query, dk_near, dv_near = back_near(queries, d_mixed, lse, delta, kv, kv, seg_col, seg_row, dq_part)
    dkv_other = far_terms[0] if t_size == 2 else sum(term.astype(F32) for term in far_terms)
    d_cap = axis_sum(jnp.concatenate([dck, dcv], 1), t_axis)
    out_sum = grad_columns(mixed_both, two_cores_half(d_attended_sq))
    inner_q, inner_k, head_sums, gain_qk = heads_out(
        d_query, dk_near, dkv_other, projected, projected, inv, gain_q, gain_k, cosine, sine
    )
    inner_c = d_cap[:, :width] * gain_c
    sums, sums_c = square_sum(jnp.sum(head_sums, 0).T, jnp.sum(inner_c * unit_c, -1))
    mean = (sums / D).T
    d_q_raw = inv[:, 0:1] * (inner_q - q_raw * inv[:, 0:1] * mean[:, 0:1])
    d_k_raw = inv[:, 1:2] * (inner_k - k_raw * inv[:, 1:2] * mean[:, 1:2])
    d_value = dv_near + dkv_other[1].astype(F32)
    d_projected = jnp.concatenate([d_q_raw, d_k_raw, d_value], 1).astype(LOW)
    rows_qkv = qkv_weight.shape[0]
    quarter = rows_qkv // 4
    qkv_part = dot(first_in, d_projected, ((0,), (0,))).astype(LOW)
    qkv_part = row_blocks(qkv_part).reshape(outer, 4, 2, 2, quarter, -1)
    qkv_core = swap(lax.dynamic_index_in_dim(qkv_part, 1 - core, 3, keepdims=False), "core")
    qkv_own = lax.dynamic_index_in_dim(qkv_part, core, 3, keepdims=False)
    qkv_part = (qkv_own.astype(F32) + qkv_core.astype(F32)).astype(LOW)
    qkv_x = swap(lax.dynamic_index_in_dim(qkv_part, 1 - me_x, 2, keepdims=False), "x")
    qkv_own = lax.dynamic_index_in_dim(qkv_part, me_x, 2, keepdims=False)
    qkv_part = (qkv_own.astype(F32) + qkv_x.astype(F32)).astype(LOW)
    d_first = scatter_square(dot(hold(d_projected, qkv_core), qkv_mine, ((1,), (1,))))
    after_heads = when(d_projected)
    half_outer = outer // 2
    f = FF // blk
    up_low = jnp.zeros((gate_up.shape[0], 4 * up_rows.shape[2]), LOW)
    for r in range(4):
        piece = lax.dynamic_index_in_dim(up_rows, (me_c ^ r) + after_heads, 0, keepdims=False)
        piece = to_place(piece, r) if r else piece
        for j in range(half_outer):
            up_low = lax.dynamic_update_slice(up_low, piece[:, j * f : (j + 1) * f], (0, (j * 4 + (me_c ^ r)) * f))
    up_half = pair_stack(hold(up_low, qkv_x), "x", 1)
    grad_gate_up = pair_stack(up_half, "core", 1).astype(F32)
    if lead:
        grad_gate_up = unblocks(grad_gate_up.reshape(-1, 2, outer, 4, f)).reshape(gate_up.shape)


    qkv_part = low(outer_reduce(qkv_part))
    qkv_summed = qkv_part
    qkv_part = [
        to_place(lax.dynamic_index_in_dim(qkv_part, me_c ^ r, 0, keepdims=False), r) for r in range(4)
    ]
    qkv_part = lay(qkv_part, 3)
    qkv_part = pair_stack(qkv_part[None], "x", 0)
    qkv_other = swap(qkv_part, "core")
    grad_qkv = jnp.stack([jnp.where(core == i, qkv_part, qkv_other) for i in range(2)], 1)
    grad_qkv = grad_qkv.reshape(rows_qkv, -1).astype(F32)


    d_c_raw = inv_c * (inner_c - unit_c * (sums_c / D)[:, None])
    d_cap_mine = jnp.concatenate([d_c_raw, d_cap[:, width:]], 1).astype(LOW)
    cap_blocks = gather_places(hold(mirror(d_cap_mine), qkv_x))
    d_cap_low = lay(cap_blocks, 2)
    grad_caption = finish(low(grad_columns(two_cores(chosen_rows), two_cores_half(d_cap_low))), 1)
    d_chosen = dot(d_cap_low, caption_weight, ((1,), (1,))).reshape(CLIPS, CAP, -1)
    grad_null = jnp.sum(jnp.where(dropped[:, None, None] == 1, d_chosen, 0.0), 0)
    grad_null = rounded(grad_null) + swap(low(grad_null), "core").astype(F32)
    grad_null = rounded(grad_null) + swap(low(grad_null), "x").astype(F32)

    unit_in = unit_rows(source)
    d_scale_attn = d_first * unit_in * gains[0]
    d_source_norm, grad_gain0 = norm_back(d_first * (1.0 + scale_attn), source, gains[0])
    input_grad = d_middle + d_source_norm
    if mirrored:
        input_grad = jnp.where(core == me_o, input_grad, mirror(input_grad.astype(LOW)).astype(F32))
        result = jnp.where(core == me_o, result, mirror(result.astype(LOW)).astype(F32))

    onehot = (segment_here[:, None] == jnp.arange(CLIPS)[None, :]).astype(F32)

    def per_clip(grad):
        return lax.dot_general(onehot, grad, (((0,), (0,)), ((), ())), precision=PRECISE)

    grad_gain6 = jnp.where(me_t == 0, jnp.sum(d_cap[:, :width] * unit_c, 0), 0.0)
    placed = lay([jnp.concatenate([gain_qk, grad_gain6[None], d_head])], 1)
    small = jnp.concatenate(
        [
            per_clip(d_scale_attn),
            per_clip(d_gate_attn),
            per_clip(d_scale_ffn),
            per_clip(d_gate_ffn),
            grad_gain0[None],
            grad_gain1[None],
            grad_gain2[None],
            grad_gain3[None],
            placed,
        ]
    )
    small = low(hold(sum_over(small, t_axis, "y", "p"), qkv_summed))
    small_x = pair_stack(small[None], "x", 0)
    small = pair_stack(small_x[None], g_axis, 0)
    rows_low = low(
        jnp.concatenate(
            [outer_reduce(v.reshape(outer, -1, D // 4)) for v in (hold(down_sum, qkv_core), hold(out_sum, qkv_core))]
        )
    )

    rows_done = finish(hold(rows_low, small_x), 1)
    grad_down, grad_out = rows_done[: down_weight.shape[0]], rows_done[down_weight.shape[0] :]
    count = 4 * CLIPS
    d_mod = jnp.concatenate([small[:, :, CLIPS * i : CLIPS * (i + 1)] for i in range(4)], -1).reshape(-1, 4 * D)
    grad_ada = dot(cond_all, d_mod, ((0,), (0,)))
    grad_ada_b = jnp.sum(d_mod.astype(F32), 0)
    sums = jnp.sum(small[:, :, count : count + 8].astype(F32), (0, 1))
    grad_gains = sums[:7]
    grad_head = jnp.sum(sums[7].reshape(HEADS, HEAD), -1) * (1.0 - head_tanh * head_tanh)
    return (
        result,
        input_grad,
        grad_ada,
        grad_ada_b,
        grad_qkv,
        grad_out,
        grad_caption,
        grad_gate_up,
        grad_down,
        grad_null,
        grad_gains,
        grad_head,
    )


def solution(mesh):
    devices = mesh.devices
    outer = devices.shape[1] // 4
    lead = (D // devices.shape[1]) % HEAD != 0
    if lead:
        grid = Mesh(devices.reshape(2, 2, 2, 2, outer), ("x", "core", "p", "y", "o"))
        blk = ("p", "y", "o")
    else:
        grid = Mesh(devices.reshape(2, 2, outer, 2, 2), ("x", "core", "o", "p", "y"))
        blk = ("o", "p", "y")
    dp = ("x", "core")
    every = dp + blk
    in_specs = (
        P(every, None),
        P(every),
        P(None, every),
        P(dp, None),
        P(dp, None, blk),
        P(dp),
        P(None, blk),
        P(blk, None),
        P(),
        P(blk, None),
        P(blk, None),
        P(blk, None),
        P(blk, None),
        P(blk, None),
        P(),
        P(),
        P(every, None),
    )
    out_specs = (
        P(every, None),
        P(every, None),
        P(blk, None),
        P(),
        P(blk, None),
        P(blk, None),
        P(blk, None),
        P(blk, None),
        P(blk, None),
        P(None, blk),
        P(),
        P(),
    )
    return jax.shard_map(
        functools.partial(on_device, outer, lead),
        mesh=grid,
        in_specs=in_specs,
        out_specs=out_specs,
        check_vma=False,
    )
```

time: 920 us -> 707 us (0.77)
  waiting for transfers between devices: 324 us -> 228 us
  local copies, waits for them, and re-layouts: 151 us -> 64.9 us
  starting transfers between devices: 216 us -> 150 us
  Pallas kernels: 36.4 us -> 80.9 us
  other arithmetic: 111 us -> 84.3 us
  between operations: 4.55 us -> 30 us
  matrix products: 66.9 us -> 57.6 us
    ppermute x107 -> x52, waiting for transfers between devices: 293 us -> 82.3 us  [swap(): return lax.ppermute(value, axis, SWAP)]
    ppermute x107 -> x52, starting transfers between devices: 198 us -> 79.6 us  [swap(): return lax.ppermute(value, axis, SWAP)]
    ppermute x17 -> x54, waiting for transfers between devices: 31.3 us -> 145 us  [the longest x43 121 us: to_place(): return lax.ppermute(value, ('p', 'y'), across[r])]
    ppermute x17 -> x54, starting transfers between devices: 18.4 us -> 70 us  [the longest x43 45.6 us: to_place(): return lax.ppermute(value, ('p', 'y'), across[r])]
    pallas_call x4 -> x17, Pallas kernels: 36.4 us -> 80.9 us  [the longest x1 13.4 us: grad_product(): pl.pallas_call(product_kernel, grid=(parts, rows // tile), in_specs=[pl.B...]
    dynamic_update_slice x20 -> x4, local copies, waits for them, and re-layouts: 37.8 us -> 1 us  [on_device(): lax.dynamic_update_slice(up_low, piece[:, j * f:(j + 1) * f], (0, (j * 4...]
    select_n x27 -> x11, other arithmetic: 23.4 us -> 3.44 us  [pair_stack(): jnp.where(first, value, other)]
    reshape x8 -> x2, local copies, waits for them, and re-layouts: 17.8 us -> 0.02 us  [square_sum(): whole = value.reshape(count, tokens)]
  transfers between devices with their start and end apart: 124 -> 109, of which waited for: 56 -> 37; matrix products, arithmetic and copies ran while one was open for 32% -> 24% of each run, Pallas kernels for 4% -> 11%
where the time goes in v2:
time: 707 us; the launch traced here: 695 us
  waiting for transfers between devices  228 us (32%)
  starting transfers between devices  150 us (21%)
  other arithmetic  84.3 us (12%)
  Pallas kernels  80.9 us (11%)
  local copies, waits for them, and re-layouts  64.9 us (9%)
  matrix products  57.6 us (8%)
  between operations  30 us (4%)
    ppermute x43, waiting for transfers between devices, to_place(): return lax.ppermute(value, ('p', 'y'), across[r])  121 us
    ppermute x52, waiting for transfers between devices, swap(): return lax.ppermute(value, axis, SWAP)  82.3 us
    ppermute x52, starting transfers between devices, swap(): return lax.ppermute(value, axis, SWAP)  79.6 us
    dot_general x18, matrix products, dot(): return lax.dot_general(a, b, (dims, ((), ())), preferred_element_type=F32)  48.3 us
    ppermute x43, starting transfers between devices, to_place(): return lax.ppermute(value, ('p', 'y'), across[r])  45.6 us
    unnamed x357, local copies, waits for them, and re-layouts  29.6 us
    ppermute x6, starting transfers between devices, mirror(): other = lax.ppermute(value, ('core', 'o'), [(1, 2), (2, 1)])  21.4 us
    ppermute x6, waiting for transfers between devices, mirror(): other = lax.ppermute(value, ('core', 'o'), [(1, 2), (2, 1)])  21 us
  transfers between devices with their start and end apart: 109, of which 37 were waited for; matrix products, arithmetic and copies ran while one was open for 24% of the time, Pallas kernels for 11%

profile of v2, /device:TPU:1, one launch (start us, length us, event | category | flops | bytes accessed | tf_op | source)
XLA Modules:
  0.0 695.0 jit_solution(1279842822544001715)
XLA Ops:
  28.2 8.0 %collective-permute-done.4 = bf16[48,1152]{1,0:T(8,128)(2,1)S(1)} collective-permute-done((bf16[48,1152]{1,0:T(8,128)(2,1)}, bf16[48,1152]{1,0:T(8,128)(2,1)S(1)}, u32[]{:S(2)}, u32[]{:S(2)}) %collective-permute-start.4) | collective-permute-done | bytes 110624 | tf_op jit(solution)/shard_map/ppermute | solution.py:553
  38.6 6.2 collective-permute-start
  49.8 19.4 %collective-permute-done = bf16[128,1664]{1,0:T(8,128)(2,1)S(1)} collective-permute-done((bf16[128,1664]{1,0:T(8,128)(2,1)}, bf16[128,1664]{1,0:T(8,128)(2,1)S(1)}, u32[]{:S(2)}, u32[]{:S(2)}) %collective-permute-start) | collective-permute-done | bytes 426016 | tf_op jit(solution)/shard_map/ppermute | solution.py:546
  71.4 3.3 collective-permute-start.14
  77.0 11.9 %collective-permute-done.14 = bf16[128,1664]{1,0:T(8,128)(2,1)S(1)} collective-permute-done((bf16[128,1664]{1,0:T(8,128)(2,1)S(1)}, bf16[128,1664]{1,0:T(8,128)(2,1)S(1)}, u32[]{:S(2)}, u32[]{:S(2)}) %collective-permute-start.14) | collective-permute-done | bytes 426016 | tf_op jit(solution)/shard_map/ppermute | solution.py:553
  99.5 2.7 sine_multiply_fusion
  106.2 2.8 collective-permute-start.15
  112.6 4.2 collective-permute-start.17
  121.4 6.3 assemble.4
  135.3 5.1 collective-permute-done.41
  156.8 3.0 collective-permute-done.27.refs_2_
  161.0 12.3 %collective-permute-start.30 = (bf16[192,384]{1,0:T(8,128)(2,1)S(1)}, bf16[192,384]{1,0:T(8,128)(2,1)S(1)}, u32[]{:S(2)}, u32[]{:S(2)}) collective-permute-start(bf16[192,384]{1,0:T(8,128)(2,1)S(1)} %collective-permute-done.27.refs_2_), channel_id=1, source_target_pairs={{0,16},{16,0},{1,17},{17,1},{2,18},{18,2},{3,19},{19,3},{4,20},{20... | collective-permute-start | bytes 442376 | tf_op jit(solution)/shard_map/ppermute | solution.py:429
  174.3 4.4 heads_in.1
  195.8 6.2 attn_near.1
  202.0 10.4 %attn_far.1 = (f32[512,384]{1,0:T(8,128)S(1)}, bf16[512,384]{1,0:T(8,128)(2,1)S(1)}, f32[3,512,2]{2,1,0:T(8,128)S(1)}) custom-call(bf16[512,384]{1,0:T(8,128)(2,1)S(1)} %copy-done.6, bf16[1,2,512,384]{3,2,1,0:T(8,128)(2,1)S(1)} %bitcast.184, bf16[1,2,512,384]{3,2,1,0:T(8,128)(2,1)S(1)} %bitcast.185, s32[512,1]{1,0:T(8,128)S(1)} %get-tuple-element.105.sq_ref, ...), custom_call_target="tpu_custom_call" | custom-call | flops 402653184 | bytes 6291456 | tf_op jit(solution)/shard_map/attn_far/pallas_call | solution.py:761
  212.6 2.6 fusion.182
  222.0 5.3 collective-permute-done.35
  227.3 9.4 %collective-permute-done.36 = bf16[128,1536]{1,0:T(8,128)(2,1)} collective-permute-done((bf16[128,1536]{1,0:T(8,128)(2,1)}, bf16[128,1536]{1,0:T(8,128)(2,1)}, u32[]{:S(2)}, u32[]{:S(2)}) %collective-permute-start.36) | collective-permute-done | bytes 393248 | tf_op jit(solution)/shard_map/ppermute | solution.py:553
  236.7 16.6 %collective-permute-done.37 = bf16[128,1536]{1,0:T(8,128)(2,1)} collective-permute-done((bf16[128,1536]{1,0:T(8,128)(2,1)}, bf16[128,1536]{1,0:T(8,128)(2,1)}, u32[]{:S(2)}, u32[]{:S(2)}) %collective-permute-start.37) | collective-permute-done | bytes 393248 | tf_op jit(solution)/shard_map/ppermute | solution.py:553
  260.5 2.6 collective-permute-done.66
  268.4 2.8 copy-done.3
  273.0 4.1 collective-permute-done.40
  277.0 4.9 fusion.161
  284.2 3.0 fusion.183
  290.4 2.9 collective-permute-start.84
  297.1 8.3 %collective-permute-done.45 = bf16[128,1536]{1,0:T(8,128)(2,1)S(1)} collective-permute-done((bf16[128,1536]{1,0:T(8,128)(2,1)S(1)}, bf16[128,1536]{1,0:T(8,128)(2,1)S(1)}, u32[]{:S(2)}, u32[]{:S(2)}) %collective-permute-start.45) | collective-permute-done | bytes 393248 | tf_op jit(solution)/shard_map/ppermute | solution.py:553
  310.6 2.9 pad_maximum_fusion.4.left_ref
  313.5 4.0 collective-permute-start.80
  319.8 4.8 collective-permute-done.50
  324.6 3.5 multiply_convert_fusion.1
  328.1 3.5 fusion.184
  331.6 5.6 collective-permute-start.51
  344.2 6.9 collective-permute-done.53
  358.1 6.7 collective-permute-start.81
  369.0 12.8 %attn_back_far.1 = (f32[512,384]{1,0:T(8,128)S(1)}, bf16[1,2,512,384]{3,2,1,0:T(8,128)(2,1)}, f32[256,384]{1,0:T(8,128)S(1)}, f32[256,384]{1,0:T(8,128)S(1)}, f3...) custom-call(bf16[512,384]{1,0:T(8,128)(2,1)S(1)} %copy-done.6, bf16[512,384]{1,0:T(8,128)(2,1)S(1)} %convolution_convert_fusion.3.g_ref, ...), custom_call_target="tpu_custom_call" | custom-call | flops 1509949440 | bytes 6291456 | tf_op jit(solution)/shard_map/attn_back_far/pallas_call | solution.py:810
  383.5 7.4 %collective-permute-start.58 = (bf16[256,768]{1,0:T(8,128)(2,1)}, bf16[256,768]{1,0:T(8,128)(2,1)}, u32[]{:S(2)}, u32[]{:S(2)}) collective-permute-start(bf16[256,768]{1,0:T(8,128)(2,1)} %fusion.71), channel_id=1, source_target_pairs={{0,8},{8,0},{1,9},{9,1},{2,10},{10,2},{3,11},{11,3},{4,12},{12,4},... | collective-permute-start | bytes 1179656 | tf_op jit(solution)/shard_map/ppermute | solution.py:429
  390.9 13.4 %grad_product.1 = bf16[4,1536,512]{2,1,0:T(8,128)(2,1)} custom-call(bf16[512,1536]{1,0:T(8,128)(2,1)} %pad_maximum_fusion.4.left_ref, bf16[512,2048]{1,0:T(8,128)(2,1)} %pad_maximum_fusion.right_ref), custom_call_target="tpu_custom_call" | custom-call | flops 3221225472 | bytes 9961472 | tf_op jit(solution)/shard_map/grad_product/pallas_call | solution.py:309
  405.6 2.6 fusion.61
  408.2 6.8 attn_back_near.1
  417.6 6.0 heads_back.1
  426.6 2.7 pad_maximum_fusion.6
  444.1 3.8 convolution_convert_fusion.2
  448.0 3.7 collective-permute-start.82
  456.2 2.9 convolution_convert_fusion.4
  466.2 4.1 collective-permute-start.91
  472.2 3.5 fusion.185
  483.5 3.3 add_add_fusion
  488.6 14.9 %collective-permute-done.87 = bf16[192,384]{1,0:T(8,128)(2,1)S(1)} collective-permute-done((bf16[192,384]{1,0:T(8,128)(2,1)S(1)}, bf16[192,384]{1,0:T(8,128)(2,1)S(1)}, u32[]{:S(2)}, u32[]{:S(2)}) %collective-permute-start.87) | collective-permute-done | bytes 147488 | tf_op jit(solution)/shard_map/ppermute | solution.py:429
  505.3 2.9 collective-permute-start.83
  514.3 4.6 collective-permute-start.65
  519.5 10.9 %collective-permute-done.83 = bf16[512,384]{1,0:T(8,128)(2,1)} collective-permute-done((bf16[512,384]{1,0:T(8,128)(2,1)}, bf16[512,384]{1,0:T(8,128)(2,1)}, u32[]{:S(2)}, u32[]{:S(2)}) %collective-permute-start.83) | collective-permute-done | bytes 393248 | tf_op jit(solution)/shard_map/ppermute | solution.py:429
  544.5 4.9 collective-permute-done.92.refs_1_
  549.4 7.0 %collective-permute-done.93.refs_2_ = bf16[256,768]{1,0:T(8,128)(2,1)S(1)} collective-permute-done((bf16[256,768]{1,0:T(8,128)(2,1)S(1)}, bf16[256,768]{1,0:T(8,128)(2,1)S(1)}, u32[]{:S(2)}, u32[]{:S(2)}) %collective-permute-start.93) | collective-permute-done | bytes 393248 | tf_op jit(solution)/shard_map/ppermute | solution.py:553
  557.2 11.5 %collective-permute-done.94.refs_3_ = bf16[256,768]{1,0:T(8,128)(2,1)} collective-permute-done((bf16[256,768]{1,0:T(8,128)(2,1)S(1)}, bf16[256,768]{1,0:T(8,128)(2,1)}, u32[]{:S(2)}, u32[]{:S(2)}) %collective-permute-start.94) | collective-permute-done | bytes 393248 | tf_op jit(solution)/shard_map/ppermute | solution.py:553
  568.6 2.9 lay.5
  595.5 15.1 %collective-permute-done.78 = bf16[1,48,4608]{2,1,0:T(8,128)(2,1)S(1)} collective-permute-done((bf16[1,48,4608]{2,1,0:T(8,128)(2,1)}, bf16[1,48,4608]{2,1,0:T(8,128)(2,1)S(1)}, u32[]{:S(2)}, u32[]{:S(2)}) %collective-permute-start.78) | collective-permute-done | bytes 442400 | tf_op jit(solution)/shard_map/ppermute | solution.py:429
  615.2 2.6 convolution_convert_fusion.1
  623.1 14.1 %collective-permute-done.96 = bf16[512,768]{1,0:T(8,128)(2,1)} collective-permute-done((bf16[512,768]{1,0:T(8,128)(2,1)}, bf16[512,768]{1,0:T(8,128)(2,1)}, u32[]{:S(2)}, u32[]{:S(2)}) %collective-permute-start.96) | collective-permute-done | bytes 786464 | tf_op jit(solution)/shard_map/ppermute | solution.py:429
  645.7 4.6 collective-permute-done.101
  652.1 5.5 collective-permute-done.97
  657.8 3.0 collective-permute-start.98
  660.9 13.6 %collective-permute-done.102 = bf16[192,2048]{1,0:T(8,128)(2,1)S(1)} collective-permute-done((bf16[192,2048]{1,0:T(8,128)(2,1)S(1)}, bf16[192,2048]{1,0:T(8,128)(2,1)S(1)}, u32[]{:S(2)}, u32[]{:S(2)}) %collective-permute-start.102) | collective-permute-done | bytes 786464 | tf_op jit(solution)/shard_map/ppermute | solution.py:429
  680.2 3.5 maximum_convert_fusion
  684.6 3.4 maximum_convert_fusion.1
  (756 shorter events, 260.3 us)
Async XLA Ops:
  7.2 256.6 %all-gather.5.cloned.1.call-start = ((), (), s32[]{:S(2)}) async-start(), calls=%async_computation.2 | async-start | bytes 3538944 | tf_op jit(solution)/shard_map/all_gather | solution.py:648
  13.3 25.3 %collective-permute-start.5 = (bf16[256,768]{1,0:T(8,128)(2,1)}, bf16[256,768]{1,0:T(8,128)(2,1)}, u32[]{:S(2)}, u32[]{:S(2)}) collective-permute-start(bf16[256,768]{1,0:T(8,128)(2,1)} %get-tuple-element.150), channel_id=1, source_target_pairs={{0,1},{1,0},{2,3},{3,2},{4,5},{5,4},{6,7},{7,6},{8,9},{9,8},{10,11... | collective-permute-start | bytes 1179656 | tf_op jit(solution)/shard_map/ppermute | solution.py:553
  15.3 29.5 %collective-permute-start.6 = (bf16[256,768]{1,0:T(8,128)(2,1)}, bf16[256,768]{1,0:T(8,128)(2,1)}, u32[]{:S(2)}, u32[]{:S(2)}) collective-permute-start(bf16[256,768]{1,0:T(8,128)(2,1)} %get-tuple-element.152), channel_id=1, source_target_pairs={{0,2},{1,3},{2,0},{3,1},{4,6},{5,7},{6,4},{7,5},{8,10},{9,11},{10,... | collective-permute-start | bytes 1179656 | tf_op jit(solution)/shard_map/ppermute | solution.py:553
  16.6 28.2 %collective-permute-start.7 = (bf16[256,768]{1,0:T(8,128)(2,1)}, bf16[256,768]{1,0:T(8,128)(2,1)}, u32[]{:S(2)}, u32[]{:S(2)}) collective-permute-start(bf16[256,768]{1,0:T(8,128)(2,1)} %get-tuple-element.151), channel_id=1, source_target_pairs={{0,3},{1,2},{2,1},{3,0},{4,7},{5,6},{6,5},{7,4},{8,11},{9,10},{10,... | collective-permute-start | bytes 1179656 | tf_op jit(solution)/shard_map/ppermute | solution.py:553
  19.4 16.8 %collective-permute-start.4 = (bf16[48,1152]{1,0:T(8,128)(2,1)}, bf16[48,1152]{1,0:T(8,128)(2,1)S(1)}, u32[]{:S(2)}, u32[]{:S(2)}) collective-permute-start(bf16[48,1152]{1,0:T(8,128)(2,1)} %get-tuple-element.40), channel_id=1, source_target_pairs={{0,3},{1,2},{2,1},{3,0},{4,7},{5,6},{6,5},{7,4},{8,11},{9,10},{10,... | collective-permute-start | bytes 331784 | tf_op jit(solution)/shard_map/ppermute | solution.py:553
  27.2 20.5 %collective-permute-start.2 = (bf16[48,1152]{1,0:T(8,128)(2,1)}, bf16[48,1152]{1,0:T(8,128)(2,1)S(1)}, u32[]{:S(2)}, u32[]{:S(2)}) collective-permute-start(bf16[48,1152]{1,0:T(8,128)(2,1)} %get-tuple-element.38), channel_id=1, source_target_pairs={{0,1},{1,0},{2,3},{3,2},{4,5},{5,4},{6,7},{7,6},{8,9},{9,8},{10,11... | collective-permute-start | bytes 331784 | tf_op jit(solution)/shard_map/ppermute | solution.py:553
  38.6 30.6 %collective-permute-start = (bf16[128,1664]{1,0:T(8,128)(2,1)}, bf16[128,1664]{1,0:T(8,128)(2,1)S(1)}, u32[]{:S(2)}, u32[]{:S(2)}) collective-permute-start(bf16[128,1664]{1,0:T(8,128)(2,1)} %fusion.77), channel_id=1, source_target_pairs={{4,8},{8,4},{5,9},{9,5},{6,10},{10,6},{7,11},{11,7},{20,24},{24,20... | collective-permute-start | bytes 1277960 | tf_op jit(solution)/shard_map/ppermute | solution.py:546
  47.8 23.6 %collective-permute-start.8 = (bf16[192,1152]{1,0:T(8,128)(2,1)S(1)}, bf16[192,1152]{1,0:T(8,128)(2,1)S(1)}, u32[]{:S(2)}, u32[]{:S(2)}) collective-permute-start(bf16[192,1152]{1,0:T(8,128)(2,1)S(1)} %maximum_add_fusion.1.refs_0_), channel_id=1, source_target_pairs={{0,4},{4,0},{1,5},{5,1},{2,6},{6,2},{3,7},{7,3},{8,12},{12,8},{9,1... | collective-permute-start | bytes 1327112 | tf_op jit(solution)/shard_map/ppermute | solution.py:592
  47.9 69.0 %collective-permute-start.18 = (bf16[192,1152]{1,0:T(8,128)(2,1)S(1)}, bf16[192,1152]{1,0:T(8,128)(2,1)S(1)}, u32[]{:S(2)}, u32[]{:S(2)}) collective-permute-start(bf16[192,1152]{1,0:T(8,128)(2,1)S(1)} %maximum_add_fusion.1.refs_0_), channel_id=1, source_target_pairs={{0,16},{16,0},{1,17},{17,1},{2,18},{18,2},{3,19},{19,3},{4,20},{20... | collective-permute-start | bytes 1327112 | tf_op jit(solution)/shard_map/ppermute | solution.py:429
  49.1 72.2 %collective-permute-start.20 = (bf16[192,1152]{1,0:T(8,128)(2,1)S(1)}, bf16[192,1152]{1,0:T(8,128)(2,1)S(1)}, u32[]{:S(2)}, u32[]{:S(2)}) collective-permute-start(bf16[192,1152]{1,0:T(8,128)(2,1)S(1)} %maximum_add_fusion.1.refs_0_), channel_id=1, source_target_pairs={{0,8},{8,0},{1,9},{9,1},{2,10},{10,2},{3,11},{11,3},{4,12},{12,4},... | collective-permute-start | bytes 1327112 | tf_op jit(solution)/shard_map/ppermute | solution.py:429
  70.1 22.6 %collective-permute-start.12 = (bf16[128,1664]{1,0:T(8,128)(2,1)S(1)}, bf16[128,1664]{1,0:T(8,128)(2,1)S(1)}, u32[]{:S(2)}, u32[]{:S(2)}) collective-permute-start(bf16[128,1664]{1,0:T(8,128)(2,1)S(1)} %get-tuple-element.106), channel_id=1, source_target_pairs={{0,1},{1,0},{2,3},{3,2},{4,5},{5,4},{6,7},{7,6},{8,9},{9,8},{10,11... | collective-permute-start | bytes 1277960 | tf_op jit(solution)/shard_map/ppermute | solution.py:553
  71.4 21.4 %collective-permute-start.13 = (bf16[128,1664]{1,0:T(8,128)(2,1)S(1)}, bf16[128,1664]{1,0:T(8,128)(2,1)}, u32[]{:S(2)}, u32[]{:S(2)}) collective-permute-start(bf16[128,1664]{1,0:T(8,128)(2,1)S(1)} %get-tuple-element.106), channel_id=1, source_target_pairs={{0,2},{1,3},{2,0},{3,1},{4,6},{5,7},{6,4},{7,5},{8,10},{9,11},{10,... | collective-permute-start | bytes 1277960 | tf_op jit(solution)/shard_map/ppermute | solution.py:553
  71.4 17.5 %collective-permute-start.14 = (bf16[128,1664]{1,0:T(8,128)(2,1)S(1)}, bf16[128,1664]{1,0:T(8,128)(2,1)S(1)}, u32[]{:S(2)}, u32[]{:S(2)}) collective-permute-start(bf16[128,1664]{1,0:T(8,128)(2,1)S(1)} %get-tuple-element.106), channel_id=1, source_target_pairs={{0,3},{1,2},{2,1},{3,0},{4,7},{5,6},{6,5},{7,4},{8,11},{9,10},{10,... | collective-permute-start | bytes 1277960 | tf_op jit(solution)/shard_map/ppermute | solution.py:553
  88.9 20.2 %collective-permute-start.16 = (bf16[256,768]{1,0:T(8,128)(2,1)}, bf16[256,768]{1,0:T(8,128)(2,1)}, u32[]{:S(2)}, u32[]{:S(2)}) collective-permute-start(bf16[256,768]{1,0:T(8,128)(2,1)} %add_convert_fusion), channel_id=1, source_target_pairs={{4,8},{8,4},{5,9},{9,5},{6,10},{10,6},{7,11},{11,7},{20,24},{24,20... | collective-permute-start | bytes 1179656 | tf_op jit(solution)/shard_map/ppermute | solution.py:546
  92.8 25.8 %collective-permute-start.19 = (bf16[192,1152]{1,0:T(8,128)(2,1)S(1)}, bf16[192,1152]{1,0:T(8,128)(2,1)S(1)}, u32[]{:S(2)}, u32[]{:S(2)}) collective-permute-start(bf16[192,1152]{1,0:T(8,128)(2,1)S(1)} %collective-permute-done.8.refs_2_), channel_id=1, source_target_pairs={{0,16},{16,0},{1,17},{17,1},{2,18},{18,2},{3,19},{19,3},{4,20},{20... | collective-permute-start | bytes 1327112 | tf_op jit(solution)/shard_map/ppermute | solution.py:429
  133.4 135.0 %all-gather.3.cloned.1.call-start = ((), (), s32[]{:S(2)}) async-start(), calls=%async_computation.1 | async-start | bytes 7077888 | tf_op jit(solution)/shard_map/all_gather | solution.py:636
  143.7 477.5 %reduce-scatter.2.cloned.1.call-start = ((), (), s32[]{:S(2)}) async-start(), calls=%async_computation.3 | async-start | bytes 7077888 | tf_op jit(solution)/shard_map/reduce_scatter | solution.py:799
  152.2 21.1 %collective-permute-start.25 = (f32[10,128]{1,0:T(8,128)S(1)}, f32[10,128]{1,0:T(8,128)S(1)}, u32[]{:S(2)}, u32[]{:S(2)}) collective-permute-start(f32[10,128]{1,0:T(8,128)S(1)} %fusion.142), channel_id=1, source_target_pairs={{0,2},{2,0},{1,3},{3,1},{4,6},{6,4},{5,7},{7,5},{8,10},{10,8},{9,1... | collective-permute-start | bytes 15368 | tf_op jit(solution)/shard_map/ppermute | solution.py:429
  154.2 26.0 %collective-permute-start.29 = (bf16[192,384]{1,0:T(8,128)(2,1)S(1)}, bf16[192,384]{1,0:T(8,128)(2,1)S(1)}, u32[]{:S(2)}, u32[]{:S(2)}) collective-permute-start(bf16[192,384]{1,0:T(8,128)(2,1)S(1)} %constant_dynamic-slice_fusion.5.refs_0_), channel_id=1, source_target_pairs={{0,16},{16,0},{1,17},{17,1},{2,18},{18,2},{3,19},{19,3},{4,20},{20... | collective-permute-start | bytes 442376 | tf_op jit(solution)/shard_map/ppermute | solution.py:429
  161.0 19.9 %collective-permute-start.30 = (bf16[192,384]{1,0:T(8,128)(2,1)S(1)}, bf16[192,384]{1,0:T(8,128)(2,1)S(1)}, u32[]{:S(2)}, u32[]{:S(2)}) collective-permute-start(bf16[192,384]{1,0:T(8,128)(2,1)S(1)} %collective-permute-done.27.refs_2_), channel_id=1, source_target_pairs={{0,16},{16,0},{1,17},{17,1},{2,18},{18,2},{3,19},{19,3},{4,20},{20... | collective-permute-start | bytes 442376 | tf_op jit(solution)/shard_map/ppermute | solution.py:429
  178.7 23.3 %collective-permute-start.28 = (bf16[2,512,384]{2,1,0:T(8,128)(2,1)}, bf16[2,512,384]{2,1,0:T(8,128)(2,1)S(1)}, u32[]{:S(2)}, u32[]{:S(2)}) collective-permute-start(bf16[2,512,384]{2,1,0:T(8,128)(2,1)} %get-tuple-element.42.k_ref.v_ref), channel_id=1, source_target_pairs={{0,8},{8,0},{1,9},{9,1},{2,10},{10,2},{3,11},{11,3},{4,12},{12,4},... | collective-permute-start | bytes 2359304 | tf_op jit(solution)/shard_map/ppermute | solution.py:550
  217.6 19.1 %collective-permute-start.36 = (bf16[128,1536]{1,0:T(8,128)(2,1)}, bf16[128,1536]{1,0:T(8,128)(2,1)}, u32[]{:S(2)}, u32[]{:S(2)}) collective-permute-start(bf16[128,1536]{1,0:T(8,128)(2,1)} %get-tuple-element.149), channel_id=1, source_target_pairs={{0,2},{1,3},{2,0},{3,1},{4,6},{5,7},{6,4},{7,5},{8,10},{9,11},{10,... | collective-permute-start | bytes 1179656 | tf_op jit(solution)/shard_map/ppermute | solution.py:553
  217.6 35.7 %collective-permute-start.37 = (bf16[128,1536]{1,0:T(8,128)(2,1)}, bf16[128,1536]{1,0:T(8,128)(2,1)}, u32[]{:S(2)}, u32[]{:S(2)}) collective-permute-start(bf16[128,1536]{1,0:T(8,128)(2,1)} %get-tuple-element.148), channel_id=1, source_target_pairs={{0,3},{1,2},{2,1},{3,0},{4,7},{5,6},{6,5},{7,4},{8,11},{9,10},{10,... | collective-permute-start | bytes 1179656 | tf_op jit(solution)/shard_map/ppermute | solution.py:553
  219.0 86.7 %collective-permute-start.47 = (bf16[128,1536]{1,0:T(8,128)(2,1)}, bf16[128,1536]{1,0:T(8,128)(2,1)}, u32[]{:S(2)}, u32[]{:S(2)}) collective-permute-start(bf16[128,1536]{1,0:T(8,128)(2,1)} %param.33), channel_id=1, source_target_pairs={{4,8},{8,4},{5,9},{9,5},{6,10},{10,6},{7,11},{11,7},{20,24},{24,20... | collective-permute-start | bytes 1179656 | tf_op jit(solution)/shard_map/ppermute | solution.py:546
  257.5 15.4 %collective-permute-start.38 = (bf16[128,1536]{1,0:T(8,128)(2,1)}, bf16[128,1536]{1,0:T(8,128)(2,1)}, u32[]{:S(2)}, u32[]{:S(2)}) collective-permute-start(bf16[128,1536]{1,0:T(8,128)(2,1)} %multiply_convert_fusion.7), channel_id=1, source_target_pairs={{0,1},{1,0},{2,3},{3,2},{4,5},{5,4},{6,7},{7,6},{8,9},{9,8},{10,11... | collective-permute-start | bytes 1179656 | tf_op jit(solution)/shard_map/ppermute | solution.py:553
  258.9 14.0 %collective-permute-start.39 = (bf16[128,1536]{1,0:T(8,128)(2,1)}, bf16[128,1536]{1,0:T(8,128)(2,1)}, u32[]{:S(2)}, u32[]{:S(2)}) collective-permute-start(bf16[128,1536]{1,0:T(8,128)(2,1)} %multiply_convert_fusion.7), channel_id=1, source_target_pairs={{0,2},{1,3},{2,0},{3,1},{4,6},{5,7},{6,4},{7,5},{8,10},{9,11},{10,... | collective-permute-start | bytes 1179656 | tf_op jit(solution)/shard_map/ppermute | solution.py:553
  258.9 18.1 %collective-permute-start.40 = (bf16[128,1536]{1,0:T(8,128)(2,1)}, bf16[128,1536]{1,0:T(8,128)(2,1)}, u32[]{:S(2)}, u32[]{:S(2)}) collective-permute-start(bf16[128,1536]{1,0:T(8,128)(2,1)} %multiply_convert_fusion.7), channel_id=1, source_target_pairs={{0,3},{1,2},{2,1},{3,0},{4,7},{5,6},{6,5},{7,4},{8,11},{9,10},{10,... | collective-permute-start | bytes 1179656 | tf_op jit(solution)/shard_map/ppermute | solution.py:553
  289.1 16.3 %collective-permute-start.45 = (bf16[128,1536]{1,0:T(8,128)(2,1)S(1)}, bf16[128,1536]{1,0:T(8,128)(2,1)S(1)}, u32[]{:S(2)}, u32[]{:S(2)}) collective-permute-start(bf16[128,1536]{1,0:T(8,128)(2,1)S(1)} %get-tuple-element.145), channel_id=1, source_target_pairs={{0,3},{1,2},{2,1},{3,0},{4,7},{5,6},{6,5},{7,4},{8,11},{9,10},{10,... | collective-permute-start | bytes 1179656 | tf_op jit(solution)/shard_map/ppermute | solution.py:553
  290.4 20.1 %collective-permute-start.84 = (bf16[512,384]{1,0:T(8,128)(2,1)S(1)}, bf16[512,384]{1,0:T(8,128)(2,1)S(1)}, u32[]{:S(2)}, u32[]{:S(2)}) collective-permute-start(bf16[512,384]{1,0:T(8,128)(2,1)S(1)} %copy-done.19), channel_id=1, source_target_pairs={{0,8},{8,0},{1,9},{9,1},{2,10},{10,2},{3,11},{11,3},{4,12},{12,4},... | collective-permute-start | bytes 1179656 | tf_op jit(solution)/shard_map/ppermute | solution.py:429
  309.8 14.8 %collective-permute-start.50 = (bf16[128,1536]{1,0:T(8,128)(2,1)S(1)}, bf16[128,1536]{1,0:T(8,128)(2,1)S(1)}, u32[]{:S(2)}, u32[]{:S(2)}) collective-permute-start(bf16[128,1536]{1,0:T(8,128)(2,1)S(1)} %get-tuple-element.157), channel_id=1, source_target_pairs={{0,3},{1,2},{2,1},{3,0},{4,7},{5,6},{6,5},{7,4},{8,11},{9,10},{10,... | collective-permute-start | bytes 1179656 | tf_op jit(solution)/shard_map/ppermute | solution.py:553
  313.5 130.6 %collective-permute-start.80 = (bf16[512,1024]{1,0:T(8,128)(2,1)}, bf16[512,1024]{1,0:T(8,128)(2,1)}, u32[]{:S(2)}, u32[]{:S(2)}) collective-permute-start(bf16[512,1024]{1,0:T(8,128)(2,1)} %multiply_convert_fusion.2), channel_id=1, source_target_pairs={{0,8},{8,0},{1,9},{9,1},{2,10},{10,2},{3,11},{11,3},{4,12},{12,4},... | collective-permute-start | bytes 3145736 | tf_op jit(solution)/shard_map/ppermute | solution.py:429
  317.5 23.0 %collective-permute-start.46 = (bf16[128,1536]{1,0:T(8,128)(2,1)S(1)}, bf16[128,1536]{1,0:T(8,128)(2,1)S(1)}, u32[]{:S(2)}, u32[]{:S(2)}) collective-permute-start(bf16[128,1536]{1,0:T(8,128)(2,1)S(1)} %get-tuple-element.158), channel_id=1, source_target_pairs={{4,8},{8,4},{5,9},{9,5},{6,10},{10,6},{7,11},{11,7},{20,24},{24,20... | collective-permute-start | bytes 1179656 | tf_op jit(solution)/shard_map/ppermute | solution.py:546
  337.2 13.9 %collective-permute-start.53 = (bf16[128,1536]{1,0:T(8,128)(2,1)S(1)}, bf16[128,1536]{1,0:T(8,128)(2,1)S(1)}, u32[]{:S(2)}, u32[]{:S(2)}) collective-permute-start(bf16[128,1536]{1,0:T(8,128)(2,1)S(1)} %get-tuple-element.142), channel_id=1, source_target_pairs={{0,3},{1,2},{2,1},{3,0},{4,7},{5,6},{6,5},{7,4},{8,11},{9,10},{10,... | collective-permute-start | bytes 1179656 | tf_op jit(solution)/shard_map/ppermute | solution.py:553
  358.1 86.0 %collective-permute-start.81 = (bf16[512,768]{1,0:T(8,128)(2,1)}, bf16[512,768]{1,0:T(8,128)(2,1)}, u32[]{:S(2)}, u32[]{:S(2)}) collective-permute-start(bf16[512,768]{1,0:T(8,128)(2,1)} %get-tuple-element.134), channel_id=1, source_target_pairs={{0,8},{8,0},{1,9},{9,1},{2,10},{10,2},{3,11},{11,3},{4,12},{12,4},... | collective-permute-start | bytes 2359304 | tf_op jit(solution)/shard_map/ppermute | solution.py:429
  383.5 31.6 %collective-permute-start.58 = (bf16[256,768]{1,0:T(8,128)(2,1)}, bf16[256,768]{1,0:T(8,128)(2,1)}, u32[]{:S(2)}, u32[]{:S(2)}) collective-permute-start(bf16[256,768]{1,0:T(8,128)(2,1)} %fusion.71), channel_id=1, source_target_pairs={{0,8},{8,0},{1,9},{9,1},{2,10},{10,2},{3,11},{11,3},{4,12},{12,4},... | collective-permute-start | bytes 1179656 | tf_op jit(solution)/shard_map/ppermute | solution.py:429
  390.9 26.7 %collective-permute-start.57 = (bf16[2,512,384]{2,1,0:T(8,128)(2,1)}, bf16[2,512,384]{2,1,0:T(8,128)(2,1)}, u32[]{:S(2)}, u32[]{:S(2)}) collective-permute-start(bf16[2,512,384]{2,1,0:T(8,128)(2,1)} %bitcast.72), channel_id=1, source_target_pairs={{0,8},{8,0},{1,9},{9,1},{2,10},{10,2},{3,11},{11,3},{4,12},{12,4},... | collective-permute-start | bytes 2359304 | tf_op jit(solution)/shard_map/ppermute | solution.py:814
  439.7 30.6 %collective-permute-start.61 = (bf16[2,4,2,48,1152]{4,3,1,0,2:T(8,128)(2,1)}, bf16[2,4,2,48,1152]{4,3,1,0,2:T(8,128)(2,1)}, u32[]{:S(2)}, u32[]{:S(2)}) collective-permute-start(bf16[2,4,2,48,1152]{4,3,1,0,2:T(8,128)(2,1)} %bitcast.182), channel_id=1, source_target_pairs={{0,8},{8,0},{1,9},{9,1},{2,10},{10,2},{3,11},{11,3},{4,12},{12,4},... | collective-permute-start | bytes 5308424 | tf_op jit(solution)/shard_map/ppermute | solution.py:429
  442.3 13.0 %collective-permute-start.85 = (bf16[512,768]{1,0:T(8,128)(2,1)S(1)}, bf16[512,768]{1,0:T(8,128)(2,1)S(1)}, u32[]{:S(2)}, u32[]{:S(2)}) collective-permute-start(bf16[512,768]{1,0:T(8,128)(2,1)S(1)} %get-tuple-element.136), channel_id=1, source_target_pairs={{0,8},{8,0},{1,9},{9,1},{2,10},{10,2},{3,11},{11,3},{4,12},{12,4},... | collective-permute-start | bytes 2359304 | tf_op jit(solution)/shard_map/ppermute | solution.py:429
  448.0 34.3 %collective-permute-start.82 = (bf16[1024,384]{1,0:T(8,128)(2,1)}, bf16[1024,384]{1,0:T(8,128)(2,1)}, u32[]{:S(2)}, u32[]{:S(2)}) collective-permute-start(bf16[1024,384]{1,0:T(8,128)(2,1)} %convolution_convert_fusion.2), channel_id=1, source_target_pairs={{0,16},{16,0},{1,17},{17,1},{2,18},{18,2},{3,19},{19,3},{4,20},{20... | collective-permute-start | bytes 2359304 | tf_op jit(solution)/shard_map/ppermute | solution.py:429
  459.1 18.6 %collective-permute-start.86 = (bf16[384,384]{1,0:T(8,128)(2,1)}, bf16[384,384]{1,0:T(8,128)(2,1)}, u32[]{:S(2)}, u32[]{:S(2)}) collective-permute-start(bf16[384,384]{1,0:T(8,128)(2,1)} %convolution_convert_fusion.4), channel_id=1, source_target_pairs={{0,16},{16,0},{1,17},{17,1},{2,18},{18,2},{3,19},{19,3},{4,20},{20... | collective-permute-start | bytes 884744 | tf_op jit(solution)/shard_map/ppermute | solution.py:429
  466.2 71.3 %collective-permute-start.91 = (bf16[256,768]{1,0:T(8,128)(2,1)}, bf16[256,768]{1,0:T(8,128)(2,1)}, u32[]{:S(2)}, u32[]{:S(2)}) collective-permute-start(bf16[256,768]{1,0:T(8,128)(2,1)} %pad_maximum_fusion.17), channel_id=1, source_target_pairs={{4,8},{8,4},{5,9},{9,5},{6,10},{10,6},{7,11},{11,7},{20,24},{24,20... | collective-permute-start | bytes 1179656 | tf_op jit(solution)/shard_map/ppermute | solution.py:546
  475.8 29.5 %collective-permute-start.62 = (bf16[128,1536]{1,0:T(8,128)(2,1)S(1)}, bf16[128,1536]{1,0:T(8,128)(2,1)S(1)}, u32[]{:S(2)}, u32[]{:S(2)}) collective-permute-start(bf16[128,1536]{1,0:T(8,128)(2,1)S(1)} %get-tuple-element.138), channel_id=1, source_target_pairs={{0,1},{1,0},{2,3},{3,2},{4,5},{5,4},{6,7},{7,6},{8,9},{9,8},{10,11... | collective-permute-start | bytes 1179656 | tf_op jit(solution)/shard_map/ppermute | solution.py:553
  476.6 31.6 %collective-permute-start.63 = (bf16[128,1536]{1,0:T(8,128)(2,1)S(1)}, bf16[128,1536]{1,0:T(8,128)(2,1)S(1)}, u32[]{:S(2)}, u32[]{:S(2)}) collective-permute-start(bf16[128,1536]{1,0:T(8,128)(2,1)S(1)} %get-tuple-element.140), channel_id=1, source_target_pairs={{0,2},{1,3},{2,0},{3,1},{4,6},{5,7},{6,4},{7,5},{8,10},{9,11},{10,... | collective-permute-start | bytes 1179656 | tf_op jit(solution)/shard_map/ppermute | solution.py:553
  477.8 31.2 %collective-permute-start.64 = (bf16[128,1536]{1,0:T(8,128)(2,1)S(1)}, bf16[128,1536]{1,0:T(8,128)(2,1)S(1)}, u32[]{:S(2)}, u32[]{:S(2)}) collective-permute-start(bf16[128,1536]{1,0:T(8,128)(2,1)S(1)} %get-tuple-element.139), channel_id=1, source_target_pairs={{0,3},{1,2},{2,1},{3,0},{4,7},{5,6},{6,5},{7,4},{8,11},{9,10},{10,... | collective-permute-start | bytes 1179656 | tf_op jit(solution)/shard_map/ppermute | solution.py:553
  482.2 21.3 %collective-permute-start.87 = (bf16[192,384]{1,0:T(8,128)(2,1)S(1)}, bf16[192,384]{1,0:T(8,128)(2,1)S(1)}, u32[]{:S(2)}, u32[]{:S(2)}) collective-permute-start(bf16[192,384]{1,0:T(8,128)(2,1)S(1)} %fusion.97), channel_id=1, source_target_pairs={{0,4},{4,0},{1,5},{5,1},{2,6},{6,2},{3,7},{7,3},{8,12},{12,8},{9,1... | collective-permute-start | bytes 442376 | tf_op jit(solution)/shard_map/ppermute | solution.py:429
  503.5 32.1 %collective-permute-start.70 = (bf16[2,4,48,1152]{3,2,1,0:T(8,128)(2,1)}, bf16[2,4,48,1152]{3,2,1,0:T(8,128)(2,1)}, u32[]{:S(2)}, u32[]{:S(2)}) collective-permute-start(bf16[2,4,48,1152]{3,2,1,0:T(8,128)(2,1)} %dynamic-slice_bitcast_fusion), channel_id=1, source_target_pairs={{0,16},{16,0},{1,17},{17,1},{2,18},{18,2},{3,19},{19,3},{4,20},{20... | collective-permute-start | bytes 2654216 | tf_op jit(solution)/shard_map/ppermute | solution.py:429
  505.3 25.2 %collective-permute-start.83 = (bf16[512,384]{1,0:T(8,128)(2,1)}, bf16[512,384]{1,0:T(8,128)(2,1)}, u32[]{:S(2)}, u32[]{:S(2)}) collective-permute-start(bf16[512,384]{1,0:T(8,128)(2,1)} %fusion.78), channel_id=1, source_target_pairs={{0,4},{4,0},{1,5},{5,1},{2,6},{6,2},{3,7},{7,3},{8,12},{12,8},{9,1... | collective-permute-start | bytes 1179656 | tf_op jit(solution)/shard_map/ppermute | solution.py:429
  514.3 20.3 %collective-permute-start.65 = (bf16[128,1536]{1,0:T(8,128)(2,1)S(1)}, bf16[128,1536]{1,0:T(8,128)(2,1)S(1)}, u32[]{:S(2)}, u32[]{:S(2)}) collective-permute-start(bf16[128,1536]{1,0:T(8,128)(2,1)S(1)} %get-tuple-element.92), channel_id=1, source_target_pairs={{4,8},{8,4},{5,9},{9,5},{6,10},{10,6},{7,11},{11,7},{20,24},{24,20... | collective-permute-start | bytes 1179656 | tf_op jit(solution)/shard_map/ppermute | solution.py:546
  518.9 13.5 %collective-permute-start.68 = (bf16[16,1536]{1,0:T(8,128)(2,1)S(1)}, bf16[16,1536]{1,0:T(8,128)(2,1)S(1)}, u32[]{:S(2)}, u32[]{:S(2)}) collective-permute-start(bf16[16,1536]{1,0:T(8,128)(2,1)S(1)} %fusion.117), channel_id=1, source_target_pairs={{0,1},{1,0},{2,3},{3,2},{4,5},{5,4},{6,7},{7,6},{8,9},{9,8},{10,11... | collective-permute-start | bytes 147464 | tf_op jit(solution)/shard_map/ppermute | solution.py:429
  533.1 45.3 %collective-permute-start.69 = (bf16[16,1536]{1,0:T(8,128)(2,1)}, bf16[16,1536]{1,0:T(8,128)(2,1)}, u32[]{:S(2)}, u32[]{:S(2)}) collective-permute-start(bf16[16,1536]{1,0:T(8,128)(2,1)} %fusion.109), channel_id=1, source_target_pairs={{0,2},{2,0},{1,3},{3,1},{4,6},{6,4},{5,7},{7,5},{8,10},{10,8},{9,1... | collective-permute-start | bytes 147464 | tf_op jit(solution)/shard_map/ppermute | solution.py:429
  539.4 17.0 %collective-permute-start.93 = (bf16[256,768]{1,0:T(8,128)(2,1)S(1)}, bf16[256,768]{1,0:T(8,128)(2,1)S(1)}, u32[]{:S(2)}, u32[]{:S(2)}) collective-permute-start(bf16[256,768]{1,0:T(8,128)(2,1)S(1)} %select_add_fusion.1.refs_0_), channel_id=1, source_target_pairs={{0,2},{1,3},{2,0},{3,1},{4,6},{5,7},{6,4},{7,5},{8,10},{9,11},{10,... | collective-permute-start | bytes 1179656 | tf_op jit(solution)/shard_map/ppermute | solution.py:553
  539.6 29.1 %collective-permute-start.94 = (bf16[256,768]{1,0:T(8,128)(2,1)S(1)}, bf16[256,768]{1,0:T(8,128)(2,1)}, u32[]{:S(2)}, u32[]{:S(2)}) collective-permute-start(bf16[256,768]{1,0:T(8,128)(2,1)S(1)} %select_add_fusion.1.refs_0_), channel_id=1, source_target_pairs={{0,3},{1,2},{2,1},{3,0},{4,7},{5,6},{6,5},{7,4},{8,11},{9,10},{10,... | collective-permute-start | bytes 1179656 | tf_op jit(solution)/shard_map/ppermute | solution.py:553
  544.5 31.5 %collective-permute-start.71 = (bf16[4,48,1152]{2,1,0:T(8,128)(2,1)}, bf16[4,48,1152]{2,1,0:T(8,128)(2,1)}, u32[]{:S(2)}, u32[]{:S(2)}) collective-permute-start(bf16[4,48,1152]{2,1,0:T(8,128)(2,1)} %dynamic-slice_bitcast_fusion.1), channel_id=1, source_target_pairs={{0,4},{4,0},{1,5},{5,1},{2,6},{6,2},{3,7},{7,3},{8,12},{12,8},{9,1... | collective-permute-start | bytes 1327112 | tf_op jit(solution)/shard_map/ppermute | solution.py:429
  584.0 30.3 %collective-permute-start.90 = (bf16[256,512]{1,0:T(8,128)(2,1)S(1)}, bf16[256,512]{1,0:T(8,128)(2,1)}, u32[]{:S(2)}, u32[]{:S(2)}) collective-permute-start(bf16[256,512]{1,0:T(8,128)(2,1)S(1)} %bitcast.189), channel_id=1, source_target_pairs={{0,8},{8,0},{1,9},{9,1},{2,10},{10,2},{3,11},{11,3},{4,12},{12,4},... | collective-permute-start | bytes 786440 | tf_op jit(solution)/shard_map/ppermute | solution.py:429
  585.4 28.9 %collective-permute-start.95 = (bf16[256,1536]{1,0:T(8,128)(2,1)}, bf16[256,1536]{1,0:T(8,128)(2,1)}, u32[]{:S(2)}, u32[]{:S(2)}) collective-permute-start(bf16[256,1536]{1,0:T(8,128)(2,1)} %get-tuple-element.132), channel_id=1, source_target_pairs={{0,8},{8,0},{1,9},{9,1},{2,10},{10,2},{3,11},{11,3},{4,12},{12,4},... | collective-permute-start | bytes 2359304 | tf_op jit(solution)/shard_map/ppermute | solution.py:429
  585.5 28.5 %collective-permute-start.88 = (bf16[704,384]{1,0:T(8,128)(2,1)S(1)}, bf16[704,384]{1,0:T(8,128)(2,1)S(1)}, u32[]{:S(2)}, u32[]{:S(2)}) collective-permute-start(bf16[704,384]{1,0:T(8,128)(2,1)S(1)} %fusion.76), channel_id=1, source_target_pairs={{0,16},{16,0},{1,17},{17,1},{2,18},{18,2},{3,19},{19,3},{4,20},{20... | collective-permute-start | bytes 1622024 | tf_op jit(solution)/shard_map/ppermute | solution.py:429
  586.8 26.5 %collective-permute-start.105 = (bf16[128,512]{1,0:T(8,128)(2,1)S(1)}, bf16[128,512]{1,0:T(8,128)(2,1)S(1)}, u32[]{:S(2)}, u32[]{:S(2)}) collective-permute-start(bf16[128,512]{1,0:T(8,128)(2,1)S(1)} %fusion.96), channel_id=1, source_target_pairs={{0,16},{16,0},{1,17},{17,1},{2,18},{18,2},{3,19},{19,3},{4,20},{20... | collective-permute-start | bytes 393224 | tf_op jit(solution)/shard_map/ppermute | solution.py:429
  590.9 19.7 %collective-permute-start.78 = (bf16[1,48,4608]{2,1,0:T(8,128)(2,1)}, bf16[1,48,4608]{2,1,0:T(8,128)(2,1)S(1)}, u32[]{:S(2)}, u32[]{:S(2)}) collective-permute-start(bf16[1,48,4608]{2,1,0:T(8,128)(2,1)} %bitcast.204), channel_id=1, source_target_pairs={{0,16},{16,0},{1,17},{17,1},{2,18},{18,2},{3,19},{19,3},{4,20},{20... | collective-permute-start | bytes 1327112 | tf_op jit(solution)/shard_map/ppermute | solution.py:429
  614.3 37.4 %collective-permute-start.89 = (bf16[704,768]{1,0:T(8,128)(2,1)S(1)}, bf16[704,768]{1,0:T(8,128)(2,1)S(1)}, u32[]{:S(2)}, u32[]{:S(2)}) collective-permute-start(bf16[704,768]{1,0:T(8,128)(2,1)S(1)} %pad_maximum_fusion.12), channel_id=1, source_target_pairs={{0,8},{8,0},{1,9},{9,1},{2,10},{10,2},{3,11},{11,3},{4,12},{12,4},... | collective-permute-start | bytes 3244040 | tf_op jit(solution)/shard_map/ppermute | solution.py:429
  617.7 19.5 %collective-permute-start.96 = (bf16[512,768]{1,0:T(8,128)(2,1)}, bf16[512,768]{1,0:T(8,128)(2,1)}, u32[]{:S(2)}, u32[]{:S(2)}) collective-permute-start(bf16[512,768]{1,0:T(8,128)(2,1)} %convolution_convert_fusion.1), channel_id=1, source_target_pairs={{0,16},{16,0},{1,17},{17,1},{2,18},{18,2},{3,19},{19,3},{4,20},{20... | collective-permute-start | bytes 2359304 | tf_op jit(solution)/shard_map/ppermute | solution.py:429
  622.3 20.9 %collective-permute-start.99 = (bf16[192,512]{1,0:T(8,128)(2,1)S(1)}, bf16[192,512]{1,0:T(8,128)(2,1)S(1)}, u32[]{:S(2)}, u32[]{:S(2)}) collective-permute-start(bf16[192,512]{1,0:T(8,128)(2,1)S(1)} %get-tuple-element.162), channel_id=1, source_target_pairs={{0,1},{1,0},{2,3},{3,2},{4,5},{5,4},{6,7},{7,6},{8,9},{9,8},{10,11... | collective-permute-start | bytes 589832 | tf_op jit(solution)/shard_map/ppermute | solution.py:553
  639.3 18.3 %collective-permute-start.97 = (bf16[512,768]{1,0:T(8,128)(2,1)S(1)}, bf16[512,768]{1,0:T(8,128)(2,1)S(1)}, u32[]{:S(2)}, u32[]{:S(2)}) collective-permute-start(bf16[512,768]{1,0:T(8,128)(2,1)S(1)} %reduce-precision_convert_fusion), channel_id=1, source_target_pairs={{0,16},{16,0},{1,17},{17,1},{2,18},{18,2},{3,19},{19,3},{4,20},{20... | collective-permute-start | bytes 2359304 | tf_op jit(solution)/shard_map/ppermute | solution.py:429
  650.4 24.1 %collective-permute-start.102 = (bf16[192,2048]{1,0:T(8,128)(2,1)S(1)}, bf16[192,2048]{1,0:T(8,128)(2,1)S(1)}, u32[]{:S(2)}, u32[]{:S(2)}) collective-permute-start(bf16[192,2048]{1,0:T(8,128)(2,1)S(1)} %broadcast_add_fusion), channel_id=1, source_target_pairs={{0,16},{16,0},{1,17},{17,1},{2,18},{18,2},{3,19},{19,3},{4,20},{20... | collective-permute-start | bytes 2359304 | tf_op jit(solution)/shard_map/ppermute | solution.py:429
  657.8 21.9 %collective-permute-start.98 = (bf16[512,1536]{1,0:T(8,128)(2,1)S(1)}, bf16[512,1536]{1,0:T(8,128)(2,1)S(1)}, u32[]{:S(2)}, u32[]{:S(2)}) collective-permute-start(bf16[512,1536]{1,0:T(8,128)(2,1)S(1)} %pad_maximum_fusion.7), channel_id=1, source_target_pairs={{0,8},{8,0},{1,9},{9,1},{2,10},{10,2},{3,11},{11,3},{4,12},{12,4},... | collective-permute-start | bytes 4718600 | tf_op jit(solution)/shard_map/ppermute | solution.py:429
  (223 other events, 2414.4 us)
Sparse Core Ops, SparseCore 0:
  133.5 45.5 all-gather.4
  181.6 80.2 all-gather.2
  404.5 97.0 reduce-scatter.1

commit v3 on v2

--- a/solution.py
+++ b/solution.py
@@ -435,19 +435,8 @@
     return jnp.concatenate([jnp.where(first, value, other), jnp.where(first, other, value)], dim)
 
 
-def first_of(value):
-    return value[(0,) * value.ndim].astype(F32)
-
-
-def when(value):
-    probe = first_of(value)
-    return jnp.where(probe != probe, 1, 0)
-
-
 def hold(value, *after):
-    for other in after:
-        value = value + (first_of(other) * 0.0).astype(value.dtype)
-    return value
+    return lax.optimization_barrier((value, after))[0]
 
 
 def on_device(
@@ -584,17 +573,19 @@
             value = axis_sum(value, axis)
         return value
 
-    def hand_on(own, split, sent=None, later=(), last=()):
+    def hand_on(own, split):
         pieces = [(own, 0, 0, 0)]
         if split:
             pieces += [(swap(own, "x"), 0, 1, 0)]
         for r in range(1, outer):
-            far_piece = hold(lax.ppermute(own if sent is None else sent, "o", beyond[r]), *later)
+            far_piece = lax.ppermute(own, "o", beyond[r])
             pieces += [(far_piece, 0, 0, r)]
             if split:
-                pieces += [(hold(swap(far_piece, "x"), *last), 0, 1, r)]
+                pieces += [(swap(far_piece, "x"), 0, 1, r)]
         if split:
-            pieces += [(swap(value, "core"), 1, x, o) for value, _, x, o in pieces]
+            other = swap(jnp.concatenate([piece[0] for piece in pieces]), "core")
+            size = own.shape[0]
+            pieces += [(other[i * size : (i + 1) * size], 1, x, o) for i, (_, _, x, o) in enumerate(pieces)]
         return pieces
 
     def fetch_qkv(weight, after):
@@ -615,7 +606,7 @@
         whole = assemble([piece[0] for piece in pieces], plan, places, (D, 3 * D // 4))
         return whole, pieces, arrived
 
-    def start_gate_up(weight, start):
+    def start_gate_up(weight):
         rows = weight.shape[0]
         f = FF // blk
 
@@ -623,7 +614,7 @@
             cols = []
             for j in range(outer // 2):
                 o = me_x * (outer // 2) + j
-                at = core * FF + block_index(o, me_c ^ r) * f + start
+                at = core * FF + block_index(o, me_c ^ r) * f
                 cols.append(lax.dynamic_slice(weight, (0, at), (rows, f)))
             return jnp.concatenate(cols, 1) if len(cols) > 1 else cols[0]
 
@@ -650,10 +641,10 @@
         places = [(o * rows, q * quarter) for q in range(4) for o in range(outer)]
         return assemble([whole], plan, places, (outer * rows, D))
 
-    def fetch_rows(weight, start, after, later):
+    def fetch_rows(weight):
         rows, quarter = weight.shape[0], D // 4
-        mine = lax.dynamic_slice(weight, (0, (core * 2 + me_x) * quarter + start), (rows, quarter))
-        pieces = hand_on(mine, True, hold(mine, *after), later)
+        mine = lax.dynamic_slice(weight, (0, (core * 2 + me_x) * quarter), (rows, quarter))
+        pieces = hand_on(mine, True)
         plan = [(i, 0, rows) for i in range(len(pieces))]
         places = [((me_o ^ o) * rows, ((core ^ k) * 2 + (me_x ^ x)) * quarter) for _, k, x, o in pieces]
         return assemble([piece[0] for piece in pieces], plan, places, (outer * rows, D)), pieces
@@ -698,8 +689,14 @@
     caption_parts = [lax.dynamic_index_in_dim(caption_parts, me_c ^ r, 0, keepdims=False) for r in range(4)]
     caption_half = scatter_places([caption_parts[0].astype(F32)] + caption_parts[1:])
 
+    cond_rows = ada_weight.shape[0]
+    cond_low = lax.dynamic_slice_in_dim(jax.nn.silu(condition), me_b * cond_rows, cond_rows, 1).astype(LOW)
+    cond_both = pair_stack(cond_low, "core", 0)
+    cond_all = pair_stack(cond_both.reshape(2, 1, CLIPS, cond_rows), "x", 1).reshape(-1, cond_rows)
+    modulation = sum_over(dot(cond_both, ada_weight), "o", "y", "p")
+    modulation = lax.dynamic_slice_in_dim(modulation, me_g * CLIPS, CLIPS, 0) + ada_bias
     qkv_mine, qkv_pieces, qkv_arrived = fetch_qkv(qkv_weight, caption_half)
-    tokens_blocks = gather_places(hold(mine, qkv_arrived[2], caption_half))
+    tokens_blocks = gather_places(hold(mine, qkv_arrived, modulation))
     tokens_square = jnp.concatenate(tokens_blocks)
     hidden_square = tokens_square[:, :D].astype(F32)
     seg_square = tokens_square[:, D].astype(jnp.int32)
@@ -708,16 +705,9 @@
     seg_far = far(seg_row)
 
     qkv_here = qkv_pieces[2][0] if outer == 2 else qkv_pieces[-1][0]
-    late = when(qkv_here)
-
-    cond_rows = ada_weight.shape[0]
-    cond_low = lax.dynamic_slice_in_dim(jax.nn.silu(condition), me_b * cond_rows, cond_rows, 1).astype(LOW)
-    cond_both = pair_stack(cond_low, "core", 0)
-    cond_all = pair_stack(cond_both.reshape(2, 1, CLIPS, cond_rows), "x", 1).reshape(-1, cond_rows)
-    modulation = sum_over(hold(dot(cond_both, ada_weight), qkv_here), "o", "y", "p")
-    modulation = lax.dynamic_slice_in_dim(modulation, me_g * CLIPS, CLIPS, 0) + ada_bias
-
-    up_own, up_arrived = start_gate_up(gate_up, when(tokens_blocks[3]))
+
+
+    up_own, up_arrived = start_gate_up(hold(gate_up, tokens_blocks[3]))
     up_own = hold(up_own, qkv_here)
 
 
@@ -736,7 +726,7 @@
         return jnp.where(sel, rows[0:1], rows[1:2])
 
     caption_mine = axis_sum(mirror(hold(caption_half, qkv_here).astype(LOW)).astype(F32), t_axis)
-    scale_square = per_token(hold(modulation[:, :D], up_arrived[2], caption_mine, cosine), seg_col == 0)
+    scale_square = per_token(hold(modulation[:, :D], up_arrived, caption_mine, cosine), seg_col == 0)
     first_in = (unit_rows(hidden_square) * gains[0] * (1.0 + scale_square)).astype(LOW)
     projected = dot(first_in, qkv_mine)
     q_raw, k_raw = projected[:, :width], projected[:, width : 2 * width]
@@ -744,7 +734,7 @@
     sums, sums_c = square_sum(
         jnp.stack([jnp.sum(q_raw * q_raw, -1), jnp.sum(k_raw * k_raw, -1)]), jnp.sum(ck_raw * ck_raw, -1)
     )
-    outw, out_pieces = fetch_rows(out_weight, late, (), ())
+    outw, out_pieces = fetch_rows(hold(out_weight, qkv_here))
     gate_up_mine = fetch_gate_up(up_own)
     down_mine = fetch_down(down_weight, projected)
     inv = hold(lax.rsqrt(sums / D + EPSILON).T, seg_far, out_pieces[2][0])
@@ -837,12 +827,12 @@
     qkv_own = lax.dynamic_index_in_dim(qkv_part, me_x, 2, keepdims=False)
     qkv_part = (qkv_own.astype(F32) + qkv_x.astype(F32)).astype(LOW)
     d_first = scatter_square(dot(hold(d_projected, qkv_core), qkv_mine, ((1,), (1,))))
-    after_heads = when(d_projected)
+    up_rows = hold(up_rows, d_projected)
     half_outer = outer // 2
     f = FF // blk
     up_low = jnp.zeros((gate_up.shape[0], 4 * up_rows.shape[2]), LOW)
     for r in range(4):
-        piece = lax.dynamic_index_in_dim(up_rows, (me_c ^ r) + after_heads, 0, keepdims=False)
+        piece = lax.dynamic_index_in_dim(up_rows, me_c ^ r, 0, keepdims=False)
         piece = to_place(piece, r) if r else piece
         for j in range(half_outer):
             up_low = lax.dynamic_update_slice(up_low, piece[:, j * f : (j + 1) * f], (0, (j * 4 + (me_c ^ r)) * f))

time: 707 us -> 639 us (0.904)
  local copies, waits for them, and re-layouts: 64.9 us -> 42.3 us
  starting transfers between devices: 150 us -> 134 us
  between operations: 30 us -> 17.1 us
  other arithmetic: 84.3 us -> 76.3 us
    ppermute x43, waiting for transfers between devices: 121 us -> 87.8 us  [to_place(): return lax.ppermute(value, ('p', 'y'), across[r])]
    all_gather x1, waiting for transfers between devices: 0.01 us -> 20.1 us  [fetch_gate_up(): whole = lax.all_gather(own, ('core', 'x', 'o'), axis=0, tiled=True)]
    ppermute x2, waiting for transfers between devices: 3.02 us -> 23 us  [hand_on(): far_piece = lax.ppermute(own, 'o', beyond[r])]
    ppermute x52 -> x46, starting transfers between devices: 79.6 us -> 65 us  [swap(): return lax.ppermute(value, axis, SWAP)]
    unnamed x357 -> x306, local copies, waits for them, and re-layouts: 29.6 us -> 17.5 us
    slice x15 -> x4, local copies, waits for them, and re-layouts: 9.85 us -> 0.2 us  [the longest x2 0.2 us: hand_on(): other[i * size:(i + 1) * size]]
    ppermute x52 -> x46, waiting for transfers between devices: 82.3 us -> 76.9 us  [swap(): return lax.ppermute(value, axis, SWAP)]
  transfers between devices with their start and end apart: 109 -> 103, of which waited for: 37 -> 36; matrix products, arithmetic and copies ran while one was open for 24% -> 23% of each run, Pallas kernels for 11% -> 11%
where the time goes in v3:
time: 639 us; the launch traced here: 629 us
  waiting for transfers between devices  225 us (35%)
  starting transfers between devices  134 us (21%)
  Pallas kernels  79.6 us (12%)
  other arithmetic  76.3 us (12%)
  matrix products  55.2 us (9%)
  local copies, waits for them, and re-layouts  42.3 us (7%)
  between operations  17.1 us (3%)
    ppermute x43, waiting for transfers between devices, to_place(): return lax.ppermute(value, ('p', 'y'), across[r])  87.8 us
    ppermute x46, waiting for transfers between devices, swap(): return lax.ppermute(value, axis, SWAP)  76.9 us
    ppermute x46, starting transfers between devices, swap(): return lax.ppermute(value, axis, SWAP)  65 us
    dot_general x18, matrix products, dot(): return lax.dot_general(a, b, (dims, ((), ())), preferred_element_type=F32)  50.1 us
    ppermute x43, starting transfers between devices, to_place(): return lax.ppermute(value, ('p', 'y'), across[r])  39.6 us
    ppermute x6, starting transfers between devices, mirror(): other = lax.ppermute(value, ('core', 'o'), [(1, 2), (2, 1)])  25 us
    ppermute x2, waiting for transfers between devices, hand_on(): far_piece = lax.ppermute(own, 'o', beyond[r])  23 us
    all_gather x1, waiting for transfers between devices, fetch_gate_up(): whole = lax.all_gather(own, ('core', 'x', 'o'), axis=0, tiled=True)  20.1 us
  transfers between devices with their start and end apart: 103, of which 36 were waited for; matrix products, arithmetic and copies ran while one was open for 23% of the time, Pallas kernels for 11%

profile of v3, /device:TPU:1, one launch (start us, length us, event | category | flops | bytes accessed | tf_op | source)
XLA Modules:
  0.0 629.3 jit_solution(14242811182052157236)
XLA Ops:
  25.6 2.8 collective-permute-start.2
  36.3 6.8 %collective-permute-start = (bf16[128,1664]{1,0:T(8,128)(2,1)S(1)}, bf16[128,1664]{1,0:T(8,128)(2,1)S(1)}, u32[]{:S(2)}, u32[]{:S(2)}) collective-permute-start(bf16[128,1664]{1,0:T(8,128)(2,1)S(1)} %fusion.70), channel_id=1, source_target_pairs={{4,8},{8,4},{5,9},{9,5},{6,10},{10,6},{7,11},{11,7},{20,24},{24,20... | collective-permute-start | bytes 1277960 | tf_op jit(solution)/shard_map/ppermute | solution.py:535
  44.9 8.2 %collective-permute-done.4 = bf16[4,6144]{1,0:T(4,128)(2,1)S(1)} collective-permute-done((bf16[4,6144]{1,0:T(4,128)(2,1)S(1)}, bf16[4,6144]{1,0:T(4,128)(2,1)S(1)}, u32[]{:S(2)}, u32[]{:S(2)}) %collective-permute-start.4) | collective-permute-done | bytes 49184 | tf_op jit(solution)/shard_map/ppermute | solution.py:429
  61.1 14.2 %collective-permute-done.17.refs_2_ = bf16[192,1152]{1,0:T(8,128)(2,1)S(1)} collective-permute-done((bf16[192,1152]{1,0:T(8,128)(2,1)S(1)}, bf16[192,1152]{1,0:T(8,128)(2,1)S(1)}, u32[]{:S(2)}, u32[]{:S(2)}) %collective-permute-start.17) | collective-permute-done | bytes 442400 | tf_op jit(solution)/shard_map/ppermute | solution.py:581
  76.8 6.0 collective-permute-start.18
  89.8 6.4 %collective-permute-start.22 = (bf16[768,1152]{1,0:T(8,128)(2,1)S(1)}, bf16[768,1152]{1,0:T(8,128)(2,1)S(1)}, u32[]{:S(2)}, u32[]{:S(2)}) collective-permute-start(bf16[768,1152]{1,0:T(8,128)(2,1)S(1)} %pad_maximum_fusion.2), channel_id=1, source_target_pairs={{0,8},{8,0},{1,9},{9,1},{2,10},{10,2},{3,11},{11,3},{4,12},{12,4},... | collective-permute-start | bytes 5308424 | tf_op jit(solution)/shard_map/ppermute | solution.py:429
  101.7 6.3 assemble.4
  123.4 3.3 collective-permute-start.25
  126.7 8.8 %collective-permute-done.26.refs_2_ = bf16[192,384]{1,0:T(8,128)(2,1)S(1)} collective-permute-done((bf16[192,384]{1,0:T(8,128)(2,1)S(1)}, bf16[192,384]{1,0:T(8,128)(2,1)S(1)}, u32[]{:S(2)}, u32[]{:S(2)}) %collective-permute-start.26) | collective-permute-done | bytes 147488 | tf_op jit(solution)/shard_map/ppermute | solution.py:581
  135.7 3.8 collective-permute-done.29.refs_3_
  139.6 3.0 collective-permute-start.30
  143.6 4.4 heads_in.1
  152.1 6.2 attn_near.1
  158.4 10.5 %attn_far.1 = (f32[512,384]{1,0:T(8,128)S(1)}, bf16[512,384]{1,0:T(8,128)(2,1)S(1)}, f32[3,512,2]{2,1,0:T(8,128)S(1)}) custom-call(bf16[512,384]{1,0:T(8,128)(2,1)S(1)} %copy-done.6, bf16[1,2,512,384]{3,2,1,0:T(8,128)(2,1)S(1)} %bitcast.169, bf16[1,2,512,384]{3,2,1,0:T(8,128)(2,1)S(1)} %bitcast.170, s32[512,1]{1,0:T(8,128)S(1)} %slice_convert_fusion.2.sq_ref, ...), custom_call_target="tpu_custom_call" | custom-call | flops 402653184 | bytes 6291456 | tf_op jit(solution)/shard_map/attn_far/pallas_call | solution.py:751
  168.9 2.6 fusion.163
  175.2 3.3 collective-permute-start.41
  180.2 2.9 collective-permute-done.31
  183.1 9.6 %collective-permute-done.32 = bf16[128,1536]{1,0:T(8,128)(2,1)} collective-permute-done((bf16[128,1536]{1,0:T(8,128)(2,1)}, bf16[128,1536]{1,0:T(8,128)(2,1)}, u32[]{:S(2)}, u32[]{:S(2)}) %collective-permute-start.32) | collective-permute-done | bytes 393248 | tf_op jit(solution)/shard_map/ppermute | solution.py:542
  192.7 13.4 %collective-permute-done.33 = bf16[128,1536]{1,0:T(8,128)(2,1)} collective-permute-done((bf16[128,1536]{1,0:T(8,128)(2,1)S(1)}, bf16[128,1536]{1,0:T(8,128)(2,1)}, u32[]{:S(2)}, u32[]{:S(2)}) %collective-permute-start.33) | collective-permute-done | bytes 393248 | tf_op jit(solution)/shard_map/ppermute | solution.py:542
  221.3 20.1 %all-gather.3.cloned.1.call-done.refs_0_ = bf16[6144,512]{1,0:T(8,128)(2,1)} async-done(((bf16[768,512]{1,0:T(8,128)(2,1)}), bf16[6144,512]{1,0:T(8,128)(2,1)}) %all-gather.3.cloned.1.call-update) | async-done | bytes 6291472 | tf_op jit(solution)/shard_map/all_gather | solution.py:627
  241.3 2.8 copy-done.3
  247.5 4.9 fusion.141
  254.7 3.0 fusion.164
  262.2 4.9 collective-permute-done.37
  267.1 9.3 %collective-permute-done.39 = bf16[128,1536]{1,0:T(8,128)(2,1)S(1)} collective-permute-done((bf16[128,1536]{1,0:T(8,128)(2,1)S(1)}, bf16[128,1536]{1,0:T(8,128)(2,1)S(1)}, u32[]{:S(2)}, u32[]{:S(2)}) %collective-permute-start.39) | collective-permute-done | bytes 393248 | tf_op jit(solution)/shard_map/ppermute | solution.py:542
  285.1 3.4 collective-permute-start.74
  291.4 10.1 %collective-permute-done.44 = bf16[128,1536]{1,0:T(8,128)(2,1)S(1)} collective-permute-done((bf16[128,1536]{1,0:T(8,128)(2,1)S(1)}, bf16[128,1536]{1,0:T(8,128)(2,1)S(1)}, u32[]{:S(2)}, u32[]{:S(2)}) %collective-permute-start.44) | collective-permute-done | bytes 393248 | tf_op jit(solution)/shard_map/ppermute | solution.py:542
  301.5 3.5 multiply_convert_fusion.1
  305.0 5.1 fusion.165
  312.7 2.6 collective-permute-start.47
  315.3 13.4 %grad_product.1 = bf16[4,1536,512]{2,1,0:T(8,128)(2,1)} custom-call(bf16[512,1536]{1,0:T(8,128)(2,1)} %pad_maximum_fusion.4.left_ref, bf16[512,2048]{1,0:T(8,128)(2,1)} %pad_maximum_fusion.right_ref), custom_call_target="tpu_custom_call" | custom-call | flops 3221225472 | bytes 9961472 | tf_op jit(solution)/shard_map/grad_product/pallas_call | solution.py:309
  330.4 4.6 collective-permute-start.75
  335.1 3.5 multiply_reduce_fusion.1
  344.5 4.9 collective-permute-done.48
  349.4 10.5 %collective-permute-done.50 = bf16[128,1536]{1,0:T(8,128)(2,1)S(1)} collective-permute-done((bf16[128,1536]{1,0:T(8,128)(2,1)S(1)}, bf16[128,1536]{1,0:T(8,128)(2,1)S(1)}, u32[]{:S(2)}, u32[]{:S(2)}) %collective-permute-start.50) | collective-permute-done | bytes 393248 | tf_op jit(solution)/shard_map/ppermute | solution.py:542
  360.9 12.5 %attn_back_far.1 = (f32[512,384]{1,0:T(8,128)S(1)}, bf16[1,2,512,384]{3,2,1,0:T(8,128)(2,1)S(1)}, f32[256,384]{1,0:T(8,128)S(1)}, f32[256,384]{1,0:T(8,128)S(1)}...) custom-call(bf16[512,384]{1,0:T(8,128)(2,1)S(1)} %copy-done.6, bf16[512,384]{1,0:T(8,128)(2,1)S(1)} %convolution_convert_fusion.3.g_ref, ...), custom_call_target="tpu_custom_call" | custom-call | flops 1509949440 | bytes 6291456 | tf_op jit(solution)/shard_map/attn_back_far/pallas_call | solution.py:800
  373.5 3.2 collective-permute-start.52
  376.8 4.0 convolution_convert_fusion.2
  382.7 6.8 %attn_back_near.1 = (f32[512,384]{1,0:T(8,128)S(1)}, f32[512,384]{1,0:T(8,128)S(1)}, f32[512,384]{1,0:T(8,128)S(1)}) custom-call(bf16[512,384]{1,0:T(8,128)(2,1)S(1)} %copy-done.6, bf16[512,384]{1,0:T(8,128)(2,1)S(1)} %convolution_convert_fusion.3.g_ref, f32[3,512,2]{2,1,0:T(8,128)S(1)} %copy-done.9, f32[3,512,2]{2,1,0:T(8,128)S(1)} %get-tuple-element.75.delta_ref, ...), custom_call_target="tpu_custom_call" | custom-call | flops 1006632960 | bytes 6291456 | tf_op jit(solution)/shard_map/attn_back_near/pallas_call | solution.py:805
  392.4 5.3 heads_back.1
  402.2 3.3 collective-permute-start.54
  405.5 2.7 convolution_convert_fusion.4
  419.0 3.3 convert_add_fusion.2
  427.8 9.4 %collective-permute-done.85 = bf16[256,768]{1,0:T(8,128)(2,1)S(1)} collective-permute-done((bf16[256,768]{1,0:T(8,128)(2,1)S(1)}, bf16[256,768]{1,0:T(8,128)(2,1)S(1)}, u32[]{:S(2)}, u32[]{:S(2)}) %collective-permute-start.85) | collective-permute-done | bytes 393248 | tf_op jit(solution)/shard_map/ppermute | solution.py:535
  447.3 9.7 %collective-permute-done.81 = bf16[192,384]{1,0:T(8,128)(2,1)S(1)} collective-permute-done((bf16[192,384]{1,0:T(8,128)(2,1)S(1)}, bf16[192,384]{1,0:T(8,128)(2,1)S(1)}, u32[]{:S(2)}, u32[]{:S(2)}) %collective-permute-start.81) | collective-permute-done | bytes 147488 | tf_op jit(solution)/shard_map/ppermute | solution.py:429
  457.0 3.2 collective-permute-start.77
  461.7 9.8 %collective-permute-done.77 = bf16[512,384]{1,0:T(8,128)(2,1)} collective-permute-done((bf16[512,384]{1,0:T(8,128)(2,1)}, bf16[512,384]{1,0:T(8,128)(2,1)}, u32[]{:S(2)}, u32[]{:S(2)}) %collective-permute-start.77) | collective-permute-done | bytes 393248 | tf_op jit(solution)/shard_map/ppermute | solution.py:429
  478.2 4.5 collective-permute-start.59
  483.4 8.0 %collective-permute-done.59 = bf16[128,1536]{1,0:T(8,128)(2,1)S(1)} collective-permute-done((bf16[128,1536]{1,0:T(8,128)(2,1)S(1)}, bf16[128,1536]{1,0:T(8,128)(2,1)S(1)}, u32[]{:S(2)}, u32[]{:S(2)}) %collective-permute-start.59) | collective-permute-done | bytes 393248 | tf_op jit(solution)/shard_map/ppermute | solution.py:535
  493.4 2.9 collective-permute-start.87
  503.1 3.1 collective-permute-done.87.refs_2_
  507.0 5.5 collective-permute-done.88.refs_3_
  512.5 2.9 lay.5
  527.1 3.3 collective-permute-start.84
  541.8 3.6 collective-permute-done.72
  547.4 3.1 collective-permute-start.73
  550.6 2.7 convolution_convert_fusion.1
  559.7 13.1 %collective-permute-done.90 = bf16[512,768]{1,0:T(8,128)(2,1)} collective-permute-done((bf16[512,768]{1,0:T(8,128)(2,1)}, bf16[512,768]{1,0:T(8,128)(2,1)}, u32[]{:S(2)}, u32[]{:S(2)}) %collective-permute-start.90) | collective-permute-done | bytes 786464 | tf_op jit(solution)/shard_map/ppermute | solution.py:429
  581.0 4.5 collective-permute-done.95
  587.3 5.7 collective-permute-done.91
  593.3 3.0 collective-permute-start.92
  596.3 13.6 %collective-permute-done.96 = bf16[192,2048]{1,0:T(8,128)(2,1)S(1)} collective-permute-done((bf16[192,2048]{1,0:T(8,128)(2,1)S(1)}, bf16[192,2048]{1,0:T(8,128)(2,1)S(1)}, u32[]{:S(2)}, u32[]{:S(2)}) %collective-permute-start.96) | collective-permute-done | bytes 786464 | tf_op jit(solution)/shard_map/ppermute | solution.py:429
  614.8 3.5 maximum_convert_fusion
  619.2 3.4 maximum_convert_fusion.1
  (684 shorter events, 223.4 us)
Async XLA Ops:
  7.2 209.5 %all-gather.5.cloned.1.call-start = ((), (), s32[]{:S(2)}) async-start(), calls=%async_computation.2 | async-start | bytes 3538944 | tf_op jit(solution)/shard_map/all_gather | solution.py:639
  13.3 39.9 %collective-permute-start.14 = (bf16[256,768]{1,0:T(8,128)(2,1)}, bf16[256,768]{1,0:T(8,128)(2,1)}, u32[]{:S(2)}, u32[]{:S(2)}) collective-permute-start(bf16[256,768]{1,0:T(8,128)(2,1)} %get-tuple-element.184), channel_id=1, source_target_pairs={{0,1},{1,0},{2,3},{3,2},{4,5},{5,4},{6,7},{7,6},{8,9},{9,8},{10,11... | collective-permute-start | bytes 1179656 | tf_op jit(solution)/shard_map/ppermute | solution.py:542
  15.3 37.9 %collective-permute-start.15 = (bf16[256,768]{1,0:T(8,128)(2,1)}, bf16[256,768]{1,0:T(8,128)(2,1)}, u32[]{:S(2)}, u32[]{:S(2)}) collective-permute-start(bf16[256,768]{1,0:T(8,128)(2,1)} %get-tuple-element.186), channel_id=1, source_target_pairs={{0,2},{1,3},{2,0},{3,1},{4,6},{5,7},{6,4},{7,5},{8,10},{9,11},{10,... | collective-permute-start | bytes 1179656 | tf_op jit(solution)/shard_map/ppermute | solution.py:542
  19.4 16.8 %collective-permute-start.5 = (bf16[48,1152]{1,0:T(8,128)(2,1)}, bf16[48,1152]{1,0:T(8,128)(2,1)S(1)}, u32[]{:S(2)}, u32[]{:S(2)}) collective-permute-start(bf16[48,1152]{1,0:T(8,128)(2,1)} %get-tuple-element.54), channel_id=1, source_target_pairs={{0,1},{1,0},{2,3},{3,2},{4,5},{5,4},{6,7},{7,6},{8,9},{9,8},{10,11... | collective-permute-start | bytes 331784 | tf_op jit(solution)/shard_map/ppermute | solution.py:542
  19.6 16.7 %collective-permute-start.6 = (bf16[48,1152]{1,0:T(8,128)(2,1)}, bf16[48,1152]{1,0:T(8,128)(2,1)S(1)}, u32[]{:S(2)}, u32[]{:S(2)}) collective-permute-start(bf16[48,1152]{1,0:T(8,128)(2,1)} %get-tuple-element.55), channel_id=1, source_target_pairs={{0,2},{1,3},{2,0},{3,1},{4,6},{5,7},{6,4},{7,5},{8,10},{9,11},{10,... | collective-permute-start | bytes 331784 | tf_op jit(solution)/shard_map/ppermute | solution.py:542
  36.2 17.0 %collective-permute-start.16 = (bf16[256,768]{1,0:T(8,128)(2,1)S(1)}, bf16[256,768]{1,0:T(8,128)(2,1)S(1)}, u32[]{:S(2)}, u32[]{:S(2)}) collective-permute-start(bf16[256,768]{1,0:T(8,128)(2,1)S(1)} %copy-done.91), channel_id=1, source_target_pairs={{0,3},{1,2},{2,1},{3,0},{4,7},{5,6},{6,5},{7,4},{8,11},{9,10},{10,... | collective-permute-start | bytes 1179656 | tf_op jit(solution)/shard_map/ppermute | solution.py:542
  36.3 18.5 %collective-permute-start = (bf16[128,1664]{1,0:T(8,128)(2,1)S(1)}, bf16[128,1664]{1,0:T(8,128)(2,1)S(1)}, u32[]{:S(2)}, u32[]{:S(2)}) collective-permute-start(bf16[128,1664]{1,0:T(8,128)(2,1)S(1)} %fusion.70), channel_id=1, source_target_pairs={{4,8},{8,4},{5,9},{9,5},{6,10},{10,6},{7,11},{11,7},{20,24},{24,20... | collective-permute-start | bytes 1277960 | tf_op jit(solution)/shard_map/ppermute | solution.py:535
  54.5 20.8 %collective-permute-start.17 = (bf16[192,1152]{1,0:T(8,128)(2,1)S(1)}, bf16[192,1152]{1,0:T(8,128)(2,1)S(1)}, u32[]{:S(2)}, u32[]{:S(2)}) collective-permute-start(bf16[192,1152]{1,0:T(8,128)(2,1)S(1)} %pad_maximum_fusion.17.refs_0_), channel_id=1, source_target_pairs={{0,4},{4,0},{1,5},{5,1},{2,6},{6,2},{3,7},{7,3},{8,12},{12,8},{9,1... | collective-permute-start | bytes 1327112 | tf_op jit(solution)/shard_map/ppermute | solution.py:581
  55.9 20.8 %collective-permute-start.10 = (bf16[128,1664]{1,0:T(8,128)(2,1)S(1)}, bf16[128,1664]{1,0:T(8,128)(2,1)S(1)}, u32[]{:S(2)}, u32[]{:S(2)}) collective-permute-start(bf16[128,1664]{1,0:T(8,128)(2,1)S(1)} %broadcast_select_fusion.20), channel_id=1, source_target_pairs={{0,3},{1,2},{2,1},{3,0},{4,7},{5,6},{6,5},{7,4},{8,11},{9,10},{10,... | collective-permute-start | bytes 1277960 | tf_op jit(solution)/shard_map/ppermute | solution.py:542
  57.9 26.2 %collective-permute-start.8 = (bf16[128,1664]{1,0:T(8,128)(2,1)S(1)}, bf16[128,1664]{1,0:T(8,128)(2,1)S(1)}, u32[]{:S(2)}, u32[]{:S(2)}) collective-permute-start(bf16[128,1664]{1,0:T(8,128)(2,1)S(1)} %broadcast_select_fusion.20), channel_id=1, source_target_pairs={{0,1},{1,0},{2,3},{3,2},{4,5},{5,4},{6,7},{7,6},{8,9},{9,8},{10,11... | collective-permute-start | bytes 1277960 | tf_op jit(solution)/shard_map/ppermute | solution.py:542
  59.9 24.3 %collective-permute-start.20 = (bf16[192,1152]{1,0:T(8,128)(2,1)S(1)}, bf16[192,1152]{1,0:T(8,128)(2,1)S(1)}, u32[]{:S(2)}, u32[]{:S(2)}) collective-permute-start(bf16[192,1152]{1,0:T(8,128)(2,1)S(1)} %pad_maximum_fusion.17.refs_0_), channel_id=1, source_target_pairs={{0,16},{16,0},{1,17},{17,1},{2,18},{18,2},{3,19},{19,3},{4,20},{20... | collective-permute-start | bytes 1327112 | tf_op jit(solution)/shard_map/ppermute | solution.py:429
  76.6 13.1 %collective-permute-start.9 = (bf16[128,1664]{1,0:T(8,128)(2,1)S(1)}, bf16[128,1664]{1,0:T(8,128)(2,1)S(1)}, u32[]{:S(2)}, u32[]{:S(2)}) collective-permute-start(bf16[128,1664]{1,0:T(8,128)(2,1)S(1)} %broadcast_select_fusion.20), channel_id=1, source_target_pairs={{0,2},{1,3},{2,0},{3,1},{4,6},{5,7},{6,4},{7,5},{8,10},{9,11},{10,... | collective-permute-start | bytes 1277960 | tf_op jit(solution)/shard_map/ppermute | solution.py:542
  76.8 19.9 %collective-permute-start.18 = (bf16[256,768]{1,0:T(8,128)(2,1)S(1)}, bf16[256,768]{1,0:T(8,128)(2,1)S(1)}, u32[]{:S(2)}, u32[]{:S(2)}) collective-permute-start(bf16[256,768]{1,0:T(8,128)(2,1)S(1)} %fusion.50), channel_id=1, source_target_pairs={{4,8},{8,4},{5,9},{9,5},{6,10},{10,6},{7,11},{11,7},{20,24},{24,20... | collective-permute-start | bytes 1179656 | tf_op jit(solution)/shard_map/ppermute | solution.py:535
  84.1 17.0 %collective-permute-start.11 = (bf16[192,512]{1,0:T(8,128)(2,1)S(1)}, bf16[192,512]{1,0:T(8,128)(2,1)S(1)}, u32[]{:S(2)}, u32[]{:S(2)}) collective-permute-start(bf16[192,512]{1,0:T(8,128)(2,1)S(1)} %get-tuple-element.151), channel_id=1, source_target_pairs={{0,1},{1,0},{2,3},{3,2},{4,5},{5,4},{6,7},{7,6},{8,9},{9,8},{10,11... | collective-permute-start | bytes 589832 | tf_op jit(solution)/shard_map/ppermute | solution.py:542
  84.2 16.8 %collective-permute-start.12 = (bf16[192,512]{1,0:T(8,128)(2,1)S(1)}, bf16[192,512]{1,0:T(8,128)(2,1)S(1)}, u32[]{:S(2)}, u32[]{:S(2)}) collective-permute-start(bf16[192,512]{1,0:T(8,128)(2,1)S(1)} %get-tuple-element.150), channel_id=1, source_target_pairs={{0,2},{1,3},{2,0},{3,1},{4,6},{5,7},{6,4},{7,5},{8,10},{9,11},{10,... | collective-permute-start | bytes 589832 | tf_op jit(solution)/shard_map/ppermute | solution.py:542
  86.2 14.9 %collective-permute-start.13 = (bf16[192,512]{1,0:T(8,128)(2,1)S(1)}, bf16[192,512]{1,0:T(8,128)(2,1)S(1)}, u32[]{:S(2)}, u32[]{:S(2)}) collective-permute-start(bf16[192,512]{1,0:T(8,128)(2,1)S(1)} %get-tuple-element.149), channel_id=1, source_target_pairs={{0,3},{1,2},{2,1},{3,0},{4,7},{5,6},{6,5},{7,4},{8,11},{9,10},{10,... | collective-permute-start | bytes 589832 | tf_op jit(solution)/shard_map/ppermute | solution.py:542
  112.4 128.9 %all-gather.3.cloned.1.call-start = ((), (), s32[]{:S(2)}) async-start(), calls=%async_computation.1 | async-start | bytes 7077888 | tf_op jit(solution)/shard_map/all_gather | solution.py:627
  113.6 444.3 %reduce-scatter.2.cloned.1.call-start = ((), (), s32[]{:S(2)}) async-start(), calls=%async_computation.3 | async-start | bytes 7077888 | tf_op jit(solution)/shard_map/reduce_scatter | solution.py:789
  119.6 16.0 %collective-permute-start.26 = (bf16[192,384]{1,0:T(8,128)(2,1)S(1)}, bf16[192,384]{1,0:T(8,128)(2,1)S(1)}, u32[]{:S(2)}, u32[]{:S(2)}) collective-permute-start(bf16[192,384]{1,0:T(8,128)(2,1)S(1)} %constant_dynamic-slice_fusion.4.refs_0_), channel_id=1, source_target_pairs={{0,4},{4,0},{1,5},{5,1},{2,6},{6,2},{3,7},{7,3},{8,12},{12,8},{9,1... | collective-permute-start | bytes 442376 | tf_op jit(solution)/shard_map/ppermute | solution.py:581
  119.7 16.0 %collective-permute-start.28 = (bf16[192,384]{1,0:T(8,128)(2,1)S(1)}, bf16[192,384]{1,0:T(8,128)(2,1)S(1)}, u32[]{:S(2)}, u32[]{:S(2)}) collective-permute-start(bf16[192,384]{1,0:T(8,128)(2,1)S(1)} %constant_dynamic-slice_fusion.4.refs_0_), channel_id=1, source_target_pairs={{0,16},{16,0},{1,17},{17,1},{2,18},{18,2},{3,19},{19,3},{4,20},{20... | collective-permute-start | bytes 442376 | tf_op jit(solution)/shard_map/ppermute | solution.py:429
  121.4 14.2 %collective-permute-start.23 = (f32[10,128]{1,0:T(8,128)S(1)}, f32[10,128]{1,0:T(8,128)S(1)}, u32[]{:S(2)}, u32[]{:S(2)}) collective-permute-start(f32[10,128]{1,0:T(8,128)S(1)} %pad_maximum_fusion.28), channel_id=1, source_target_pairs={{0,1},{1,0},{2,3},{3,2},{4,5},{5,4},{6,7},{7,6},{8,9},{9,8},{10,11... | collective-permute-start | bytes 15368 | tf_op jit(solution)/shard_map/ppermute | solution.py:429
  123.4 20.2 %collective-permute-start.25 = (s32[1,512]{1,0:T(1,128)S(1)}, s32[1,512]{1,0:T(1,128)S(1)}, u32[]{:S(2)}, u32[]{:S(2)}) collective-permute-start(s32[1,512]{1,0:T(1,128)S(1)} %bitcast.179), channel_id=1, source_target_pairs={{0,8},{8,0},{1,9},{9,1},{2,10},{10,2},{3,11},{11,3},{4,12},{12,4},... | collective-permute-start | bytes 6152 | tf_op jit(solution)/shard_map/ppermute | solution.py:539
  172.7 20.0 %collective-permute-start.32 = (bf16[128,1536]{1,0:T(8,128)(2,1)}, bf16[128,1536]{1,0:T(8,128)(2,1)}, u32[]{:S(2)}, u32[]{:S(2)}) collective-permute-start(bf16[128,1536]{1,0:T(8,128)(2,1)} %get-tuple-element.183), channel_id=1, source_target_pairs={{0,2},{1,3},{2,0},{3,1},{4,6},{5,7},{6,4},{7,5},{8,10},{9,11},{10,... | collective-permute-start | bytes 1179656 | tf_op jit(solution)/shard_map/ppermute | solution.py:542
  172.7 33.4 %collective-permute-start.33 = (bf16[128,1536]{1,0:T(8,128)(2,1)S(1)}, bf16[128,1536]{1,0:T(8,128)(2,1)}, u32[]{:S(2)}, u32[]{:S(2)}) collective-permute-start(bf16[128,1536]{1,0:T(8,128)(2,1)S(1)} %get-tuple-element.182), channel_id=1, source_target_pairs={{0,3},{1,2},{2,1},{3,0},{4,7},{5,6},{6,5},{7,4},{8,11},{9,10},{10,... | collective-permute-start | bytes 1179656 | tf_op jit(solution)/shard_map/ppermute | solution.py:542
  175.2 101.6 %collective-permute-start.41 = (bf16[128,1536]{1,0:T(8,128)(2,1)}, bf16[128,1536]{1,0:T(8,128)(2,1)}, u32[]{:S(2)}, u32[]{:S(2)}) collective-permute-start(bf16[128,1536]{1,0:T(8,128)(2,1)} %param.33), channel_id=1, source_target_pairs={{4,8},{8,4},{5,9},{9,5},{6,10},{10,6},{7,11},{11,7},{20,24},{24,20... | collective-permute-start | bytes 1179656 | tf_op jit(solution)/shard_map/ppermute | solution.py:535
  178.7 34.6 %collective-permute-start.60 = (bf16[2,1,2,128]{3,2,1,0:T(2,128)(2,1)S(1)}, bf16[2,1,2,128]{3,2,1,0:T(2,128)(2,1)S(1)}, u32[]{:S(2)}, u32[]{:S(2)}) collective-permute-start(bf16[2,1,2,128]{3,2,1,0:T(2,128)(2,1)S(1)} %bitcast.211), channel_id=1, source_target_pairs={{0,16},{16,0},{1,17},{17,1},{2,18},{18,2},{3,19},{19,3},{4,20},{20... | collective-permute-start | bytes 3080 | tf_op jit(solution)/shard_map/ppermute | solution.py:429
  210.7 35.1 %collective-permute-start.34 = (bf16[128,1536]{1,0:T(8,128)(2,1)}, bf16[128,1536]{1,0:T(8,128)(2,1)}, u32[]{:S(2)}, u32[]{:S(2)}) collective-permute-start(bf16[128,1536]{1,0:T(8,128)(2,1)} %multiply_convert_fusion.7), channel_id=1, source_target_pairs={{0,1},{1,0},{2,3},{3,2},{4,5},{5,4},{6,7},{7,6},{8,9},{9,8},{10,11... | collective-permute-start | bytes 1179656 | tf_op jit(solution)/shard_map/ppermute | solution.py:542
  210.8 35.0 %collective-permute-start.35 = (bf16[128,1536]{1,0:T(8,128)(2,1)}, bf16[128,1536]{1,0:T(8,128)(2,1)}, u32[]{:S(2)}, u32[]{:S(2)}) collective-permute-start(bf16[128,1536]{1,0:T(8,128)(2,1)} %multiply_convert_fusion.7), channel_id=1, source_target_pairs={{0,2},{1,3},{2,0},{3,1},{4,6},{5,7},{6,4},{7,5},{8,10},{9,11},{10,... | collective-permute-start | bytes 1179656 | tf_op jit(solution)/shard_map/ppermute | solution.py:542
  210.9 36.7 %collective-permute-start.36 = (bf16[128,1536]{1,0:T(8,128)(2,1)}, bf16[128,1536]{1,0:T(8,128)(2,1)}, u32[]{:S(2)}, u32[]{:S(2)}) collective-permute-start(bf16[128,1536]{1,0:T(8,128)(2,1)} %multiply_convert_fusion.7), channel_id=1, source_target_pairs={{0,3},{1,2},{2,1},{3,0},{4,7},{5,6},{6,5},{7,4},{8,11},{9,10},{10,... | collective-permute-start | bytes 1179656 | tf_op jit(solution)/shard_map/ppermute | solution.py:542
  215.2 45.3 %collective-permute-start.78 = (bf16[512,384]{1,0:T(8,128)(2,1)S(1)}, bf16[512,384]{1,0:T(8,128)(2,1)}, u32[]{:S(2)}, u32[]{:S(2)}) collective-permute-start(bf16[512,384]{1,0:T(8,128)(2,1)S(1)} %copy-done.19), channel_id=1, source_target_pairs={{0,8},{8,0},{1,9},{9,1},{2,10},{10,2},{3,11},{11,3},{4,12},{12,4},... | collective-permute-start | bytes 1179656 | tf_op jit(solution)/shard_map/ppermute | solution.py:429
  257.9 18.5 %collective-permute-start.39 = (bf16[128,1536]{1,0:T(8,128)(2,1)S(1)}, bf16[128,1536]{1,0:T(8,128)(2,1)S(1)}, u32[]{:S(2)}, u32[]{:S(2)}) collective-permute-start(bf16[128,1536]{1,0:T(8,128)(2,1)S(1)} %get-tuple-element.179), channel_id=1, source_target_pairs={{0,3},{1,2},{2,1},{3,0},{4,7},{5,6},{6,5},{7,4},{8,11},{9,10},{10,... | collective-permute-start | bytes 1179656 | tf_op jit(solution)/shard_map/ppermute | solution.py:542
  280.1 21.3 %collective-permute-start.44 = (bf16[128,1536]{1,0:T(8,128)(2,1)S(1)}, bf16[128,1536]{1,0:T(8,128)(2,1)S(1)}, u32[]{:S(2)}, u32[]{:S(2)}) collective-permute-start(bf16[128,1536]{1,0:T(8,128)(2,1)S(1)} %get-tuple-element.191), channel_id=1, source_target_pairs={{0,3},{1,2},{2,1},{3,0},{4,7},{5,6},{6,5},{7,4},{8,11},{9,10},{10,... | collective-permute-start | bytes 1179656 | tf_op jit(solution)/shard_map/ppermute | solution.py:542
  285.1 91.7 %collective-permute-start.74 = (bf16[512,1024]{1,0:T(8,128)(2,1)}, bf16[512,1024]{1,0:T(8,128)(2,1)}, u32[]{:S(2)}, u32[]{:S(2)}) collective-permute-start(bf16[512,1024]{1,0:T(8,128)(2,1)} %multiply_convert_fusion.2), channel_id=1, source_target_pairs={{0,8},{8,0},{1,9},{9,1},{2,10},{10,2},{3,11},{11,3},{4,12},{12,4},... | collective-permute-start | bytes 3145736 | tf_op jit(solution)/shard_map/ppermute | solution.py:429
  288.5 42.0 %collective-permute-start.40 = (bf16[128,1536]{1,0:T(8,128)(2,1)}, bf16[128,1536]{1,0:T(8,128)(2,1)}, u32[]{:S(2)}, u32[]{:S(2)}) collective-permute-start(bf16[128,1536]{1,0:T(8,128)(2,1)} %get-tuple-element.192), channel_id=1, source_target_pairs={{4,8},{8,4},{5,9},{9,5},{6,10},{10,6},{7,11},{11,7},{20,24},{24,20... | collective-permute-start | bytes 1179656 | tf_op jit(solution)/shard_map/ppermute | solution.py:535
  312.7 22.4 %collective-permute-start.45 = (bf16[128,1536]{1,0:T(8,128)(2,1)}, bf16[128,1536]{1,0:T(8,128)(2,1)}, u32[]{:S(2)}, u32[]{:S(2)}) collective-permute-start(bf16[128,1536]{1,0:T(8,128)(2,1)} %get-tuple-element.175), channel_id=1, source_target_pairs={{0,1},{1,0},{2,3},{3,2},{4,5},{5,4},{6,7},{7,6},{8,9},{9,8},{10,11... | collective-permute-start | bytes 1179656 | tf_op jit(solution)/shard_map/ppermute | solution.py:542
  312.7 22.4 %collective-permute-start.46 = (bf16[128,1536]{1,0:T(8,128)(2,1)}, bf16[128,1536]{1,0:T(8,128)(2,1)}, u32[]{:S(2)}, u32[]{:S(2)}) collective-permute-start(bf16[128,1536]{1,0:T(8,128)(2,1)} %get-tuple-element.177), channel_id=1, source_target_pairs={{0,2},{1,3},{2,0},{3,1},{4,6},{5,7},{6,4},{7,5},{8,10},{9,11},{10,... | collective-permute-start | bytes 1179656 | tf_op jit(solution)/shard_map/ppermute | solution.py:542
  312.7 22.4 %collective-permute-start.47 = (bf16[128,1536]{1,0:T(8,128)(2,1)}, bf16[128,1536]{1,0:T(8,128)(2,1)}, u32[]{:S(2)}, u32[]{:S(2)}) collective-permute-start(bf16[128,1536]{1,0:T(8,128)(2,1)} %get-tuple-element.176), channel_id=1, source_target_pairs={{0,3},{1,2},{2,1},{3,0},{4,7},{5,6},{6,5},{7,4},{8,11},{9,10},{10,... | collective-permute-start | bytes 1179656 | tf_op jit(solution)/shard_map/ppermute | solution.py:542
  330.4 46.3 %collective-permute-start.75 = (bf16[512,768]{1,0:T(8,128)(2,1)S(1)}, bf16[512,768]{1,0:T(8,128)(2,1)S(1)}, u32[]{:S(2)}, u32[]{:S(2)}) collective-permute-start(bf16[512,768]{1,0:T(8,128)(2,1)S(1)} %get-tuple-element.168), channel_id=1, source_target_pairs={{0,8},{8,0},{1,9},{9,1},{2,10},{10,2},{3,11},{11,3},{4,12},{12,4},... | collective-permute-start | bytes 2359304 | tf_op jit(solution)/shard_map/ppermute | solution.py:429
  340.0 19.9 %collective-permute-start.50 = (bf16[128,1536]{1,0:T(8,128)(2,1)S(1)}, bf16[128,1536]{1,0:T(8,128)(2,1)S(1)}, u32[]{:S(2)}, u32[]{:S(2)}) collective-permute-start(bf16[128,1536]{1,0:T(8,128)(2,1)S(1)} %multiply_convert_fusion.5), channel_id=1, source_target_pairs={{0,3},{1,2},{2,1},{3,0},{4,7},{5,6},{6,5},{7,4},{8,11},{9,10},{10,... | collective-permute-start | bytes 1179656 | tf_op jit(solution)/shard_map/ppermute | solution.py:542
  373.5 16.1 %collective-permute-start.52 = (bf16[256,768]{1,0:T(8,128)(2,1)S(1)}, bf16[256,768]{1,0:T(8,128)(2,1)S(1)}, u32[]{:S(2)}, u32[]{:S(2)}) collective-permute-start(bf16[256,768]{1,0:T(8,128)(2,1)S(1)} %fusion.66), channel_id=1, source_target_pairs={{0,8},{8,0},{1,9},{9,1},{2,10},{10,2},{3,11},{11,3},{4,12},{12,4},... | collective-permute-start | bytes 1179656 | tf_op jit(solution)/shard_map/ppermute | solution.py:429
  376.7 14.8 %collective-permute-start.51 = (bf16[2,512,384]{2,1,0:T(8,128)(2,1)S(1)}, bf16[2,512,384]{2,1,0:T(8,128)(2,1)S(1)}, u32[]{:S(2)}, u32[]{:S(2)}) collective-permute-start(bf16[2,512,384]{2,1,0:T(8,128)(2,1)S(1)} %bitcast.182), channel_id=1, source_target_pairs={{0,8},{8,0},{1,9},{9,1},{2,10},{10,2},{3,11},{11,3},{4,12},{12,4},... | collective-permute-start | bytes 2359304 | tf_op jit(solution)/shard_map/ppermute | solution.py:804
  380.8 38.2 %collective-permute-start.76 = (bf16[1024,384]{1,0:T(8,128)(2,1)}, bf16[1024,384]{1,0:T(8,128)(2,1)}, u32[]{:S(2)}, u32[]{:S(2)}) collective-permute-start(bf16[1024,384]{1,0:T(8,128)(2,1)} %convolution_convert_fusion.2), channel_id=1, source_target_pairs={{0,16},{16,0},{1,17},{17,1},{2,18},{18,2},{3,19},{19,3},{4,20},{20... | collective-permute-start | bytes 2359304 | tf_op jit(solution)/shard_map/ppermute | solution.py:429
  382.3 23.2 %collective-permute-start.79 = (bf16[512,768]{1,0:T(8,128)(2,1)}, bf16[512,768]{1,0:T(8,128)(2,1)}, u32[]{:S(2)}, u32[]{:S(2)}) collective-permute-start(bf16[512,768]{1,0:T(8,128)(2,1)} %get-tuple-element.170), channel_id=1, source_target_pairs={{0,8},{8,0},{1,9},{9,1},{2,10},{10,2},{3,11},{11,3},{4,12},{12,4},... | collective-permute-start | bytes 2359304 | tf_op jit(solution)/shard_map/ppermute | solution.py:429
  414.4 23.7 %collective-permute-start.55 = (bf16[2,4,2,48,1152]{4,3,1,0,2:T(8,128)(2,1)S(1)}, bf16[2,4,2,48,1152]{4,3,1,0,2:T(8,128)(2,1)}, u32[]{:S(2)}, u32[]{:S(2)}) collective-permute-start(bf16[2,4,2,48,1152]{4,3,1,0,2:T(8,128)(2,1)S(1)} %bitcast.191), channel_id=1, source_target_pairs={{0,8},{8,0},{1,9},{9,1},{2,10},{10,2},{3,11},{11,3},{4,12},{12,4},... | collective-permute-start | bytes 5308424 | tf_op jit(solution)/shard_map/ppermute | solution.py:429
  422.6 14.6 %collective-permute-start.85 = (bf16[256,768]{1,0:T(8,128)(2,1)S(1)}, bf16[256,768]{1,0:T(8,128)(2,1)S(1)}, u32[]{:S(2)}, u32[]{:S(2)}) collective-permute-start(bf16[256,768]{1,0:T(8,128)(2,1)S(1)} %pad_maximum_fusion.18), channel_id=1, source_target_pairs={{4,8},{8,4},{5,9},{9,5},{6,10},{10,6},{7,11},{11,7},{20,24},{24,20... | collective-permute-start | bytes 1179656 | tf_op jit(solution)/shard_map/ppermute | solution.py:535
  440.4 19.8 %collective-permute-start.56 = (bf16[128,1536]{1,0:T(8,128)(2,1)S(1)}, bf16[128,1536]{1,0:T(8,128)(2,1)S(1)}, u32[]{:S(2)}, u32[]{:S(2)}) collective-permute-start(bf16[128,1536]{1,0:T(8,128)(2,1)S(1)} %get-tuple-element.172), channel_id=1, source_target_pairs={{0,1},{1,0},{2,3},{3,2},{4,5},{5,4},{6,7},{7,6},{8,9},{9,8},{10,11... | collective-permute-start | bytes 1179656 | tf_op jit(solution)/shard_map/ppermute | solution.py:542
  441.2 19.0 %collective-permute-start.57 = (bf16[128,1536]{1,0:T(8,128)(2,1)S(1)}, bf16[128,1536]{1,0:T(8,128)(2,1)S(1)}, u32[]{:S(2)}, u32[]{:S(2)}) collective-permute-start(bf16[128,1536]{1,0:T(8,128)(2,1)S(1)} %get-tuple-element.174), channel_id=1, source_target_pairs={{0,2},{1,3},{2,0},{3,1},{4,6},{5,7},{6,4},{7,5},{8,10},{9,11},{10,... | collective-permute-start | bytes 1179656 | tf_op jit(solution)/shard_map/ppermute | solution.py:542
  441.2 19.0 %collective-permute-start.58 = (bf16[128,1536]{1,0:T(8,128)(2,1)S(1)}, bf16[128,1536]{1,0:T(8,128)(2,1)S(1)}, u32[]{:S(2)}, u32[]{:S(2)}) collective-permute-start(bf16[128,1536]{1,0:T(8,128)(2,1)S(1)} %get-tuple-element.173), channel_id=1, source_target_pairs={{0,3},{1,2},{2,1},{3,0},{4,7},{5,6},{6,5},{7,4},{8,11},{9,10},{10,... | collective-permute-start | bytes 1179656 | tf_op jit(solution)/shard_map/ppermute | solution.py:542
  443.1 13.8 %collective-permute-start.81 = (bf16[192,384]{1,0:T(8,128)(2,1)S(1)}, bf16[192,384]{1,0:T(8,128)(2,1)S(1)}, u32[]{:S(2)}, u32[]{:S(2)}) collective-permute-start(bf16[192,384]{1,0:T(8,128)(2,1)S(1)} %fusion.90), channel_id=1, source_target_pairs={{0,4},{4,0},{1,5},{5,1},{2,6},{6,2},{3,7},{7,3},{8,12},{12,8},{9,1... | collective-permute-start | bytes 442376 | tf_op jit(solution)/shard_map/ppermute | solution.py:429
  446.2 46.1 %collective-permute-start.64 = (bf16[2,4,48,1152]{3,2,1,0:T(8,128)(2,1)}, bf16[2,4,48,1152]{3,2,1,0:T(8,128)(2,1)}, u32[]{:S(2)}, u32[]{:S(2)}) collective-permute-start(bf16[2,4,48,1152]{3,2,1,0:T(8,128)(2,1)} %dynamic-slice_bitcast_fusion), channel_id=1, source_target_pairs={{0,16},{16,0},{1,17},{17,1},{2,18},{18,2},{3,19},{19,3},{4,20},{20... | collective-permute-start | bytes 2654216 | tf_op jit(solution)/shard_map/ppermute | solution.py:429
  457.0 14.5 %collective-permute-start.77 = (bf16[512,384]{1,0:T(8,128)(2,1)}, bf16[512,384]{1,0:T(8,128)(2,1)}, u32[]{:S(2)}, u32[]{:S(2)}) collective-permute-start(bf16[512,384]{1,0:T(8,128)(2,1)} %fusion.71), channel_id=1, source_target_pairs={{0,4},{4,0},{1,5},{5,1},{2,6},{6,2},{3,7},{7,3},{8,12},{12,8},{9,1... | collective-permute-start | bytes 1179656 | tf_op jit(solution)/shard_map/ppermute | solution.py:429
  472.9 26.1 %collective-permute-start.82 = (bf16[704,384]{1,0:T(8,128)(2,1)S(1)}, bf16[704,384]{1,0:T(8,128)(2,1)S(1)}, u32[]{:S(2)}, u32[]{:S(2)}) collective-permute-start(bf16[704,384]{1,0:T(8,128)(2,1)S(1)} %fusion.11), channel_id=1, source_target_pairs={{0,16},{16,0},{1,17},{17,1},{2,18},{18,2},{3,19},{19,3},{4,20},{20... | collective-permute-start | bytes 1622024 | tf_op jit(solution)/shard_map/ppermute | solution.py:429
  478.2 13.2 %collective-permute-start.59 = (bf16[128,1536]{1,0:T(8,128)(2,1)S(1)}, bf16[128,1536]{1,0:T(8,128)(2,1)S(1)}, u32[]{:S(2)}, u32[]{:S(2)}) collective-permute-start(bf16[128,1536]{1,0:T(8,128)(2,1)S(1)} %get-tuple-element.126), channel_id=1, source_target_pairs={{4,8},{8,4},{5,9},{9,5},{6,10},{10,6},{7,11},{11,7},{20,24},{24,20... | collective-permute-start | bytes 1179656 | tf_op jit(solution)/shard_map/ppermute | solution.py:535
  496.3 16.2 %collective-permute-start.88 = (bf16[256,768]{1,0:T(8,128)(2,1)S(1)}, bf16[256,768]{1,0:T(8,128)(2,1)}, u32[]{:S(2)}, u32[]{:S(2)}) collective-permute-start(bf16[256,768]{1,0:T(8,128)(2,1)S(1)} %copy-done.82), channel_id=1, source_target_pairs={{0,3},{1,2},{2,1},{3,0},{4,7},{5,6},{6,5},{7,4},{8,11},{9,10},{10,... | collective-permute-start | bytes 1179656 | tf_op jit(solution)/shard_map/ppermute | solution.py:542
  498.8 21.4 %collective-permute-start.65 = (bf16[4,48,1152]{2,1,0:T(8,128)(2,1)}, bf16[4,48,1152]{2,1,0:T(8,128)(2,1)}, u32[]{:S(2)}, u32[]{:S(2)}) collective-permute-start(bf16[4,48,1152]{2,1,0:T(8,128)(2,1)} %dynamic-slice_bitcast_fusion.1), channel_id=1, source_target_pairs={{0,4},{4,0},{1,5},{5,1},{2,6},{6,2},{3,7},{7,3},{8,12},{12,8},{9,1... | collective-permute-start | bytes 1327112 | tf_op jit(solution)/shard_map/ppermute | solution.py:429
  527.1 23.5 %collective-permute-start.84 = (bf16[256,512]{1,0:T(8,128)(2,1)S(1)}, bf16[256,512]{1,0:T(8,128)(2,1)}, u32[]{:S(2)}, u32[]{:S(2)}) collective-permute-start(bf16[256,512]{1,0:T(8,128)(2,1)S(1)} %bitcast.174), channel_id=1, source_target_pairs={{0,8},{8,0},{1,9},{9,1},{2,10},{10,2},{3,11},{11,3},{4,12},{12,4},... | collective-permute-start | bytes 786440 | tf_op jit(solution)/shard_map/ppermute | solution.py:429
  530.4 23.8 %collective-permute-start.83 = (bf16[704,768]{1,0:T(8,128)(2,1)S(1)}, bf16[704,768]{1,0:T(8,128)(2,1)S(1)}, u32[]{:S(2)}, u32[]{:S(2)}) collective-permute-start(bf16[704,768]{1,0:T(8,128)(2,1)S(1)} %copy-done.85), channel_id=1, source_target_pairs={{0,8},{8,0},{1,9},{9,1},{2,10},{10,2},{3,11},{11,3},{4,12},{12,4},... | collective-permute-start | bytes 3244040 | tf_op jit(solution)/shard_map/ppermute | solution.py:429
  530.5 20.1 %collective-permute-start.89 = (bf16[256,1536]{1,0:T(8,128)(2,1)}, bf16[256,1536]{1,0:T(8,128)(2,1)}, u32[]{:S(2)}, u32[]{:S(2)}) collective-permute-start(bf16[256,1536]{1,0:T(8,128)(2,1)} %get-tuple-element.166), channel_id=1, source_target_pairs={{0,8},{8,0},{1,9},{9,1},{2,10},{10,2},{3,11},{11,3},{4,12},{12,4},... | collective-permute-start | bytes 2359304 | tf_op jit(solution)/shard_map/ppermute | solution.py:429
  547.4 38.6 %collective-permute-start.73 = (bf16[2,48,4608]{2,1,0:T(8,128)(2,1)}, bf16[2,48,4608]{2,1,0:T(8,128)(2,1)}, u32[]{:S(2)}, u32[]{:S(2)}) collective-permute-start(bf16[2,48,4608]{2,1,0:T(8,128)(2,1)} %pad_maximum_fusion.13), channel_id=1, source_target_pairs={{0,8},{8,0},{1,9},{9,1},{2,10},{10,2},{3,11},{11,3},{4,12},{12,4},... | collective-permute-start | bytes 2654216 | tf_op jit(solution)/shard_map/ppermute | solution.py:429
  553.3 19.5 %collective-permute-start.90 = (bf16[512,768]{1,0:T(8,128)(2,1)}, bf16[512,768]{1,0:T(8,128)(2,1)}, u32[]{:S(2)}, u32[]{:S(2)}) collective-permute-start(bf16[512,768]{1,0:T(8,128)(2,1)} %convolution_convert_fusion.1), channel_id=1, source_target_pairs={{0,16},{16,0},{1,17},{17,1},{2,18},{18,2},{3,19},{19,3},{4,20},{20... | collective-permute-start | bytes 2359304 | tf_op jit(solution)/shard_map/ppermute | solution.py:429
  559.0 19.5 %collective-permute-start.93 = (bf16[192,512]{1,0:T(8,128)(2,1)S(1)}, bf16[192,512]{1,0:T(8,128)(2,1)S(1)}, u32[]{:S(2)}, u32[]{:S(2)}) collective-permute-start(bf16[192,512]{1,0:T(8,128)(2,1)S(1)} %get-tuple-element.196), channel_id=1, source_target_pairs={{0,1},{1,0},{2,3},{3,2},{4,5},{5,4},{6,7},{7,6},{8,9},{9,8},{10,11... | collective-permute-start | bytes 589832 | tf_op jit(solution)/shard_map/ppermute | solution.py:542
  574.7 18.3 %collective-permute-start.91 = (bf16[512,768]{1,0:T(8,128)(2,1)S(1)}, bf16[512,768]{1,0:T(8,128)(2,1)S(1)}, u32[]{:S(2)}, u32[]{:S(2)}) collective-permute-start(bf16[512,768]{1,0:T(8,128)(2,1)S(1)} %reduce-precision_convert_fusion), channel_id=1, source_target_pairs={{0,16},{16,0},{1,17},{17,1},{2,18},{18,2},{3,19},{19,3},{4,20},{20... | collective-permute-start | bytes 2359304 | tf_op jit(solution)/shard_map/ppermute | solution.py:429
  585.6 24.3 %collective-permute-start.96 = (bf16[192,2048]{1,0:T(8,128)(2,1)S(1)}, bf16[192,2048]{1,0:T(8,128)(2,1)S(1)}, u32[]{:S(2)}, u32[]{:S(2)}) collective-permute-start(bf16[192,2048]{1,0:T(8,128)(2,1)S(1)} %constant_dynamic-update-slice_fusion.6), channel_id=1, source_target_pairs={{0,16},{16,0},{1,17},{17,1},{2,18},{18,2},{3,19},{19,3},{4,20},{20... | collective-permute-start | bytes 2359304 | tf_op jit(solution)/shard_map/ppermute | solution.py:429
  593.3 20.9 %collective-permute-start.92 = (bf16[512,1536]{1,0:T(8,128)(2,1)S(1)}, bf16[512,1536]{1,0:T(8,128)(2,1)S(1)}, u32[]{:S(2)}, u32[]{:S(2)}) collective-permute-start(bf16[512,1536]{1,0:T(8,128)(2,1)S(1)} %pad_maximum_fusion.7), channel_id=1, source_target_pairs={{0,8},{8,0},{1,9},{9,1},{2,10},{10,2},{3,11},{11,3},{4,12},{12,4},... | collective-permute-start | bytes 4718600 | tf_op jit(solution)/shard_map/ppermute | solution.py:429
  (191 other events, 1845.3 us)
Sparse Core Ops, SparseCore 0:
  112.5 50.2 all-gather.4
  165.3 76.0 all-gather.2
  328.9 88.4 reduce-scatter.1

commit v4 on v3

--- a/solution.py
+++ b/solution.py
@@ -844,9 +844,8 @@
 
     qkv_part = low(outer_reduce(qkv_part))
     qkv_summed = qkv_part
-    qkv_part = [
-        to_place(lax.dynamic_index_in_dim(qkv_part, me_c ^ r, 0, keepdims=False), r) for r in range(4)
-    ]
+    qkv_part = [lax.dynamic_index_in_dim(qkv_part, me_c ^ r, 0, keepdims=False) for r in range(4)]
+    qkv_part = qkv_part[:1] + [to_place(qkv_part[r], r) for r in (1, 2, 3)]
     qkv_part = lay(qkv_part, 3)
     qkv_part = pair_stack(qkv_part[None], "x", 0)
     qkv_other = swap(qkv_part, "core")

time: 639 us -> 640 us (level)
    unnamed x306 -> x302, local copies, waits for them, and re-layouts: 17.5 us -> 16.7 us
    ppermute x43 -> x42, waiting for transfers between devices: 87.8 us -> 87.1 us  [to_place(): return lax.ppermute(value, ('p', 'y'), across[r])]
    ppermute x43 -> x42, starting transfers between devices: 39.6 us -> 39.7 us  [to_place(): return lax.ppermute(value, ('p', 'y'), across[r])]
  transfers between devices with their start and end apart: 103 -> 102, of which waited for: 36 -> 37; matrix products, arithmetic and copies ran while one was open for 23% -> 23% of each run, Pallas kernels for 11% -> 11%
where the time goes in v4:
time: 640 us; the launch traced here: 630 us
  waiting for transfers between devices  221 us (35%)
  starting transfers between devices  137 us (21%)
  Pallas kernels  80.6 us (13%)
  other arithmetic  76.9 us (12%)
  matrix products  55.4 us (9%)
  local copies, waits for them, and re-layouts  42.1 us (7%)
  between operations  17 us (3%)
    ppermute x42, waiting for transfers between devices, to_place(): return lax.ppermute(value, ('p', 'y'), across[r])  87.1 us
    ppermute x46, waiting for transfers between devices, swap(): return lax.ppermute(value, axis, SWAP)  73.2 us
    ppermute x46, starting transfers between devices, swap(): return lax.ppermute(value, axis, SWAP)  68.3 us
    dot_general x18, matrix products, dot(): return lax.dot_general(a, b, (dims, ((), ())), preferred_element_type=F32)  50.2 us
    ppermute x42, starting transfers between devices, to_place(): return lax.ppermute(value, ('p', 'y'), across[r])  39.7 us
    ppermute x6, starting transfers between devices, mirror(): other = lax.ppermute(value, ('core', 'o'), [(1, 2), (2, 1)])  25.5 us
    ppermute x2, waiting for transfers between devices, hand_on(): far_piece = lax.ppermute(own, 'o', beyond[r])  23 us
    all_gather x1, waiting for transfers between devices, fetch_gate_up(): whole = lax.all_gather(own, ('core', 'x', 'o'), axis=0, tiled=True)  20.1 us
  transfers between devices with their start and end apart: 102, of which 37 were waited for; matrix products, arithmetic and copies ran while one was open for 23% of the time, Pallas kernels for 11%

profile of v4, /device:TPU:1, one launch (start us, length us, event | category | flops | bytes accessed | tf_op | source)
XLA Modules:
  0.0 630.1 jit_solution(6890361400092754471)
XLA Ops:
  27.1 2.8 collective-permute-start.2
  35.1 2.6 collective-permute-start.7
  37.8 6.8 %collective-permute-start = (bf16[128,1664]{1,0:T(8,128)(2,1)S(1)}, bf16[128,1664]{1,0:T(8,128)(2,1)S(1)}, u32[]{:S(2)}, u32[]{:S(2)}) collective-permute-start(bf16[128,1664]{1,0:T(8,128)(2,1)S(1)} %fusion.70), channel_id=1, source_target_pairs={{4,8},{8,4},{5,9},{9,5},{6,10},{10,6},{7,11},{11,7},{20,24},{24,20... | collective-permute-start | bytes 1277960 | tf_op jit(solution)/shard_map/ppermute | solution.py:535
  46.4 8.2 %collective-permute-done.4 = bf16[4,6144]{1,0:T(4,128)(2,1)S(1)} collective-permute-done((bf16[4,6144]{1,0:T(4,128)(2,1)S(1)}, bf16[4,6144]{1,0:T(4,128)(2,1)S(1)}, u32[]{:S(2)}, u32[]{:S(2)}) %collective-permute-start.4) | collective-permute-done | bytes 49184 | tf_op jit(solution)/shard_map/ppermute | solution.py:429
  62.7 14.2 %collective-permute-done.17.refs_2_ = bf16[192,1152]{1,0:T(8,128)(2,1)S(1)} collective-permute-done((bf16[192,1152]{1,0:T(8,128)(2,1)S(1)}, bf16[192,1152]{1,0:T(8,128)(2,1)S(1)}, u32[]{:S(2)}, u32[]{:S(2)}) %collective-permute-start.17) | collective-permute-done | bytes 442400 | tf_op jit(solution)/shard_map/ppermute | solution.py:581
  78.3 6.0 collective-permute-start.18
  91.3 6.4 %collective-permute-start.22 = (bf16[768,1152]{1,0:T(8,128)(2,1)S(1)}, bf16[768,1152]{1,0:T(8,128)(2,1)S(1)}, u32[]{:S(2)}, u32[]{:S(2)}) collective-permute-start(bf16[768,1152]{1,0:T(8,128)(2,1)S(1)} %pad_maximum_fusion.2), channel_id=1, source_target_pairs={{0,8},{8,0},{1,9},{9,1},{2,10},{10,2},{3,11},{11,3},{4,12},{12,4},... | collective-permute-start | bytes 5308424 | tf_op jit(solution)/shard_map/ppermute | solution.py:429
  103.3 6.3 assemble.4
  124.9 3.3 collective-permute-start.25
  128.2 8.8 %collective-permute-done.26.refs_2_ = bf16[192,384]{1,0:T(8,128)(2,1)S(1)} collective-permute-done((bf16[192,384]{1,0:T(8,128)(2,1)S(1)}, bf16[192,384]{1,0:T(8,128)(2,1)S(1)}, u32[]{:S(2)}, u32[]{:S(2)}) %collective-permute-start.26) | collective-permute-done | bytes 147488 | tf_op jit(solution)/shard_map/ppermute | solution.py:581
  137.2 3.8 collective-permute-done.29.refs_3_
  141.1 3.1 collective-permute-start.30
  145.1 4.4 heads_in.1
  153.6 6.2 attn_near.1
  159.9 10.5 %attn_far.1 = (f32[512,384]{1,0:T(8,128)S(1)}, bf16[512,384]{1,0:T(8,128)(2,1)S(1)}, f32[3,512,2]{2,1,0:T(8,128)S(1)}) custom-call(bf16[512,384]{1,0:T(8,128)(2,1)S(1)} %copy-done.6, bf16[1,2,512,384]{3,2,1,0:T(8,128)(2,1)S(1)} %bitcast.169, bf16[1,2,512,384]{3,2,1,0:T(8,128)(2,1)S(1)} %bitcast.170, s32[512,1]{1,0:T(8,128)S(1)} %slice_convert_fusion.2.sq_ref, ...), custom_call_target="tpu_custom_call" | custom-call | flops 402653184 | bytes 6291456 | tf_op jit(solution)/shard_map/attn_far/pallas_call | solution.py:751
  170.4 2.6 fusion.163
  176.7 3.3 collective-permute-start.41
  181.7 2.9 collective-permute-done.31
  184.6 9.6 %collective-permute-done.32 = bf16[128,1536]{1,0:T(8,128)(2,1)} collective-permute-done((bf16[128,1536]{1,0:T(8,128)(2,1)}, bf16[128,1536]{1,0:T(8,128)(2,1)}, u32[]{:S(2)}, u32[]{:S(2)}) %collective-permute-start.32) | collective-permute-done | bytes 393248 | tf_op jit(solution)/shard_map/ppermute | solution.py:542
  194.2 13.4 %collective-permute-done.33 = bf16[128,1536]{1,0:T(8,128)(2,1)} collective-permute-done((bf16[128,1536]{1,0:T(8,128)(2,1)S(1)}, bf16[128,1536]{1,0:T(8,128)(2,1)}, u32[]{:S(2)}, u32[]{:S(2)}) %collective-permute-start.33) | collective-permute-done | bytes 393248 | tf_op jit(solution)/shard_map/ppermute | solution.py:542
  222.8 20.1 %all-gather.3.cloned.1.call-done.refs_0_ = bf16[6144,512]{1,0:T(8,128)(2,1)} async-done(((bf16[768,512]{1,0:T(8,128)(2,1)}), bf16[6144,512]{1,0:T(8,128)(2,1)}) %all-gather.3.cloned.1.call-update) | async-done | bytes 6291472 | tf_op jit(solution)/shard_map/all_gather | solution.py:627
  242.9 2.8 copy-done.3
  249.0 4.9 fusion.141
  256.2 3.0 fusion.164
  263.7 4.9 collective-permute-done.37
  268.6 9.3 %collective-permute-done.39 = bf16[128,1536]{1,0:T(8,128)(2,1)S(1)} collective-permute-done((bf16[128,1536]{1,0:T(8,128)(2,1)S(1)}, bf16[128,1536]{1,0:T(8,128)(2,1)S(1)}, u32[]{:S(2)}, u32[]{:S(2)}) %collective-permute-start.39) | collective-permute-done | bytes 393248 | tf_op jit(solution)/shard_map/ppermute | solution.py:542
  284.0 2.6 pad_maximum_fusion.4.left_ref
  286.6 3.4 collective-permute-start.73
  292.9 10.1 %collective-permute-done.44 = bf16[128,1536]{1,0:T(8,128)(2,1)S(1)} collective-permute-done((bf16[128,1536]{1,0:T(8,128)(2,1)S(1)}, bf16[128,1536]{1,0:T(8,128)(2,1)S(1)}, u32[]{:S(2)}, u32[]{:S(2)}) %collective-permute-start.44) | collective-permute-done | bytes 393248 | tf_op jit(solution)/shard_map/ppermute | solution.py:542
  303.0 3.5 multiply_convert_fusion.1
  306.5 5.1 fusion.165
  314.2 2.6 collective-permute-start.47
  316.8 13.4 %grad_product.1 = bf16[4,1536,512]{2,1,0:T(8,128)(2,1)} custom-call(bf16[512,1536]{1,0:T(8,128)(2,1)} %pad_maximum_fusion.4.left_ref, bf16[512,2048]{1,0:T(8,128)(2,1)} %pad_maximum_fusion.right_ref), custom_call_target="tpu_custom_call" | custom-call | flops 3221225472 | bytes 9961472 | tf_op jit(solution)/shard_map/grad_product/pallas_call | solution.py:309
  331.9 4.6 collective-permute-start.74
  336.6 3.6 multiply_reduce_fusion.1
  346.0 5.0 collective-permute-done.48
  351.0 2.6 collective-permute-start.83
  353.6 7.9 %collective-permute-done.50 = bf16[128,1536]{1,0:T(8,128)(2,1)S(1)} collective-permute-done((bf16[128,1536]{1,0:T(8,128)(2,1)S(1)}, bf16[128,1536]{1,0:T(8,128)(2,1)S(1)}, u32[]{:S(2)}, u32[]{:S(2)}) %collective-permute-start.50) | collective-permute-done | bytes 393248 | tf_op jit(solution)/shard_map/ppermute | solution.py:542
  362.5 12.5 %attn_back_far.1 = (f32[512,384]{1,0:T(8,128)S(1)}, bf16[1,2,512,384]{3,2,1,0:T(8,128)(2,1)S(1)}, f32[256,384]{1,0:T(8,128)S(1)}, f32[256,384]{1,0:T(8,128)S(1)}...) custom-call(bf16[512,384]{1,0:T(8,128)(2,1)S(1)} %copy-done.6, bf16[512,384]{1,0:T(8,128)(2,1)S(1)} %convolution_convert_fusion.3.g_ref, ...), custom_call_target="tpu_custom_call" | custom-call | flops 1509949440 | bytes 6291456 | tf_op jit(solution)/shard_map/attn_back_far/pallas_call | solution.py:800
  375.0 3.1 collective-permute-start.52
  378.2 4.0 convolution_convert_fusion.2
  384.1 6.8 %attn_back_near.1 = (f32[512,384]{1,0:T(8,128)S(1)}, f32[512,384]{1,0:T(8,128)S(1)}, f32[512,384]{1,0:T(8,128)S(1)}) custom-call(bf16[512,384]{1,0:T(8,128)(2,1)S(1)} %copy-done.6, bf16[512,384]{1,0:T(8,128)(2,1)S(1)} %convolution_convert_fusion.3.g_ref, f32[3,512,2]{2,1,0:T(8,128)S(1)} %copy-done.9, f32[3,512,2]{2,1,0:T(8,128)S(1)} %get-tuple-element.75.delta_ref, ...), custom_call_target="tpu_custom_call" | custom-call | flops 1006632960 | bytes 6291456 | tf_op jit(solution)/shard_map/attn_back_near/pallas_call | solution.py:805
  393.8 5.3 heads_back.1
  403.6 3.6 collective-permute-start.54
  407.2 2.7 convolution_convert_fusion.4
  420.5 3.3 convert_add_fusion.2
  429.1 9.6 %collective-permute-done.84 = bf16[256,768]{1,0:T(8,128)(2,1)S(1)} collective-permute-done((bf16[256,768]{1,0:T(8,128)(2,1)S(1)}, bf16[256,768]{1,0:T(8,128)(2,1)S(1)}, u32[]{:S(2)}, u32[]{:S(2)}) %collective-permute-start.84) | collective-permute-done | bytes 393248 | tf_op jit(solution)/shard_map/ppermute | solution.py:535
  448.5 7.7 %collective-permute-done.80 = bf16[192,384]{1,0:T(8,128)(2,1)S(1)} collective-permute-done((bf16[192,384]{1,0:T(8,128)(2,1)S(1)}, bf16[192,384]{1,0:T(8,128)(2,1)S(1)}, u32[]{:S(2)}, u32[]{:S(2)}) %collective-permute-start.80) | collective-permute-done | bytes 147488 | tf_op jit(solution)/shard_map/ppermute | solution.py:429
  458.4 3.3 collective-permute-start.76
  463.0 10.8 %collective-permute-done.76 = bf16[512,384]{1,0:T(8,128)(2,1)} collective-permute-done((bf16[512,384]{1,0:T(8,128)(2,1)}, bf16[512,384]{1,0:T(8,128)(2,1)}, u32[]{:S(2)}, u32[]{:S(2)}) %collective-permute-start.76) | collective-permute-done | bytes 393248 | tf_op jit(solution)/shard_map/ppermute | solution.py:429
  479.4 5.0 collective-permute-start.59
  485.2 7.7 %collective-permute-done.59 = bf16[128,1536]{1,0:T(8,128)(2,1)S(1)} collective-permute-done((bf16[128,1536]{1,0:T(8,128)(2,1)S(1)}, bf16[128,1536]{1,0:T(8,128)(2,1)S(1)}, u32[]{:S(2)}, u32[]{:S(2)}) %collective-permute-start.59) | collective-permute-done | bytes 393248 | tf_op jit(solution)/shard_map/ppermute | solution.py:535
  494.7 2.6 collective-permute-start.86
  506.9 6.7 %collective-permute-done.87.refs_3_ = bf16[256,768]{1,0:T(8,128)(2,1)} collective-permute-done((bf16[256,768]{1,0:T(8,128)(2,1)S(1)}, bf16[256,768]{1,0:T(8,128)(2,1)}, u32[]{:S(2)}, u32[]{:S(2)}) %collective-permute-start.87) | collective-permute-done | bytes 393248 | tf_op jit(solution)/shard_map/ppermute | solution.py:542
  513.6 2.9 lay.5
  547.8 3.4 collective-permute-start.72
  551.2 2.8 convolution_convert_fusion.1
  560.6 12.8 %collective-permute-done.89 = bf16[512,768]{1,0:T(8,128)(2,1)} collective-permute-done((bf16[512,768]{1,0:T(8,128)(2,1)}, bf16[512,768]{1,0:T(8,128)(2,1)}, u32[]{:S(2)}, u32[]{:S(2)}) %collective-permute-start.89) | collective-permute-done | bytes 786464 | tf_op jit(solution)/shard_map/ppermute | solution.py:429
  582.1 4.5 collective-permute-done.94
  588.6 5.3 collective-permute-done.90
  594.1 3.0 collective-permute-start.91
  597.1 13.6 %collective-permute-done.95 = bf16[192,2048]{1,0:T(8,128)(2,1)S(1)} collective-permute-done((bf16[192,2048]{1,0:T(8,128)(2,1)S(1)}, bf16[192,2048]{1,0:T(8,128)(2,1)S(1)}, u32[]{:S(2)}, u32[]{:S(2)}) %collective-permute-start.95) | collective-permute-done | bytes 786464 | tf_op jit(solution)/shard_map/ppermute | solution.py:429
  615.6 3.5 maximum_convert_fusion
  620.0 3.4 maximum_convert_fusion.1
  (678 shorter events, 228.9 us)
Async XLA Ops:
  7.2 211.0 %all-gather.5.cloned.1.call-start = ((), (), s32[]{:S(2)}) async-start(), calls=%async_computation.2 | async-start | bytes 3538944 | tf_op jit(solution)/shard_map/all_gather | solution.py:639
  14.8 39.9 %collective-permute-start.14 = (bf16[256,768]{1,0:T(8,128)(2,1)}, bf16[256,768]{1,0:T(8,128)(2,1)}, u32[]{:S(2)}, u32[]{:S(2)}) collective-permute-start(bf16[256,768]{1,0:T(8,128)(2,1)} %get-tuple-element.184), channel_id=1, source_target_pairs={{0,1},{1,0},{2,3},{3,2},{4,5},{5,4},{6,7},{7,6},{8,9},{9,8},{10,11... | collective-permute-start | bytes 1179656 | tf_op jit(solution)/shard_map/ppermute | solution.py:542
  16.9 37.9 %collective-permute-start.15 = (bf16[256,768]{1,0:T(8,128)(2,1)}, bf16[256,768]{1,0:T(8,128)(2,1)}, u32[]{:S(2)}, u32[]{:S(2)}) collective-permute-start(bf16[256,768]{1,0:T(8,128)(2,1)} %get-tuple-element.186), channel_id=1, source_target_pairs={{0,2},{1,3},{2,0},{3,1},{4,6},{5,7},{6,4},{7,5},{8,10},{9,11},{10,... | collective-permute-start | bytes 1179656 | tf_op jit(solution)/shard_map/ppermute | solution.py:542
  20.9 16.8 %collective-permute-start.5 = (bf16[48,1152]{1,0:T(8,128)(2,1)}, bf16[48,1152]{1,0:T(8,128)(2,1)S(1)}, u32[]{:S(2)}, u32[]{:S(2)}) collective-permute-start(bf16[48,1152]{1,0:T(8,128)(2,1)} %get-tuple-element.54), channel_id=1, source_target_pairs={{0,1},{1,0},{2,3},{3,2},{4,5},{5,4},{6,7},{7,6},{8,9},{9,8},{10,11... | collective-permute-start | bytes 331784 | tf_op jit(solution)/shard_map/ppermute | solution.py:542
  21.1 16.7 %collective-permute-start.6 = (bf16[48,1152]{1,0:T(8,128)(2,1)}, bf16[48,1152]{1,0:T(8,128)(2,1)S(1)}, u32[]{:S(2)}, u32[]{:S(2)}) collective-permute-start(bf16[48,1152]{1,0:T(8,128)(2,1)} %get-tuple-element.55), channel_id=1, source_target_pairs={{0,2},{1,3},{2,0},{3,1},{4,6},{5,7},{6,4},{7,5},{8,10},{9,11},{10,... | collective-permute-start | bytes 331784 | tf_op jit(solution)/shard_map/ppermute | solution.py:542
  37.8 17.0 %collective-permute-start.16 = (bf16[256,768]{1,0:T(8,128)(2,1)S(1)}, bf16[256,768]{1,0:T(8,128)(2,1)S(1)}, u32[]{:S(2)}, u32[]{:S(2)}) collective-permute-start(bf16[256,768]{1,0:T(8,128)(2,1)S(1)} %copy-done.89), channel_id=1, source_target_pairs={{0,3},{1,2},{2,1},{3,0},{4,7},{5,6},{6,5},{7,4},{8,11},{9,10},{10,... | collective-permute-start | bytes 1179656 | tf_op jit(solution)/shard_map/ppermute | solution.py:542
  37.8 18.5 %collective-permute-start = (bf16[128,1664]{1,0:T(8,128)(2,1)S(1)}, bf16[128,1664]{1,0:T(8,128)(2,1)S(1)}, u32[]{:S(2)}, u32[]{:S(2)}) collective-permute-start(bf16[128,1664]{1,0:T(8,128)(2,1)S(1)} %fusion.70), channel_id=1, source_target_pairs={{4,8},{8,4},{5,9},{9,5},{6,10},{10,6},{7,11},{11,7},{20,24},{24,20... | collective-permute-start | bytes 1277960 | tf_op jit(solution)/shard_map/ppermute | solution.py:535
  56.1 20.8 %collective-permute-start.17 = (bf16[192,1152]{1,0:T(8,128)(2,1)S(1)}, bf16[192,1152]{1,0:T(8,128)(2,1)S(1)}, u32[]{:S(2)}, u32[]{:S(2)}) collective-permute-start(bf16[192,1152]{1,0:T(8,128)(2,1)S(1)} %pad_maximum_fusion.17.refs_0_), channel_id=1, source_target_pairs={{0,4},{4,0},{1,5},{5,1},{2,6},{6,2},{3,7},{7,3},{8,12},{12,8},{9,1... | collective-permute-start | bytes 1327112 | tf_op jit(solution)/shard_map/ppermute | solution.py:581
  57.5 20.8 %collective-permute-start.10 = (bf16[128,1664]{1,0:T(8,128)(2,1)S(1)}, bf16[128,1664]{1,0:T(8,128)(2,1)S(1)}, u32[]{:S(2)}, u32[]{:S(2)}) collective-permute-start(bf16[128,1664]{1,0:T(8,128)(2,1)S(1)} %broadcast_select_fusion.20), channel_id=1, source_target_pairs={{0,3},{1,2},{2,1},{3,0},{4,7},{5,6},{6,5},{7,4},{8,11},{9,10},{10,... | collective-permute-start | bytes 1277960 | tf_op jit(solution)/shard_map/ppermute | solution.py:542
  59.4 26.2 %collective-permute-start.8 = (bf16[128,1664]{1,0:T(8,128)(2,1)S(1)}, bf16[128,1664]{1,0:T(8,128)(2,1)S(1)}, u32[]{:S(2)}, u32[]{:S(2)}) collective-permute-start(bf16[128,1664]{1,0:T(8,128)(2,1)S(1)} %broadcast_select_fusion.20), channel_id=1, source_target_pairs={{0,1},{1,0},{2,3},{3,2},{4,5},{5,4},{6,7},{7,6},{8,9},{9,8},{10,11... | collective-permute-start | bytes 1277960 | tf_op jit(solution)/shard_map/ppermute | solution.py:542
  61.4 24.3 %collective-permute-start.20 = (bf16[192,1152]{1,0:T(8,128)(2,1)S(1)}, bf16[192,1152]{1,0:T(8,128)(2,1)S(1)}, u32[]{:S(2)}, u32[]{:S(2)}) collective-permute-start(bf16[192,1152]{1,0:T(8,128)(2,1)S(1)} %pad_maximum_fusion.17.refs_0_), channel_id=1, source_target_pairs={{0,16},{16,0},{1,17},{17,1},{2,18},{18,2},{3,19},{19,3},{4,20},{20... | collective-permute-start | bytes 1327112 | tf_op jit(solution)/shard_map/ppermute | solution.py:429
  78.2 13.1 %collective-permute-start.9 = (bf16[128,1664]{1,0:T(8,128)(2,1)S(1)}, bf16[128,1664]{1,0:T(8,128)(2,1)S(1)}, u32[]{:S(2)}, u32[]{:S(2)}) collective-permute-start(bf16[128,1664]{1,0:T(8,128)(2,1)S(1)} %broadcast_select_fusion.20), channel_id=1, source_target_pairs={{0,2},{1,3},{2,0},{3,1},{4,6},{5,7},{6,4},{7,5},{8,10},{9,11},{10,... | collective-permute-start | bytes 1277960 | tf_op jit(solution)/shard_map/ppermute | solution.py:542
  78.3 19.9 %collective-permute-start.18 = (bf16[256,768]{1,0:T(8,128)(2,1)S(1)}, bf16[256,768]{1,0:T(8,128)(2,1)S(1)}, u32[]{:S(2)}, u32[]{:S(2)}) collective-permute-start(bf16[256,768]{1,0:T(8,128)(2,1)S(1)} %fusion.50), channel_id=1, source_target_pairs={{4,8},{8,4},{5,9},{9,5},{6,10},{10,6},{7,11},{11,7},{20,24},{24,20... | collective-permute-start | bytes 1179656 | tf_op jit(solution)/shard_map/ppermute | solution.py:535
  85.6 17.0 %collective-permute-start.11 = (bf16[192,512]{1,0:T(8,128)(2,1)S(1)}, bf16[192,512]{1,0:T(8,128)(2,1)S(1)}, u32[]{:S(2)}, u32[]{:S(2)}) collective-permute-start(bf16[192,512]{1,0:T(8,128)(2,1)S(1)} %get-tuple-element.151), channel_id=1, source_target_pairs={{0,1},{1,0},{2,3},{3,2},{4,5},{5,4},{6,7},{7,6},{8,9},{9,8},{10,11... | collective-permute-start | bytes 589832 | tf_op jit(solution)/shard_map/ppermute | solution.py:542
  85.7 16.8 %collective-permute-start.12 = (bf16[192,512]{1,0:T(8,128)(2,1)S(1)}, bf16[192,512]{1,0:T(8,128)(2,1)S(1)}, u32[]{:S(2)}, u32[]{:S(2)}) collective-permute-start(bf16[192,512]{1,0:T(8,128)(2,1)S(1)} %get-tuple-element.150), channel_id=1, source_target_pairs={{0,2},{1,3},{2,0},{3,1},{4,6},{5,7},{6,4},{7,5},{8,10},{9,11},{10,... | collective-permute-start | bytes 589832 | tf_op jit(solution)/shard_map/ppermute | solution.py:542
  87.7 14.9 %collective-permute-start.13 = (bf16[192,512]{1,0:T(8,128)(2,1)S(1)}, bf16[192,512]{1,0:T(8,128)(2,1)S(1)}, u32[]{:S(2)}, u32[]{:S(2)}) collective-permute-start(bf16[192,512]{1,0:T(8,128)(2,1)S(1)} %get-tuple-element.149), channel_id=1, source_target_pairs={{0,3},{1,2},{2,1},{3,0},{4,7},{5,6},{6,5},{7,4},{8,11},{9,10},{10,... | collective-permute-start | bytes 589832 | tf_op jit(solution)/shard_map/ppermute | solution.py:542
  113.9 128.9 %all-gather.3.cloned.1.call-start = ((), (), s32[]{:S(2)}) async-start(), calls=%async_computation.1 | async-start | bytes 7077888 | tf_op jit(solution)/shard_map/all_gather | solution.py:627
  115.1 443.7 %reduce-scatter.2.cloned.1.call-start = ((), (), s32[]{:S(2)}) async-start(), calls=%async_computation.3 | async-start | bytes 7077888 | tf_op jit(solution)/shard_map/reduce_scatter | solution.py:789
  121.1 15.9 %collective-permute-start.26 = (bf16[192,384]{1,0:T(8,128)(2,1)S(1)}, bf16[192,384]{1,0:T(8,128)(2,1)S(1)}, u32[]{:S(2)}, u32[]{:S(2)}) collective-permute-start(bf16[192,384]{1,0:T(8,128)(2,1)S(1)} %constant_dynamic-slice_fusion.4.refs_0_), channel_id=1, source_target_pairs={{0,4},{4,0},{1,5},{5,1},{2,6},{6,2},{3,7},{7,3},{8,12},{12,8},{9,1... | collective-permute-start | bytes 442376 | tf_op jit(solution)/shard_map/ppermute | solution.py:581
  121.2 16.0 %collective-permute-start.28 = (bf16[192,384]{1,0:T(8,128)(2,1)S(1)}, bf16[192,384]{1,0:T(8,128)(2,1)S(1)}, u32[]{:S(2)}, u32[]{:S(2)}) collective-permute-start(bf16[192,384]{1,0:T(8,128)(2,1)S(1)} %constant_dynamic-slice_fusion.4.refs_0_), channel_id=1, source_target_pairs={{0,16},{16,0},{1,17},{17,1},{2,18},{18,2},{3,19},{19,3},{4,20},{20... | collective-permute-start | bytes 442376 | tf_op jit(solution)/shard_map/ppermute | solution.py:429
  122.9 14.1 %collective-permute-start.23 = (f32[10,128]{1,0:T(8,128)S(1)}, f32[10,128]{1,0:T(8,128)S(1)}, u32[]{:S(2)}, u32[]{:S(2)}) collective-permute-start(f32[10,128]{1,0:T(8,128)S(1)} %pad_maximum_fusion.28), channel_id=1, source_target_pairs={{0,1},{1,0},{2,3},{3,2},{4,5},{5,4},{6,7},{7,6},{8,9},{9,8},{10,11... | collective-permute-start | bytes 15368 | tf_op jit(solution)/shard_map/ppermute | solution.py:429
  124.9 20.2 %collective-permute-start.25 = (s32[1,512]{1,0:T(1,128)S(1)}, s32[1,512]{1,0:T(1,128)S(1)}, u32[]{:S(2)}, u32[]{:S(2)}) collective-permute-start(s32[1,512]{1,0:T(1,128)S(1)} %bitcast.175), channel_id=1, source_target_pairs={{0,8},{8,0},{1,9},{9,1},{2,10},{10,2},{3,11},{11,3},{4,12},{12,4},... | collective-permute-start | bytes 6152 | tf_op jit(solution)/shard_map/ppermute | solution.py:539
  174.2 20.0 %collective-permute-start.32 = (bf16[128,1536]{1,0:T(8,128)(2,1)}, bf16[128,1536]{1,0:T(8,128)(2,1)}, u32[]{:S(2)}, u32[]{:S(2)}) collective-permute-start(bf16[128,1536]{1,0:T(8,128)(2,1)} %get-tuple-element.183), channel_id=1, source_target_pairs={{0,2},{1,3},{2,0},{3,1},{4,6},{5,7},{6,4},{7,5},{8,10},{9,11},{10,... | collective-permute-start | bytes 1179656 | tf_op jit(solution)/shard_map/ppermute | solution.py:542
  174.2 33.4 %collective-permute-start.33 = (bf16[128,1536]{1,0:T(8,128)(2,1)S(1)}, bf16[128,1536]{1,0:T(8,128)(2,1)}, u32[]{:S(2)}, u32[]{:S(2)}) collective-permute-start(bf16[128,1536]{1,0:T(8,128)(2,1)S(1)} %get-tuple-element.182), channel_id=1, source_target_pairs={{0,3},{1,2},{2,1},{3,0},{4,7},{5,6},{6,5},{7,4},{8,11},{9,10},{10,... | collective-permute-start | bytes 1179656 | tf_op jit(solution)/shard_map/ppermute | solution.py:542
  176.7 101.6 %collective-permute-start.41 = (bf16[128,1536]{1,0:T(8,128)(2,1)}, bf16[128,1536]{1,0:T(8,128)(2,1)}, u32[]{:S(2)}, u32[]{:S(2)}) collective-permute-start(bf16[128,1536]{1,0:T(8,128)(2,1)} %param.33), channel_id=1, source_target_pairs={{4,8},{8,4},{5,9},{9,5},{6,10},{10,6},{7,11},{11,7},{20,24},{24,20... | collective-permute-start | bytes 1179656 | tf_op jit(solution)/shard_map/ppermute | solution.py:535
  180.3 34.6 %collective-permute-start.60 = (bf16[2,1,2,128]{3,2,1,0:T(2,128)(2,1)S(1)}, bf16[2,1,2,128]{3,2,1,0:T(2,128)(2,1)S(1)}, u32[]{:S(2)}, u32[]{:S(2)}) collective-permute-start(bf16[2,1,2,128]{3,2,1,0:T(2,128)(2,1)S(1)} %bitcast.207), channel_id=1, source_target_pairs={{0,16},{16,0},{1,17},{17,1},{2,18},{18,2},{3,19},{19,3},{4,20},{20... | collective-permute-start | bytes 3080 | tf_op jit(solution)/shard_map/ppermute | solution.py:429
  212.2 35.1 %collective-permute-start.34 = (bf16[128,1536]{1,0:T(8,128)(2,1)}, bf16[128,1536]{1,0:T(8,128)(2,1)}, u32[]{:S(2)}, u32[]{:S(2)}) collective-permute-start(bf16[128,1536]{1,0:T(8,128)(2,1)} %multiply_convert_fusion.7), channel_id=1, source_target_pairs={{0,1},{1,0},{2,3},{3,2},{4,5},{5,4},{6,7},{7,6},{8,9},{9,8},{10,11... | collective-permute-start | bytes 1179656 | tf_op jit(solution)/shard_map/ppermute | solution.py:542
  212.4 35.0 %collective-permute-start.35 = (bf16[128,1536]{1,0:T(8,128)(2,1)}, bf16[128,1536]{1,0:T(8,128)(2,1)}, u32[]{:S(2)}, u32[]{:S(2)}) collective-permute-start(bf16[128,1536]{1,0:T(8,128)(2,1)} %multiply_convert_fusion.7), channel_id=1, source_target_pairs={{0,2},{1,3},{2,0},{3,1},{4,6},{5,7},{6,4},{7,5},{8,10},{9,11},{10,... | collective-permute-start | bytes 1179656 | tf_op jit(solution)/shard_map/ppermute | solution.py:542
  212.4 36.7 %collective-permute-start.36 = (bf16[128,1536]{1,0:T(8,128)(2,1)}, bf16[128,1536]{1,0:T(8,128)(2,1)}, u32[]{:S(2)}, u32[]{:S(2)}) collective-permute-start(bf16[128,1536]{1,0:T(8,128)(2,1)} %multiply_convert_fusion.7), channel_id=1, source_target_pairs={{0,3},{1,2},{2,1},{3,0},{4,7},{5,6},{6,5},{7,4},{8,11},{9,10},{10,... | collective-permute-start | bytes 1179656 | tf_op jit(solution)/shard_map/ppermute | solution.py:542
  216.7 45.3 %collective-permute-start.77 = (bf16[512,384]{1,0:T(8,128)(2,1)S(1)}, bf16[512,384]{1,0:T(8,128)(2,1)}, u32[]{:S(2)}, u32[]{:S(2)}) collective-permute-start(bf16[512,384]{1,0:T(8,128)(2,1)S(1)} %copy-done.19), channel_id=1, source_target_pairs={{0,8},{8,0},{1,9},{9,1},{2,10},{10,2},{3,11},{11,3},{4,12},{12,4},... | collective-permute-start | bytes 1179656 | tf_op jit(solution)/shard_map/ppermute | solution.py:429
  259.4 18.5 %collective-permute-start.39 = (bf16[128,1536]{1,0:T(8,128)(2,1)S(1)}, bf16[128,1536]{1,0:T(8,128)(2,1)S(1)}, u32[]{:S(2)}, u32[]{:S(2)}) collective-permute-start(bf16[128,1536]{1,0:T(8,128)(2,1)S(1)} %get-tuple-element.179), channel_id=1, source_target_pairs={{0,3},{1,2},{2,1},{3,0},{4,7},{5,6},{6,5},{7,4},{8,11},{9,10},{10,... | collective-permute-start | bytes 1179656 | tf_op jit(solution)/shard_map/ppermute | solution.py:542
  281.6 21.3 %collective-permute-start.44 = (bf16[128,1536]{1,0:T(8,128)(2,1)S(1)}, bf16[128,1536]{1,0:T(8,128)(2,1)S(1)}, u32[]{:S(2)}, u32[]{:S(2)}) collective-permute-start(bf16[128,1536]{1,0:T(8,128)(2,1)S(1)} %get-tuple-element.191), channel_id=1, source_target_pairs={{0,3},{1,2},{2,1},{3,0},{4,7},{5,6},{6,5},{7,4},{8,11},{9,10},{10,... | collective-permute-start | bytes 1179656 | tf_op jit(solution)/shard_map/ppermute | solution.py:542
  286.6 91.6 %collective-permute-start.73 = (bf16[512,1024]{1,0:T(8,128)(2,1)}, bf16[512,1024]{1,0:T(8,128)(2,1)}, u32[]{:S(2)}, u32[]{:S(2)}) collective-permute-start(bf16[512,1024]{1,0:T(8,128)(2,1)} %multiply_convert_fusion.2), channel_id=1, source_target_pairs={{0,8},{8,0},{1,9},{9,1},{2,10},{10,2},{3,11},{11,3},{4,12},{12,4},... | collective-permute-start | bytes 3145736 | tf_op jit(solution)/shard_map/ppermute | solution.py:429
  290.0 41.9 %collective-permute-start.40 = (bf16[128,1536]{1,0:T(8,128)(2,1)}, bf16[128,1536]{1,0:T(8,128)(2,1)}, u32[]{:S(2)}, u32[]{:S(2)}) collective-permute-start(bf16[128,1536]{1,0:T(8,128)(2,1)} %get-tuple-element.192), channel_id=1, source_target_pairs={{4,8},{8,4},{5,9},{9,5},{6,10},{10,6},{7,11},{11,7},{20,24},{24,20... | collective-permute-start | bytes 1179656 | tf_op jit(solution)/shard_map/ppermute | solution.py:535
  314.2 22.4 %collective-permute-start.45 = (bf16[128,1536]{1,0:T(8,128)(2,1)}, bf16[128,1536]{1,0:T(8,128)(2,1)}, u32[]{:S(2)}, u32[]{:S(2)}) collective-permute-start(bf16[128,1536]{1,0:T(8,128)(2,1)} %get-tuple-element.175), channel_id=1, source_target_pairs={{0,1},{1,0},{2,3},{3,2},{4,5},{5,4},{6,7},{7,6},{8,9},{9,8},{10,11... | collective-permute-start | bytes 1179656 | tf_op jit(solution)/shard_map/ppermute | solution.py:542
  314.2 22.4 %collective-permute-start.46 = (bf16[128,1536]{1,0:T(8,128)(2,1)}, bf16[128,1536]{1,0:T(8,128)(2,1)}, u32[]{:S(2)}, u32[]{:S(2)}) collective-permute-start(bf16[128,1536]{1,0:T(8,128)(2,1)} %get-tuple-element.177), channel_id=1, source_target_pairs={{0,2},{1,3},{2,0},{3,1},{4,6},{5,7},{6,4},{7,5},{8,10},{9,11},{10,... | collective-permute-start | bytes 1179656 | tf_op jit(solution)/shard_map/ppermute | solution.py:542
  314.2 22.4 %collective-permute-start.47 = (bf16[128,1536]{1,0:T(8,128)(2,1)}, bf16[128,1536]{1,0:T(8,128)(2,1)}, u32[]{:S(2)}, u32[]{:S(2)}) collective-permute-start(bf16[128,1536]{1,0:T(8,128)(2,1)} %get-tuple-element.176), channel_id=1, source_target_pairs={{0,3},{1,2},{2,1},{3,0},{4,7},{5,6},{6,5},{7,4},{8,11},{9,10},{10,... | collective-permute-start | bytes 1179656 | tf_op jit(solution)/shard_map/ppermute | solution.py:542
  331.9 46.3 %collective-permute-start.74 = (bf16[512,768]{1,0:T(8,128)(2,1)S(1)}, bf16[512,768]{1,0:T(8,128)(2,1)S(1)}, u32[]{:S(2)}, u32[]{:S(2)}) collective-permute-start(bf16[512,768]{1,0:T(8,128)(2,1)S(1)} %get-tuple-element.168), channel_id=1, source_target_pairs={{0,8},{8,0},{1,9},{9,1},{2,10},{10,2},{3,11},{11,3},{4,12},{12,4},... | collective-permute-start | bytes 2359304 | tf_op jit(solution)/shard_map/ppermute | solution.py:429
  341.5 20.0 %collective-permute-start.50 = (bf16[128,1536]{1,0:T(8,128)(2,1)S(1)}, bf16[128,1536]{1,0:T(8,128)(2,1)S(1)}, u32[]{:S(2)}, u32[]{:S(2)}) collective-permute-start(bf16[128,1536]{1,0:T(8,128)(2,1)S(1)} %multiply_convert_fusion.5), channel_id=1, source_target_pairs={{0,3},{1,2},{2,1},{3,0},{4,7},{5,6},{6,5},{7,4},{8,11},{9,10},{10,... | collective-permute-start | bytes 1179656 | tf_op jit(solution)/shard_map/ppermute | solution.py:542
  351.0 200.2 %collective-permute-start.83 = (bf16[256,512]{1,0:T(8,128)(2,1)}, bf16[256,512]{1,0:T(8,128)(2,1)}, u32[]{:S(2)}, u32[]{:S(2)}) collective-permute-start(bf16[256,512]{1,0:T(8,128)(2,1)} %bitcast.3.rows_ref), channel_id=1, source_target_pairs={{0,8},{8,0},{1,9},{9,1},{2,10},{10,2},{3,11},{11,3},{4,12},{12,4},... | collective-permute-start | bytes 786440 | tf_op jit(solution)/shard_map/ppermute | solution.py:429
  375.0 15.9 %collective-permute-start.52 = (bf16[256,768]{1,0:T(8,128)(2,1)S(1)}, bf16[256,768]{1,0:T(8,128)(2,1)S(1)}, u32[]{:S(2)}, u32[]{:S(2)}) collective-permute-start(bf16[256,768]{1,0:T(8,128)(2,1)S(1)} %fusion.66), channel_id=1, source_target_pairs={{0,8},{8,0},{1,9},{9,1},{2,10},{10,2},{3,11},{11,3},{4,12},{12,4},... | collective-permute-start | bytes 1179656 | tf_op jit(solution)/shard_map/ppermute | solution.py:429
  378.1 14.8 %collective-permute-start.51 = (bf16[2,512,384]{2,1,0:T(8,128)(2,1)S(1)}, bf16[2,512,384]{2,1,0:T(8,128)(2,1)S(1)}, u32[]{:S(2)}, u32[]{:S(2)}) collective-permute-start(bf16[2,512,384]{2,1,0:T(8,128)(2,1)S(1)} %bitcast.178), channel_id=1, source_target_pairs={{0,8},{8,0},{1,9},{9,1},{2,10},{10,2},{3,11},{11,3},{4,12},{12,4},... | collective-permute-start | bytes 2359304 | tf_op jit(solution)/shard_map/ppermute | solution.py:804
  382.2 38.3 %collective-permute-start.75 = (bf16[1024,384]{1,0:T(8,128)(2,1)}, bf16[1024,384]{1,0:T(8,128)(2,1)}, u32[]{:S(2)}, u32[]{:S(2)}) collective-permute-start(bf16[1024,384]{1,0:T(8,128)(2,1)} %convolution_convert_fusion.2), channel_id=1, source_target_pairs={{0,16},{16,0},{1,17},{17,1},{2,18},{18,2},{3,19},{19,3},{4,20},{20... | collective-permute-start | bytes 2359304 | tf_op jit(solution)/shard_map/ppermute | solution.py:429
  383.7 23.5 %collective-permute-start.78 = (bf16[512,768]{1,0:T(8,128)(2,1)}, bf16[512,768]{1,0:T(8,128)(2,1)}, u32[]{:S(2)}, u32[]{:S(2)}) collective-permute-start(bf16[512,768]{1,0:T(8,128)(2,1)} %get-tuple-element.170), channel_id=1, source_target_pairs={{0,8},{8,0},{1,9},{9,1},{2,10},{10,2},{3,11},{11,3},{4,12},{12,4},... | collective-permute-start | bytes 2359304 | tf_op jit(solution)/shard_map/ppermute | solution.py:429
  416.0 23.5 %collective-permute-start.55 = (bf16[2,4,2,48,1152]{4,3,1,0,2:T(8,128)(2,1)S(1)}, bf16[2,4,2,48,1152]{4,3,1,0,2:T(8,128)(2,1)}, u32[]{:S(2)}, u32[]{:S(2)}) collective-permute-start(bf16[2,4,2,48,1152]{4,3,1,0,2:T(8,128)(2,1)S(1)} %bitcast.187), channel_id=1, source_target_pairs={{0,8},{8,0},{1,9},{9,1},{2,10},{10,2},{3,11},{11,3},{4,12},{12,4},... | collective-permute-start | bytes 5308424 | tf_op jit(solution)/shard_map/ppermute | solution.py:429
  424.1 14.6 %collective-permute-start.84 = (bf16[256,768]{1,0:T(8,128)(2,1)S(1)}, bf16[256,768]{1,0:T(8,128)(2,1)S(1)}, u32[]{:S(2)}, u32[]{:S(2)}) collective-permute-start(bf16[256,768]{1,0:T(8,128)(2,1)S(1)} %pad_maximum_fusion.18), channel_id=1, source_target_pairs={{4,8},{8,4},{5,9},{9,5},{6,10},{10,6},{7,11},{11,7},{20,24},{24,20... | collective-permute-start | bytes 1179656 | tf_op jit(solution)/shard_map/ppermute | solution.py:535
  441.9 16.5 %collective-permute-start.56 = (bf16[128,1536]{1,0:T(8,128)(2,1)S(1)}, bf16[128,1536]{1,0:T(8,128)(2,1)S(1)}, u32[]{:S(2)}, u32[]{:S(2)}) collective-permute-start(bf16[128,1536]{1,0:T(8,128)(2,1)S(1)} %get-tuple-element.172), channel_id=1, source_target_pairs={{0,1},{1,0},{2,3},{3,2},{4,5},{5,4},{6,7},{7,6},{8,9},{9,8},{10,11... | collective-permute-start | bytes 1179656 | tf_op jit(solution)/shard_map/ppermute | solution.py:542
  442.5 19.2 %collective-permute-start.57 = (bf16[128,1536]{1,0:T(8,128)(2,1)S(1)}, bf16[128,1536]{1,0:T(8,128)(2,1)S(1)}, u32[]{:S(2)}, u32[]{:S(2)}) collective-permute-start(bf16[128,1536]{1,0:T(8,128)(2,1)S(1)} %get-tuple-element.174), channel_id=1, source_target_pairs={{0,2},{1,3},{2,0},{3,1},{4,6},{5,7},{6,4},{7,5},{8,10},{9,11},{10,... | collective-permute-start | bytes 1179656 | tf_op jit(solution)/shard_map/ppermute | solution.py:542
  442.5 19.2 %collective-permute-start.58 = (bf16[128,1536]{1,0:T(8,128)(2,1)S(1)}, bf16[128,1536]{1,0:T(8,128)(2,1)S(1)}, u32[]{:S(2)}, u32[]{:S(2)}) collective-permute-start(bf16[128,1536]{1,0:T(8,128)(2,1)S(1)} %get-tuple-element.173), channel_id=1, source_target_pairs={{0,3},{1,2},{2,1},{3,0},{4,7},{5,6},{6,5},{7,4},{8,11},{9,10},{10,... | collective-permute-start | bytes 1179656 | tf_op jit(solution)/shard_map/ppermute | solution.py:542
  456.2 37.7 %collective-permute-start.64 = (bf16[2,4,48,1152]{3,2,1,0:T(8,128)(2,1)}, bf16[2,4,48,1152]{3,2,1,0:T(8,128)(2,1)}, u32[]{:S(2)}, u32[]{:S(2)}) collective-permute-start(bf16[2,4,48,1152]{3,2,1,0:T(8,128)(2,1)} %dynamic-slice_bitcast_fusion), channel_id=1, source_target_pairs={{0,16},{16,0},{1,17},{17,1},{2,18},{18,2},{3,19},{19,3},{4,20},{20... | collective-permute-start | bytes 2654216 | tf_op jit(solution)/shard_map/ppermute | solution.py:429
  458.4 15.4 %collective-permute-start.76 = (bf16[512,384]{1,0:T(8,128)(2,1)}, bf16[512,384]{1,0:T(8,128)(2,1)}, u32[]{:S(2)}, u32[]{:S(2)}) collective-permute-start(bf16[512,384]{1,0:T(8,128)(2,1)} %fusion.71), channel_id=1, source_target_pairs={{0,4},{4,0},{1,5},{5,1},{2,6},{6,2},{3,7},{7,3},{8,12},{12,8},{9,1... | collective-permute-start | bytes 1179656 | tf_op jit(solution)/shard_map/ppermute | solution.py:429
  462.9 12.5 %collective-permute-start.61 = (bf16[16,1536]{1,0:T(8,128)(2,1)S(1)}, bf16[16,1536]{1,0:T(8,128)(2,1)S(1)}, u32[]{:S(2)}, u32[]{:S(2)}) collective-permute-start(bf16[16,1536]{1,0:T(8,128)(2,1)S(1)} %reduce-precision_convert_fusion.3), channel_id=1, source_target_pairs={{0,8},{8,0},{1,9},{9,1},{2,10},{10,2},{3,11},{11,3},{4,12},{12,4},... | collective-permute-start | bytes 147464 | tf_op jit(solution)/shard_map/ppermute | solution.py:429
  475.2 24.5 %collective-permute-start.81 = (bf16[704,384]{1,0:T(8,128)(2,1)S(1)}, bf16[704,384]{1,0:T(8,128)(2,1)S(1)}, u32[]{:S(2)}, u32[]{:S(2)}) collective-permute-start(bf16[704,384]{1,0:T(8,128)(2,1)S(1)} %fusion.11), channel_id=1, source_target_pairs={{0,16},{16,0},{1,17},{17,1},{2,18},{18,2},{3,19},{19,3},{4,20},{20... | collective-permute-start | bytes 1622024 | tf_op jit(solution)/shard_map/ppermute | solution.py:429
  479.4 13.4 %collective-permute-start.59 = (bf16[128,1536]{1,0:T(8,128)(2,1)S(1)}, bf16[128,1536]{1,0:T(8,128)(2,1)S(1)}, u32[]{:S(2)}, u32[]{:S(2)}) collective-permute-start(bf16[128,1536]{1,0:T(8,128)(2,1)S(1)} %get-tuple-element.126), channel_id=1, source_target_pairs={{4,8},{8,4},{5,9},{9,5},{6,10},{10,6},{7,11},{11,7},{20,24},{24,20... | collective-permute-start | bytes 1179656 | tf_op jit(solution)/shard_map/ppermute | solution.py:535
  497.3 16.4 %collective-permute-start.87 = (bf16[256,768]{1,0:T(8,128)(2,1)S(1)}, bf16[256,768]{1,0:T(8,128)(2,1)}, u32[]{:S(2)}, u32[]{:S(2)}) collective-permute-start(bf16[256,768]{1,0:T(8,128)(2,1)S(1)} %copy-done.80), channel_id=1, source_target_pairs={{0,3},{1,2},{2,1},{3,0},{4,7},{5,6},{6,5},{7,4},{8,11},{9,10},{10,... | collective-permute-start | bytes 1179656 | tf_op jit(solution)/shard_map/ppermute | solution.py:542
  499.9 22.3 %collective-permute-start.65 = (bf16[4,48,1152]{2,1,0:T(8,128)(2,1)}, bf16[4,48,1152]{2,1,0:T(8,128)(2,1)}, u32[]{:S(2)}, u32[]{:S(2)}) collective-permute-start(bf16[4,48,1152]{2,1,0:T(8,128)(2,1)} %dynamic-slice_bitcast_fusion.1), channel_id=1, source_target_pairs={{0,4},{4,0},{1,5},{5,1},{2,6},{6,2},{3,7},{7,3},{8,12},{12,8},{9,1... | collective-permute-start | bytes 1327112 | tf_op jit(solution)/shard_map/ppermute | solution.py:429
  529.2 25.9 %collective-permute-start.82 = (bf16[704,768]{1,0:T(8,128)(2,1)S(1)}, bf16[704,768]{1,0:T(8,128)(2,1)S(1)}, u32[]{:S(2)}, u32[]{:S(2)}) collective-permute-start(bf16[704,768]{1,0:T(8,128)(2,1)S(1)} %copy-done.83), channel_id=1, source_target_pairs={{0,8},{8,0},{1,9},{9,1},{2,10},{10,2},{3,11},{11,3},{4,12},{12,4},... | collective-permute-start | bytes 3244040 | tf_op jit(solution)/shard_map/ppermute | solution.py:429
  531.5 19.7 %collective-permute-start.88 = (bf16[256,1536]{1,0:T(8,128)(2,1)}, bf16[256,1536]{1,0:T(8,128)(2,1)}, u32[]{:S(2)}, u32[]{:S(2)}) collective-permute-start(bf16[256,1536]{1,0:T(8,128)(2,1)} %get-tuple-element.166), channel_id=1, source_target_pairs={{0,8},{8,0},{1,9},{9,1},{2,10},{10,2},{3,11},{11,3},{4,12},{12,4},... | collective-permute-start | bytes 2359304 | tf_op jit(solution)/shard_map/ppermute | solution.py:429
  547.8 39.4 %collective-permute-start.72 = (bf16[2,48,4608]{2,1,0:T(8,128)(2,1)}, bf16[2,48,4608]{2,1,0:T(8,128)(2,1)}, u32[]{:S(2)}, u32[]{:S(2)}) collective-permute-start(bf16[2,48,4608]{2,1,0:T(8,128)(2,1)} %pad_maximum_fusion.13), channel_id=1, source_target_pairs={{0,8},{8,0},{1,9},{9,1},{2,10},{10,2},{3,11},{11,3},{4,12},{12,4},... | collective-permute-start | bytes 2654216 | tf_op jit(solution)/shard_map/ppermute | solution.py:429
  554.0 19.5 %collective-permute-start.89 = (bf16[512,768]{1,0:T(8,128)(2,1)}, bf16[512,768]{1,0:T(8,128)(2,1)}, u32[]{:S(2)}, u32[]{:S(2)}) collective-permute-start(bf16[512,768]{1,0:T(8,128)(2,1)} %convolution_convert_fusion.1), channel_id=1, source_target_pairs={{0,16},{16,0},{1,17},{17,1},{2,18},{18,2},{3,19},{19,3},{4,20},{20... | collective-permute-start | bytes 2359304 | tf_op jit(solution)/shard_map/ppermute | solution.py:429
  560.0 19.5 %collective-permute-start.92 = (bf16[192,512]{1,0:T(8,128)(2,1)S(1)}, bf16[192,512]{1,0:T(8,128)(2,1)S(1)}, u32[]{:S(2)}, u32[]{:S(2)}) collective-permute-start(bf16[192,512]{1,0:T(8,128)(2,1)S(1)} %get-tuple-element.196), channel_id=1, source_target_pairs={{0,1},{1,0},{2,3},{3,2},{4,5},{5,4},{6,7},{7,6},{8,9},{9,8},{10,11... | collective-permute-start | bytes 589832 | tf_op jit(solution)/shard_map/ppermute | solution.py:542
  575.5 18.3 %collective-permute-start.90 = (bf16[512,768]{1,0:T(8,128)(2,1)S(1)}, bf16[512,768]{1,0:T(8,128)(2,1)S(1)}, u32[]{:S(2)}, u32[]{:S(2)}) collective-permute-start(bf16[512,768]{1,0:T(8,128)(2,1)S(1)} %reduce-precision_convert_fusion), channel_id=1, source_target_pairs={{0,16},{16,0},{1,17},{17,1},{2,18},{18,2},{3,19},{19,3},{4,20},{20... | collective-permute-start | bytes 2359304 | tf_op jit(solution)/shard_map/ppermute | solution.py:429
  586.6 24.1 %collective-permute-start.95 = (bf16[192,2048]{1,0:T(8,128)(2,1)S(1)}, bf16[192,2048]{1,0:T(8,128)(2,1)S(1)}, u32[]{:S(2)}, u32[]{:S(2)}) collective-permute-start(bf16[192,2048]{1,0:T(8,128)(2,1)S(1)} %constant_dynamic-update-slice_fusion.6), channel_id=1, source_target_pairs={{0,16},{16,0},{1,17},{17,1},{2,18},{18,2},{3,19},{19,3},{4,20},{20... | collective-permute-start | bytes 2359304 | tf_op jit(solution)/shard_map/ppermute | solution.py:429
  594.1 20.9 %collective-permute-start.91 = (bf16[512,1536]{1,0:T(8,128)(2,1)S(1)}, bf16[512,1536]{1,0:T(8,128)(2,1)S(1)}, u32[]{:S(2)}, u32[]{:S(2)}) collective-permute-start(bf16[512,1536]{1,0:T(8,128)(2,1)S(1)} %pad_maximum_fusion.7), channel_id=1, source_target_pairs={{0,8},{8,0},{1,9},{9,1},{2,10},{10,2},{3,11},{11,3},{4,12},{12,4},... | collective-permute-start | bytes 4718600 | tf_op jit(solution)/shard_map/ppermute | solution.py:429
  (188 other events, 1828.1 us)
Sparse Core Ops, SparseCore 0:
  114.1 50.2 all-gather.4
  166.8 76.0 all-gather.2
  330.4 88.4 reduce-scatter.1
